TPU v7x, 32 devices: a whole 2x2x4 slice. The times are simulated.
32 devices in a mesh: row: 8 (over y, x, core), col: 4 (over z).
Axes of the slice: x: 2, y: 2, z: 4, core: 2. Of those that a mesh axis runs over, the one named last changes fastest.
Arguments:
- image_in: bfloat16 [8, 1572864], P('row', 'col'), may hold values from -6 to 6
- text_in: bfloat16 [8, 236544], P('row', 'col'), may hold values from -6 to 6
- condition: bfloat16 [8, 1536], P('row'), may hold values from -6 to 6
- mod_image: bfloat16 [1536, 18432], P('row', 'col'), may hold values from -0.15625 to 0.15625
- mod_text: bfloat16 [1536, 18432], P('row', 'col'), may hold values from -0.15625 to 0.15625
- qkv_image: bfloat16 [1536, 9216], P('row', 'col'), may hold values from -0.15625 to 0.15625
- qkv_text: bfloat16 [1536, 9216], P('row', 'col'), may hold values from -0.15625 to 0.15625
- out_image: bfloat16 [1536, 3072], P('row', 'col'), may hold values from -1.75 to 1.75
- out_text: bfloat16 [1536, 3072], P('row', 'col'), may hold values from -1.75 to 1.75
- up_image: bfloat16 [2, 1536, 6144], P(None, 'row', 'col'), may hold values from -0.15625 to 0.15625
- up_text: bfloat16 [2, 1536, 6144], P(None, 'row', 'col'), may hold values from -0.15625 to 0.15625
- down_image: bfloat16 [2, 1536, 6144], P(None, 'row', 'col'), may hold values from -0.078125 to 0.078125
- down_text: bfloat16 [2, 1536, 6144], P(None, 'row', 'col'), may hold values from -0.078125 to 0.078125
- cot_image: bfloat16 [8, 1572864], P('row', 'col'), may hold values from -6 to 6
- cot_text: bfloat16 [8, 236544], P('row', 'col'), may hold values from -6 to 6
Outputs:
- image_out: bfloat16 [8, 1572864], P('row', 'col')
- text_out: bfloat16 [8, 236544], P('row', 'col')
- grad_image: float32 [8, 1572864], P('row', 'col')
- grad_text: float32 [8, 236544], P('row', 'col')
- grad_cond: float32 [8, 1536], P('row')
- grad_mod_image: float32 [1536, 18432], P('row', 'col')
- grad_mod_text: float32 [1536, 18432], P('row', 'col')
- grad_qkv_image: float32 [1536, 9216], P('row', 'col')
- grad_qkv_text: float32 [1536, 9216], P('row', 'col')
- grad_out_image: float32 [1536, 3072], P('row', 'col')
- grad_out_text: float32 [1536, 3072], P('row', 'col')
- grad_up_image: float32 [2, 1536, 6144], P(None, 'row', 'col')
- grad_up_text: float32 [2, 1536, 6144], P(None, 'row', 'col')
- grad_down_image: float32 [2, 1536, 6144], P(None, 'row', 'col')
- grad_down_text: float32 [2, 1536, 6144], P(None, 'row', 'col')
All inputs are finite; a program needn't handle non-finite values.
Results may differ from a plain program's by a relative error of at most 0.022.
Values may be sent and summed in bfloat16 or wider, within the bound.
No kernel may reach another device: no remote copies, remote signals or barrier semaphores. Data moves between devices by JAX's collectives and lax.ppermute only.
A program may use at most 384 MiB of HBM per device.

v0:
```python
import jax
import jax.numpy as jnp
from jax import lax
from jax.sharding import PartitionSpec as P

D = 1536
HEAD = 64
IMG_LEN = 1024
TXT_LEN = 154
LAYERS = 2


EPS = 1e-06


def column_norm(stream_a, stream_b):
    totals = lax.psum(
        (
            jnp.sum(stream_a, axis=2),
            jnp.sum(stream_a * stream_a, axis=2),
            jnp.sum(stream_b, axis=2),
            jnp.sum(stream_b * stream_b, axis=2),
        ),
        "col",
    )
    result = []
    for first, stream in ((0, stream_a), (2, stream_b)):
        average = totals[first] / D
        spread = totals[first + 1] / D - average * average
        inverse = lax.rsqrt(spread + EPS)[:, :, None]
        result.append(((stream - average[:, :, None]) * inverse, inverse))
    return result


def spread_rows(first, second):
    return (
        lax.all_gather(first, "col", axis=2, tiled=True),
        lax.all_gather(second, "col", axis=2, tiled=True),
    )


def collect_branch(first, second):
    return (
        lax.psum_scatter(first.astype(jnp.bfloat16), "col", scatter_dimension=2, tiled=True).astype(
            jnp.float32
        ),
        lax.psum_scatter(
            second.astype(jnp.bfloat16), "col", scatter_dimension=2, tiled=True
        ).astype(jnp.float32),
    )


def gather_grads(first, second):
    return (
        lax.all_gather(first, "col", axis=2, tiled=True),
        lax.all_gather(second, "col", axis=2, tiled=True),
    )


def scatter_grads(first, second):
    return (
        lax.psum_scatter(first.astype(jnp.bfloat16), "col", scatter_dimension=2, tiled=True).astype(
            jnp.float32
        ),
        lax.psum_scatter(
            second.astype(jnp.bfloat16), "col", scatter_dimension=2, tiled=True
        ).astype(jnp.float32),
    )


def modulated(normed, modul, shift_at):
    return (
        normed * (1.0 + modul[:, shift_at + 1 : shift_at + 2]) + modul[:, shift_at : shift_at + 1]
    ).astype(jnp.bfloat16)


def to_items(joint):
    seqs, length, three, local = joint.shape
    heads_here = local // HEAD
    sectioned = joint.reshape(seqs, length, three, heads_here, HEAD)
    return jnp.transpose(sectioned, (0, 3, 2, 1, 4)).reshape(seqs * heads_here, three, length, HEAD)


def from_items(items, seqs):
    heads_here = items.shape[0] // seqs
    sectioned = items.reshape(seqs, heads_here, items.shape[1], items.shape[2], HEAD)
    return jnp.transpose(sectioned, (0, 3, 2, 1, 4)).reshape(
        seqs, items.shape[2], items.shape[1], heads_here * HEAD
    )


def attend_item(item):
    queries, key_rows, values = (item[0], item[1], item[2])
    scores = jnp.einsum(
        "qe,ke->qk", queries, key_rows, preferred_element_type=jnp.float32
    ) * HEAD ** (-0.5)
    highest = jnp.max(scores, axis=1, keepdims=True)
    layer_weight_set = jnp.exp(scores - highest)
    totals = jnp.sum(layer_weight_set, axis=1, keepdims=True)
    chances = (layer_weight_set / totals).astype(jnp.bfloat16)
    output = jnp.dot(chances, values, preferred_element_type=jnp.float32).astype(jnp.bfloat16)
    return (output[None], (highest + jnp.log(totals))[:, 0])


def attend_back(packed):
    item, log_total, grad_out = packed
    queries, key_rows, values = (item[0], item[1], item[2])
    scale = HEAD ** (-0.5)
    scores = jnp.einsum("qe,ke->qk", queries, key_rows, preferred_element_type=jnp.float32) * scale
    chances = jnp.exp(scores - log_total[:, None])
    grad_chance = jnp.einsum("qe,ke->qk", grad_out[0], values, preferred_element_type=jnp.float32)
    grad_values = jnp.einsum(
        "qk,qe->ke", chances.astype(jnp.bfloat16), grad_out[0], preferred_element_type=jnp.float32
    )
    centred = jnp.sum(grad_chance * chances, axis=1, keepdims=True)
    grad_scores = (chances * (grad_chance - centred)).astype(jnp.bfloat16)
    grad_queries = (
        jnp.einsum("qk,ke->qe", grad_scores, key_rows, preferred_element_type=jnp.float32) * scale
    )
    grad_keys = (
        jnp.einsum("qk,qe->ke", grad_scores, queries, preferred_element_type=jnp.float32) * scale
    )
    return jnp.stack([grad_queries, grad_keys, grad_values])


def layer_shards(stacked, depth):
    rows_here = stacked[0].shape[0]

    def pick(weight, count):
        return weight.reshape(rows_here, -1, LAYERS, count)[:, :, depth, :]

    def pick_out(weight):
        return weight.reshape(rows_here, -1, LAYERS)[:, :, depth]

    return (
        pick(stacked[0], 6),
        pick(stacked[1], 6),
        pick(stacked[2], 3),
        pick(stacked[3], 3),
        pick_out(stacked[4]),
        pick_out(stacked[5]),
        stacked[6][depth],
        stacked[7][depth],
        stacked[8][depth],
        stacked[9][depth],
    )


def layer_forward(token_streams, cond_low, shards):
    gathered_attn = (
        lax.all_gather(shards[0], "row", axis=0, tiled=True),
        lax.all_gather(shards[1], "row", axis=0, tiled=True),
        lax.all_gather(shards[2], "row", axis=0, tiled=True),
        lax.all_gather(shards[3], "row", axis=0, tiled=True),
        lax.all_gather(shards[4], "row", axis=0, tiled=True),
        lax.all_gather(shards[5], "row", axis=0, tiled=True),
    )
    modulation_vectors = [
        jnp.einsum(
            "sd,dck->skc",
            cond_low,
            gathered_attn[selected_stream],
            preferred_element_type=jnp.float32,
        )
        for selected_stream in range(2)
    ]
    norms1 = column_norm(token_streams[0], token_streams[1])
    full1 = spread_rows(
        modulated(norms1[0][0], modulation_vectors[0], 0),
        modulated(norms1[1][0], modulation_vectors[1], 0),
    )
    query_key_value = [
        jnp.einsum(
            "epg,gyx->epxy",
            full1[selected_stream],
            gathered_attn[2 + selected_stream],
            preferred_element_type=jnp.float32,
        ).astype(jnp.bfloat16)
        for selected_stream in range(2)
    ]
    joint = jnp.concatenate(query_key_value, axis=1)
    seqs = joint.shape[0]
    items = to_items(joint)
    attended, log_totals = lax.map(attend_item, items)
    heads_out = from_items(attended, seqs)[:, :, 0]
    image_len = token_streams[0].shape[1]
    heads = [heads_out[:, :image_len], heads_out[:, image_len:]]
    partial_out = [
        jnp.einsum(
            "iau,yu->iay",
            heads[selected_stream],
            gathered_attn[4 + selected_stream],
            preferred_element_type=jnp.float32,
        )
        for selected_stream in range(2)
    ]
    branch = collect_branch(partial_out[0], partial_out[1])
    middle_results = [
        token_streams[selected_stream]
        + modulation_vectors[selected_stream][:, 2:3] * branch[selected_stream]
        for selected_stream in range(2)
    ]
    collected_feedforward = (
        lax.all_gather(shards[6], "row", axis=0, tiled=True),
        lax.all_gather(shards[7], "row", axis=0, tiled=True),
        lax.all_gather(shards[8], "row", axis=0, tiled=True),
        lax.all_gather(shards[9], "row", axis=0, tiled=True),
    )
    norms2 = column_norm(middle_results[0], middle_results[1])
    complete_second = spread_rows(
        modulated(norms2[0][0], modulation_vectors[0], 3),
        modulated(norms2[1][0], modulation_vectors[1], 3),
    )
    hidden_pre = [
        jnp.einsum(
            "aqz,zh->aqh",
            complete_second[selected_stream],
            collected_feedforward[selected_stream],
            preferred_element_type=jnp.float32,
        )
        for selected_stream in range(2)
    ]
    activated = [
        jax.nn.gelu(hidden_pre[selected_stream], approximate=True).astype(jnp.bfloat16)
        for selected_stream in range(2)
    ]
    partial_down = [
        jnp.einsum(
            "nqb,ab->nqa",
            activated[selected_stream],
            collected_feedforward[2 + selected_stream],
            preferred_element_type=jnp.float32,
        )
        for selected_stream in range(2)
    ]
    down = collect_branch(partial_down[0], partial_down[1])
    finals = [
        middle_results[selected_stream]
        + modulation_vectors[selected_stream][:, 5:6] * down[selected_stream]
        for selected_stream in range(2)
    ]
    saved = {
        "weights": tuple(gathered_attn) + tuple(collected_feedforward),
        "mods": modulation_vectors,
        "norms1": norms1,
        "full1": full1,
        "items": items,
        "log_totals": log_totals,
        "heads": heads,
        "branch": branch,
        "norms2": norms2,
        "full2": complete_second,
        "hidden_pre": hidden_pre,
        "activated": activated,
        "down": down,
    }
    return (finals, saved)


def modulation_back(grad_h, norm_pairs, modulation_vectors, shift_at):
    shift_grads = [jnp.sum(grad_h[selected_stream], axis=1) for selected_stream in range(2)]
    scale_grads = [
        jnp.sum(grad_h[selected_stream] * norm_pairs[selected_stream][0], axis=1)
        for selected_stream in range(2)
    ]
    grad_norm = [
        grad_h[selected_stream]
        * (1.0 + modulation_vectors[selected_stream][:, shift_at + 1 : shift_at + 2])
        for selected_stream in range(2)
    ]
    totals = lax.psum(
        (
            jnp.sum(grad_norm[0], axis=2),
            jnp.sum(grad_norm[0] * norm_pairs[0][0], axis=2),
            jnp.sum(grad_norm[1], axis=2),
            jnp.sum(grad_norm[1] * norm_pairs[1][0], axis=2),
        ),
        "col",
    )
    back = [
        norm_pairs[selected_stream][1]
        * (
            grad_norm[selected_stream]
            - totals[2 * selected_stream][:, :, None] / D
            - norm_pairs[selected_stream][0] * totals[2 * selected_stream + 1][:, :, None] / D
        )
        for selected_stream in range(2)
    ]
    return (shift_grads, scale_grads, back)


def layer_backward(saved, grads, cond_low):
    layer_weight_set = saved["weights"]
    modulation_vectors = saved["mods"]
    mlp_gate = [
        jnp.sum(grads[selected_stream] * saved["down"][selected_stream], axis=1)
        for selected_stream in range(2)
    ]
    complete_down_weight = gather_grads(
        (modulation_vectors[0][:, 5:6] * grads[0]).astype(jnp.bfloat16),
        (modulation_vectors[1][:, 5:6] * grads[1]).astype(jnp.bfloat16),
    )
    grad_act = [
        jnp.einsum(
            "aqz,zh->aqh",
            complete_down_weight[selected_stream],
            layer_weight_set[8 + selected_stream],
            preferred_element_type=jnp.float32,
        )
        for selected_stream in range(2)
    ]
    grad_down_w = [
        jnp.einsum(
            "qmx,qma->ax",
            saved["activated"][selected_stream],
            complete_down_weight[selected_stream],
            preferred_element_type=jnp.float32,
        )
        for selected_stream in range(2)
    ]
    gradient_before_activation = []
    for selected_stream in range(2):
        ignored, gelu_pull = jax.vjp(
            lambda value: jax.nn.gelu(value, approximate=True), saved["hidden_pre"][selected_stream]
        )
        gradient_before_activation.append(
            gelu_pull(grad_act[selected_stream])[0].astype(jnp.bfloat16)
        )
    partial_second = [
        jnp.einsum(
            "nqb,ab->nqa",
            gradient_before_activation[selected_stream],
            layer_weight_set[6 + selected_stream],
            preferred_element_type=jnp.float32,
        )
        for selected_stream in range(2)
    ]
    grad_second = scatter_grads(partial_second[0], partial_second[1])
    grad_up_w = [
        jnp.einsum(
            "wny,wnz->yz",
            saved["full2"][selected_stream],
            gradient_before_activation[selected_stream],
            preferred_element_type=jnp.float32,
        )
        for selected_stream in range(2)
    ]
    mlp_grads = (
        lax.psum_scatter(
            grad_up_w[0].astype(jnp.bfloat16), "row", scatter_dimension=0, tiled=True
        ).astype(jnp.float32),
        lax.psum_scatter(
            grad_up_w[1].astype(jnp.bfloat16), "row", scatter_dimension=0, tiled=True
        ).astype(jnp.float32),
        lax.psum_scatter(
            grad_down_w[0].astype(jnp.bfloat16), "row", scatter_dimension=0, tiled=True
        ).astype(jnp.float32),
        lax.psum_scatter(
            grad_down_w[1].astype(jnp.bfloat16), "row", scatter_dimension=0, tiled=True
        ).astype(jnp.float32),
    )
    shift2, scale2, back2 = modulation_back(grad_second, saved["norms2"], modulation_vectors, 3)
    grad_mid = [grads[selected_stream] + back2[selected_stream] for selected_stream in range(2)]
    attn_gate = [
        jnp.sum(grad_mid[selected_stream] * saved["branch"][selected_stream], axis=1)
        for selected_stream in range(2)
    ]
    complete_output_weight = gather_grads(
        (modulation_vectors[0][:, 2:3] * grad_mid[0]).astype(jnp.bfloat16),
        (modulation_vectors[1][:, 2:3] * grad_mid[1]).astype(jnp.bfloat16),
    )
    grad_heads = [
        jnp.einsum(
            "ejm,ma->eja",
            complete_output_weight[selected_stream],
            layer_weight_set[4 + selected_stream],
            preferred_element_type=jnp.float32,
        ).astype(jnp.bfloat16)
        for selected_stream in range(2)
    ]
    grad_out_w = [
        jnp.einsum(
            "eqh,eqf->fh",
            saved["heads"][selected_stream],
            complete_output_weight[selected_stream],
            preferred_element_type=jnp.float32,
        )
        for selected_stream in range(2)
    ]
    joint_grad = jnp.concatenate(grad_heads, axis=1)
    seqs = joint_grad.shape[0]
    grad_items = lax.map(
        attend_back, (saved["items"], saved["log_totals"], to_items(joint_grad[:, :, None]))
    )
    grad_joint = from_items(grad_items, seqs).astype(jnp.bfloat16)
    image_len = grads[0].shape[1]
    gradient_query_key_value = [grad_joint[:, :image_len], grad_joint[:, image_len:]]
    partial_first = [
        jnp.einsum(
            "gbhn,onh->gbo",
            gradient_query_key_value[selected_stream],
            layer_weight_set[2 + selected_stream],
            preferred_element_type=jnp.float32,
        )
        for selected_stream in range(2)
    ]
    grad_first = scatter_grads(partial_first[0], partial_first[1])
    grad_qkv_w = [
        jnp.einsum(
            "txf,txup->fpu",
            saved["full1"][selected_stream],
            gradient_query_key_value[selected_stream],
            preferred_element_type=jnp.float32,
        )
        for selected_stream in range(2)
    ]
    shift1, scale1, back1 = modulation_back(grad_first, saved["norms1"], modulation_vectors, 0)
    grad_inputs = [
        grad_mid[selected_stream] + back1[selected_stream] for selected_stream in range(2)
    ]
    grad_mod = [
        jnp.stack(
            [
                shift1[selected_stream],
                scale1[selected_stream],
                attn_gate[selected_stream],
                shift2[selected_stream],
                scale2[selected_stream],
                mlp_gate[selected_stream],
            ],
            axis=1,
        ).astype(jnp.bfloat16)
        for selected_stream in range(2)
    ]
    grad_mod_w = [
        jnp.einsum(
            "sd,skc->dck", cond_low, grad_mod[selected_stream], preferred_element_type=jnp.float32
        )
        for selected_stream in range(2)
    ]
    cond_part = jnp.einsum(
        "skc,dck->sd", grad_mod[0], layer_weight_set[0], preferred_element_type=jnp.float32
    ) + jnp.einsum(
        "skc,dck->sd", grad_mod[1], layer_weight_set[1], preferred_element_type=jnp.float32
    )
    attn_grads = (
        lax.psum_scatter(
            grad_mod_w[0].astype(jnp.bfloat16), "row", scatter_dimension=0, tiled=True
        ).astype(jnp.float32),
        lax.psum_scatter(
            grad_mod_w[1].astype(jnp.bfloat16), "row", scatter_dimension=0, tiled=True
        ).astype(jnp.float32),
        lax.psum_scatter(
            grad_qkv_w[0].astype(jnp.bfloat16), "row", scatter_dimension=0, tiled=True
        ).astype(jnp.float32),
        lax.psum_scatter(
            grad_qkv_w[1].astype(jnp.bfloat16), "row", scatter_dimension=0, tiled=True
        ).astype(jnp.float32),
        lax.psum_scatter(
            grad_out_w[0].astype(jnp.bfloat16), "row", scatter_dimension=0, tiled=True
        ).astype(jnp.float32),
        lax.psum_scatter(
            grad_out_w[1].astype(jnp.bfloat16), "row", scatter_dimension=0, tiled=True
        ).astype(jnp.float32),
    )
    return (grad_inputs, tuple(attn_grads) + tuple(mlp_grads), cond_part)


def to_tokens(flat, length):
    seqs = flat.shape[0]
    return jnp.transpose(flat.astype(jnp.float32).reshape(seqs, -1, length), (0, 2, 1))


def from_tokens(stream):
    return jnp.transpose(stream, (0, 2, 1)).reshape(stream.shape[0], -1)


def on_device(
    image_in,
    text_in,
    condition,
    mod_image,
    mod_text,
    qkv_image,
    qkv_text,
    out_image,
    out_text,
    up_image,
    up_text,
    down_image,
    down_text,
    cot_image,
    cot_text,
):
    stacked = (
        mod_image,
        mod_text,
        qkv_image,
        qkv_text,
        out_image,
        out_text,
        up_image,
        up_text,
        down_image,
        down_text,
    )
    seqs = condition.shape[0]
    rows_here = mod_image.shape[0]
    cond_float = condition.astype(jnp.float32)
    cond_low = jax.nn.silu(cond_float).astype(jnp.bfloat16)
    cond_total = jnp.zeros((seqs, D), jnp.float32)
    current = [to_tokens(image_in, IMG_LEN), to_tokens(text_in, TXT_LEN)]
    inputs = []
    kept = []
    for depth in range(LAYERS):
        inputs.append(current)
        current, saved = layer_forward(current, cond_low, layer_shards(stacked, depth))
        kept.append(saved)
    grads = [to_tokens(cot_image, IMG_LEN), to_tokens(cot_text, TXT_LEN)]
    grad_list = [None] * LAYERS
    for depth in reversed(range(LAYERS)):
        ignored, saved = layer_forward(inputs[depth], cond_low, layer_shards(stacked, depth))
        grads, layer_grads, cond_part = layer_backward(saved, grads, cond_low)
        grad_list[depth] = layer_grads
        cond_total = cond_total + cond_part
    cond_sum = lax.psum(cond_total, "col")
    ignored, silu_pull = jax.vjp(jax.nn.silu, cond_float)
    grad_cnd = silu_pull(cond_sum)[0]
    merged = [
        jnp.stack([grad_list[depth][selected_stream] for depth in range(LAYERS)], axis=2).reshape(
            rows_here, -1
        )
        for selected_stream in range(6)
    ]
    layered = [
        jnp.stack([grad_list[depth][selected_stream] for depth in range(LAYERS)], axis=0)
        for selected_stream in range(6, 10)
    ]
    return (
        from_tokens(current[0]).astype(jnp.bfloat16),
        from_tokens(current[1]).astype(jnp.bfloat16),
        from_tokens(grads[0]),
        from_tokens(grads[1]),
        grad_cnd,
        merged[0],
        merged[1],
        merged[2],
        merged[3],
        merged[4],
        merged[5],
        layered[0],
        layered[1],
        layered[2],
        layered[3],
    )


def solution(mesh):
    return jax.shard_map(
        on_device,
        mesh=mesh,
        in_specs=(
            P("row", "col"),
            P("row", "col"),
            P("row", None),
            P("row", "col"),
            P("row", "col"),
            P("row", "col"),
            P("row", "col"),
            P("row", "col"),
            P("row", "col"),
            P(None, "row", "col"),
            P(None, "row", "col"),
            P(None, "row", "col"),
            P(None, "row", "col"),
            P("row", "col"),
            P("row", "col"),
        ),
        out_specs=(
            P("row", "col"),
            P("row", "col"),
            P("row", "col"),
            P("row", "col"),
            P("row", None),
            P("row", "col"),
            P("row", "col"),
            P("row", "col"),
            P("row", "col"),
            P("row", "col"),
            P("row", "col"),
            P(None, "row", "col"),
            P(None, "row", "col"),
            P(None, "row", "col"),
            P(None, "row", "col"),
        ),
        check_vma=False,
    )
```

profile of v0, /device:TPU:0, one launch (start us, length us, event | category | flops | bytes accessed | tf_op | source)
XLA Modules:
  0.0 3913.6 jit_solution(11036763826896348442)
XLA Ops:
  195.6 65.4 %all-gather.51.cloned.1.call-done = bf16[1,1024,1536]{2,1,0:T(8,128)(2,1)} async-done(((bf16[1,1024,384]{2,1,0:T(8,128)(2,1)}), bf16[1,1024,1536]{2,1,0:T(8,128)(2,1)}) %all-gather.51.cloned.1.call-update) | async-done | bytes 3145744 | tf_op jit(solution)/shard_map/all_gather | solution.py:37
  408.0 56.2 %reduce-scatter.159.cloned.1.call-done = bf16[384,1024]{1,0:T(8,128)(2,1)} async-done(((bf16[1536,1024]{1,0:T(8,128)(2,1)}), bf16[384,1024]{1,0:T(8,128)(2,1)}) %reduce-scatter.159.cloned.1.call-update) | async-done | bytes 786448
  653.6 65.4 %all-gather.53.cloned.1.call-done = bf16[1,1024,1536]{2,1,0:T(8,128)(2,1)} async-done(((bf16[1,1024,384]{2,1,0:T(8,128)(2,1)}), bf16[1,1024,1536]{2,1,0:T(8,128)(2,1)}) %all-gather.53.cloned.1.call-update) | async-done | bytes 3145744 | tf_op jit(solution)/shard_map/all_gather | solution.py:37
  796.8 60.5 %reduce-scatter.135.cloned.1.call-done = bf16[384,1024]{1,0:T(8,128)(2,1)} async-done(((bf16[1536,1024]{1,0:T(8,128)(2,1)}), bf16[384,1024]{1,0:T(8,128)(2,1)}) %reduce-scatter.135.cloned.1.call-update) | async-done | bytes 786448
  980.9 65.5 %all-gather.55.cloned.1.call-done = bf16[1,1024,1536]{2,1,0:T(8,128)(2,1)} async-done(((bf16[1,1024,384]{2,1,0:T(8,128)(2,1)}), bf16[1,1024,1536]{2,1,0:T(8,128)(2,1)}) %all-gather.55.cloned.1.call-update) | async-done | bytes 3145744 | tf_op jit(solution)/shard_map/all_gather | solution.py:37
  1138.1 54.1 %reduce-scatter.149.cloned.1.call-done = bf16[384,1024]{1,0:T(8,128)(2,1)} async-done(((bf16[1536,1024]{1,0:T(8,128)(2,1)}), bf16[384,1024]{1,0:T(8,128)(2,1)}) %reduce-scatter.149.cloned.1.call-update) | async-done | bytes 786448
  1314.7 65.5 %all-gather.61.cloned.1.call-done = bf16[1,1024,1536]{2,1,0:T(8,128)(2,1)} async-done(((bf16[1,1024,384]{2,1,0:T(8,128)(2,1)}), bf16[1,1024,1536]{2,1,0:T(8,128)(2,1)}) %all-gather.61.cloned.1.call-update) | async-done | bytes 3145744 | tf_op jit(solution)/shard_map/all_gather | solution.py:37
  1420.2 65.4 %all-gather.59.cloned.1.call-done = bf16[1,1024,1536]{2,1,0:T(8,128)(2,1)} async-done(((bf16[1,1024,384]{2,1,0:T(8,128)(2,1)}), bf16[1,1024,1536]{2,1,0:T(8,128)(2,1)}) %all-gather.59.cloned.1.call-update) | async-done | bytes 3145744 | tf_op jit(solution)/shard_map/all_gather | solution.py:55
  1600.0 51.0 %reduce-scatter.173.cloned.1.call-done = bf16[384,1024]{1,0:T(8,128)(2,1)} async-done(((bf16[1536,1024]{1,0:T(8,128)(2,1)}), bf16[384,1024]{1,0:T(8,128)(2,1)}) %reduce-scatter.173.cloned.1.call-update) | async-done | bytes 786448
  1779.3 67.6 %while.67 = (s32[]{:T(128)}, bf16[6,3,1178,64]{2,3,1,0:T(8,128)(2,1)}, bf16[6,3,1178,64]{3,2,1,0:T(8,128)(2,1)}, f32[6,1178]{1,0:T(8,128)}, bf16[6,1,1178,64]{3,...) while((s32[]{:T(128)}, bf16[6,3,1178,64]{2,3,1,0:T(8,128)(2,1)}, ...), condition=%wide.region_74.75_spmd, body=%wide.region_72.74_spmd.sunk | while | flops 900876672 | bytes 46197940 | solution.py:392
  1973.7 61.7 %all-gather.67.cloned.1.call-done = bf16[1,1024,1536]{2,1,0:T(8,128)(2,1)} async-done(((bf16[1,1024,384]{2,1,0:T(8,128)(2,1)}), bf16[1,1024,1536]{2,1,0:T(8,128)(2,1)}) %all-gather.67.cloned.1.call-update) | async-done | bytes 3145744 | tf_op jit(solution)/shard_map/all_gather | solution.py:37
  2286.1 54.8 %reduce-scatter.161.cloned.1.call-done = bf16[384,1024]{1,0:T(8,128)(2,1)} async-done(((bf16[1536,1024]{1,0:T(8,128)(2,1)}), bf16[384,1024]{1,0:T(8,128)(2,1)}) %reduce-scatter.161.cloned.1.call-update) | async-done | bytes 786448
  2447.5 67.5 %while.69 = (s32[]{:T(128)}, bf16[6,3,1178,64]{2,3,1,0:T(8,128)(2,1)}, bf16[6,3,1178,64]{3,2,1,0:T(8,128)(2,1)}, f32[6,1178]{1,0:T(8,128)}, bf16[6,1,1178,64]{3,...) while((s32[]{:T(128)}, bf16[6,3,1178,64]{2,3,1,0:T(8,128)(2,1)}, ...), condition=%wide.region_111.112_spmd, body=%wide.region_109.111_spmd.sunk | while | flops 900876672 | bytes 46197940 | solution.py:392
  2866.5 53.4 %reduce-scatter.129.cloned.1.call-done = bf16[192,1536]{1,0:T(8,128)(2,1)} async-done(((bf16[1536,1536]{1,0:T(8,128)(2,1)}), bf16[192,1536]{1,0:T(8,128)(2,1)}) %reduce-scatter.129.cloned.1.call-update) | async-done | bytes 589840 | tf_op jit(solution)/shard_map/reduce_scatter | solution.py:358
  2922.7 54.6 %reduce-scatter.123.cloned.1.call-done = bf16[192,1536]{1,0:T(8,128)(2,1)} async-done(((bf16[1536,1536]{1,0:T(8,128)(2,1)}), bf16[192,1536]{1,0:T(8,128)(2,1)}) %reduce-scatter.123.cloned.1.call-update) | async-done | bytes 589840 | tf_op jit(solution)/shard_map/reduce_scatter | solution.py:352
  2977.3 57.6 %reduce-scatter.121.cloned.1.call-done = bf16[192,1536]{1,0:T(8,128)(2,1)} async-done(((bf16[1536,1536]{1,0:T(8,128)(2,1)}), bf16[192,1536]{1,0:T(8,128)(2,1)}) %reduce-scatter.121.cloned.1.call-update) | async-done | bytes 589840 | tf_op jit(solution)/shard_map/reduce_scatter | solution.py:352
  3037.7 54.4 %reduce-scatter.127.cloned.1.call-done = bf16[192,1536]{1,0:T(8,128)(2,1)} async-done(((bf16[1536,1536]{1,0:T(8,128)(2,1)}), bf16[192,1536]{1,0:T(8,128)(2,1)}) %reduce-scatter.127.cloned.1.call-update) | async-done | bytes 589840 | tf_op jit(solution)/shard_map/reduce_scatter | solution.py:355
  3092.1 57.8 %reduce-scatter.125.cloned.1.call-done = bf16[192,1536]{1,0:T(8,128)(2,1)} async-done(((bf16[1536,1536]{1,0:T(8,128)(2,1)}), bf16[192,1536]{1,0:T(8,128)(2,1)}) %reduce-scatter.125.cloned.1.call-update) | async-done | bytes 589840 | tf_op jit(solution)/shard_map/reduce_scatter | solution.py:355
  3152.7 54.6 %reduce-scatter.119.cloned.1.call-done = bf16[192,1536]{1,0:T(8,128)(2,1)} async-done(((bf16[1536,1536]{1,0:T(8,128)(2,1)}), bf16[192,1536]{1,0:T(8,128)(2,1)}) %reduce-scatter.119.cloned.1.call-update) | async-done | bytes 589840 | tf_op jit(solution)/shard_map/reduce_scatter | solution.py:349
  3207.3 57.8 %reduce-scatter.117.cloned.1.call-done = bf16[192,1536]{1,0:T(8,128)(2,1)} async-done(((bf16[1536,1536]{1,0:T(8,128)(2,1)}), bf16[192,1536]{1,0:T(8,128)(2,1)}) %reduce-scatter.117.cloned.1.call-update) | async-done | bytes 589840 | tf_op jit(solution)/shard_map/reduce_scatter | solution.py:349
  3565.9 58.5 %reduce-scatter.105.cloned.1.call-done = bf16[192,384,6]{1,0,2:T(8,128)(2,1)} async-done(((bf16[1536,384,6]{1,0,2:T(8,128)(2,1)}), bf16[192,384,6]{1,0,2:T(8,128)(2,1)}) %reduce-scatter.105.cloned.1.call-update) | async-done | bytes 884752 | tf_op jit(solution)/shard_map/reduce_scatter | solution.py:450
  3624.5 69.5 %reduce-scatter.107.cloned.1.call-done = bf16[192,384,6]{1,0,2:T(8,128)(2,1)} async-done(((bf16[1536,384,6]{1,0,2:T(8,128)(2,1)}), bf16[192,384,6]{1,0,2:T(8,128)(2,1)}) %reduce-scatter.107.cloned.1.call-update) | async-done | bytes 884752 | tf_op jit(solution)/shard_map/reduce_scatter | solution.py:450
  3712.8 50.0 %reduce-scatter.103.cloned.1.call-done = bf16[192,384,6]{1,0,2:T(8,128)(2,1)} async-done(((bf16[1536,384,6]{1,0,2:T(8,128)(2,1)}), bf16[192,384,6]{1,0,2:T(8,128)(2,1)}) %reduce-scatter.103.cloned.1.call-update) | async-done | bytes 884752 | tf_op jit(solution)/shard_map/reduce_scatter | solution.py:447
  3762.8 69.3 %reduce-scatter.101.cloned.1.call-done = bf16[192,384,6]{1,0,2:T(8,128)(2,1)} async-done(((bf16[1536,384,6]{1,0,2:T(8,128)(2,1)}), bf16[192,384,6]{1,0,2:T(8,128)(2,1)}) %reduce-scatter.101.cloned.1.call-update) | async-done | bytes 884752 | tf_op jit(solution)/shard_map/reduce_scatter | solution.py:447
  (1262 shorter events, 2714.8 us)
Async XLA Ops:
  98.9 300.2 %reduce-scatter.137.cloned.1.call-start = ((), (), s32[]{:S(2)}) async-start(), calls=%async_computation.92 | async-start | bytes 983040
  399.0 319.9 %all-gather.53.cloned.1.call-start = ((), (), s32[]{:S(2)}) async-start(), calls=%async_computation.45 | async-start | bytes 3932160 | tf_op jit(solution)/shard_map/all_gather | solution.py:37
  497.2 297.6 %reduce-scatter.139.cloned.1.call-start = ((), (), s32[]{:S(2)}) async-start(), calls=%async_computation.93 | async-start | bytes 983040
  762.5 283.9 %all-gather.55.cloned.1.call-start = ((), (), s32[]{:S(2)}) async-start(), calls=%async_computation.46 | async-start | bytes 3932160 | tf_op jit(solution)/shard_map/all_gather | solution.py:37
  1222.5 350.7 %reduce-scatter.155.cloned.1.call-start = ((), (), s32[]{:S(2)}) async-start(), calls=%async_computation.101 | async-start | bytes 983040
  1288.7 299.3 %reduce-scatter.151.cloned.1.call-start = ((), (), s32[]{:S(2)}) async-start(), calls=%async_computation.99 | async-start | bytes 3932160
  2685.5 291.8 %reduce-scatter.123.cloned.1.call-start = ((), (), s32[]{:S(2)}) async-start(), calls=%async_computation.65 | async-start | bytes 5308416 | tf_op jit(solution)/shard_map/reduce_scatter | solution.py:352
  2690.2 344.7 %reduce-scatter.121.cloned.1.call-start = ((), (), s32[]{:S(2)}) async-start(), calls=%async_computation.64 | async-start | bytes 5308416 | tf_op jit(solution)/shard_map/reduce_scatter | solution.py:352
  2695.0 397.2 %reduce-scatter.127.cloned.1.call-start = ((), (), s32[]{:S(2)}) async-start(), calls=%async_computation.67 | async-start | bytes 5308416 | tf_op jit(solution)/shard_map/reduce_scatter | solution.py:355
  2706.8 443.2 %reduce-scatter.125.cloned.1.call-start = ((), (), s32[]{:S(2)}) async-start(), calls=%async_computation.66 | async-start | bytes 5308416 | tf_op jit(solution)/shard_map/reduce_scatter | solution.py:355
  2718.9 488.3 %reduce-scatter.119.cloned.1.call-start = ((), (), s32[]{:S(2)}) async-start(), calls=%async_computation.63 | async-start | bytes 5308416 | tf_op jit(solution)/shard_map/reduce_scatter | solution.py:349
  2729.4 535.6 %reduce-scatter.117.cloned.1.call-start = ((), (), s32[]{:S(2)}) async-start(), calls=%async_computation.62 | async-start | bytes 5308416 | tf_op jit(solution)/shard_map/reduce_scatter | solution.py:349
  2740.1 565.4 %reduce-scatter.115.cloned.1.call-start = ((), (), s32[]{:S(2)}) async-start(), calls=%async_computation.61 | async-start | bytes 1327104 | tf_op jit(solution)/shard_map/reduce_scatter | solution.py:462
  2743.0 602.7 %reduce-scatter.113.cloned.1.call-start = ((), (), s32[]{:S(2)}) async-start(), calls=%async_computation.60 | async-start | bytes 1327104 | tf_op jit(solution)/shard_map/reduce_scatter | solution.py:462
  2744.8 641.5 %reduce-scatter.111.cloned.1.call-start = ((), (), s32[]{:S(2)}) async-start(), calls=%async_computation.59 | async-start | bytes 1327104 | tf_op jit(solution)/shard_map/reduce_scatter | solution.py:459
  2749.6 677.5 %reduce-scatter.109.cloned.1.call-start = ((), (), s32[]{:S(2)}) async-start(), calls=%async_computation.58 | async-start | bytes 1327104 | tf_op jit(solution)/shard_map/reduce_scatter | solution.py:459
  2754.9 723.7 %reduce-scatter.185.cloned.1.call-start = ((), (), s32[]{:S(2)}) async-start(), calls=%async_computation.116 | async-start | bytes 3981312
  2768.2 762.4 %reduce-scatter.181.cloned.1.call-start = ((), (), s32[]{:S(2)}) async-start(), calls=%async_computation.114 | async-start | bytes 3981312
  2790.5 772.1 %reduce-scatter.147.cloned.1.call-start = ((), (), s32[]{:S(2)}) async-start(), calls=%async_computation.97 | async-start | bytes 983040
  2815.0 809.5 %reduce-scatter.105.cloned.1.call-start = ((), (), s32[]{:S(2)}) async-start(), calls=%async_computation.56 | async-start | bytes 7962624 | tf_op jit(solution)/shard_map/reduce_scatter | solution.py:450
  2827.8 866.1 %reduce-scatter.107.cloned.1.call-start = ((), (), s32[]{:S(2)}) async-start(), calls=%async_computation.57 | async-start | bytes 7962624 | tf_op jit(solution)/shard_map/reduce_scatter | solution.py:450
  2828.6 934.2 %reduce-scatter.103.cloned.1.call-start = ((), (), s32[]{:S(2)}) async-start(), calls=%async_computation.55 | async-start | bytes 7962624 | tf_op jit(solution)/shard_map/reduce_scatter | solution.py:447
  2829.2 1002.9 %reduce-scatter.101.cloned.1.call-start = ((), (), s32[]{:S(2)}) async-start(), calls=%async_computation.54 | async-start | bytes 7962624 | tf_op jit(solution)/shard_map/reduce_scatter | solution.py:447
  2829.7 1064.8 %reduce-scatter.143.cloned.1.call-start = ((), (), s32[]{:S(2)}) async-start(), calls=%async_computation.95 | async-start | bytes 3932160
  (270 other events, 17531.9 us)
Sparse Core Ops, SparseCore 0:
  197.6 63.3 all-gather.50
  341.6 59.5 reduce-scatter.132
  403.9 60.2 reduce-scatter.158
  655.6 63.3 all-gather.52
  797.7 59.5 reduce-scatter.134
  983.0 63.3 all-gather.54
  1316.8 63.3 all-gather.60
  1422.2 63.3 all-gather.58
  1590.7 60.2 reduce-scatter.172
  1683.2 61.5 all-gather.62
  1776.8 59.9 reduce-scatter.140
  1880.0 59.5 reduce-scatter.156
  1973.6 61.7 all-gather.66
  2076.6 65.3 reduce-scatter.176
  2170.2 67.7 all-gather.64
  2281.6 59.3 reduce-scatter.160
  2376.6 63.4 all-gather.68
  2547.3 59.4 reduce-scatter.168
  2640.8 61.7 all-gather.56
  3559.7 64.6 reduce-scatter.104
  3628.4 65.4 reduce-scatter.106
  3697.3 65.4 reduce-scatter.102
  3766.6 65.4 reduce-scatter.100
  3834.3 60.2 reduce-scatter.142
  (50 shorter events, 1897.6 us)
where the time goes:
time: 3930 us; the launch traced here: 3910 us
  waiting for transfers between devices  2170 us (55%)
  local copies, waits for them, and re-layouts  651 us (17%)
  matrix products  552 us (14%)
  blocking collectives  318 us (8%)
  other arithmetic  192 us (5%)
    unnamed x102, waiting for transfers between devices  582 us
    unnamed x558, local copies, waits for them, and re-layouts  514 us
    all_gather x6, waiting for transfers between devices, spread_rows(): lax.all_gather(first, 'col', axis=2, tiled=True)  323 us
    all_gather x4, waiting for transfers between devices, gather_grads(): lax.all_gather(first, 'col', axis=2, tiled=True)  139 us
    reduce_scatter x2, waiting for transfers between devices, layer_backward(): lax.psum_scatter(grad_mod_w[1].astype(jnp.bfloat16), 'row', scatter_dimen...  128 us
    reduce_scatter x2, waiting for transfers between devices, layer_backward(): lax.psum_scatter(grad_mod_w[0].astype(jnp.bfloat16), 'row', scatter_dimen...  119 us
    reduce_scatter x2, waiting for transfers between devices, layer_backward(): lax.psum_scatter(grad_up_w[0].astype(jnp.bfloat16), 'row', scatter_dimens...  112 us
    reduce_scatter x2, waiting for transfers between devices, layer_backward(): lax.psum_scatter(grad_down_w[0].astype(jnp.bfloat16), 'row', scatter_dime...  112 us
  transfers between devices with their start and end apart: 74, of which 52 were waited for; matrix products, arithmetic and copies ran while one was open for 30% of the time, Pallas kernels for 0%

commit v1 on v0

v1 whole, which is shorter than its diff:
```python
import functools
import math

import jax
import jax.numpy as jnp
from jax import lax
from jax.experimental import pallas as pl
from jax.experimental.pallas import tpu as pltpu
from jax.sharding import PartitionSpec as P

D = 1536
HEAD = 64
IMG_LEN = 1024
TXT_LEN = 154
LAYERS = 2
EPS = 1e-06
CHUNKS = 1
F32 = jnp.float32
BF16 = jnp.bfloat16


def dot(a, b, ca, cb):
    return lax.dot_general(a, b, (((ca,), (cb,)), ((), ())), preferred_element_type=F32)


def nn(a, b):
    return dot(a, b, 1, 0)


def nt(a, b):
    return dot(a, b, 1, 1)


def tn(a, b):
    return dot(a, b, 0, 0)


class Plan:
    def __init__(self, rows, cols, swap):
        self.rows, self.cols, self.swap = rows, cols, swap
        half = cols // 2
        self.row, self.col = lax.axis_index("row"), lax.axis_index("col")
        self.a, self.x, self.k = self.row // 4, (self.row // 2) % 2, self.row % 2
        self.h, self.l = self.col // half, self.col % half
        self.member = self.x * half + self.l if swap else self.col

        def flat(a, x, k, h, l):
            return (a * 4 + x * 2 + k) * cols + h * half + l

        if swap:
            sides = [(a, k) for a in range(rows // 4) for k in range(2)]
            self.team = [
                [flat(a, x, k, h, l) for x in range(2) for l in range(half)] for a, k in sides for h in range(2)
            ]
            self.home = [(flat(a, x, k, 1 - x, l), flat(a, x, k, x, l)) for a, k in sides for x in range(2) for l in range(half)]
            self.across = [(r, r ^ 2) for r in range(rows)]
            self.levels = [(c, (c + half) % cols) for c in range(cols)]
            self.fetch = [[a * 4 + x * 2 + k for a, k in sides] for x in range(2)]

    def exchange(self, blocks):
        if self.swap:
            return lax.all_to_all(
                blocks, ("row", "col"), 0, 0, tiled=True, axis_index_groups=self.team
            )
        return lax.all_to_all(blocks, "col", 0, 0, tiled=True)


    def inner(self, natural):
        if not self.swap:
            return natural
        lead = natural.shape[:-1]
        cut = natural.reshape(lead + (self.rows // 4, 2, 2, D // self.rows))
        return jnp.swapaxes(cut, -3, -2).reshape(lead + (D,))

    natural = inner

    def pick(self, index, pair):
        return jnp.where(index == 0, pair[0], pair[1]), jnp.where(index == 0, pair[1], pair[0])

    def place(self, index, mine, other):
        return jnp.where(index == 0, mine, other), jnp.where(index == 0, other, mine)

    def swap_sides(self, pieces):
        mine = jnp.stack(pieces)
        if not self.swap:
            return mine
        wide = mine.shape[2] // 2
        mine, other = self.pick(self.x, [mine[:, :, :wide], mine[:, :, wide:]])
        return jnp.concatenate(self.place(self.x, mine, lax.ppermute(other, "row", self.across)), axis=1)

    def swap_levels(self, both, after=()):
        if not self.swap:
            return both
        h = tick(self.h, after) if len(after) else self.h
        return jnp.concatenate(self.place(h, both, lax.ppermute(both, "col", self.levels)), axis=2)

    def gather_weights(self, both):
        if not self.swap:
            return lax.all_gather(both, "row", axis=0)
        return lax.all_gather(both, "row", axis=0, axis_index_groups=self.fetch)

    def scatter_weights(self, whole):
        groups = self.fetch if self.swap else None
        return lax.psum_scatter(whole, "row", scatter_dimension=0, tiled=True, axis_index_groups=groups)[0]

    def sum_levels(self, both):
        if not self.swap:
            return both, both
        wide = both.shape[2] // 2
        mine, other = self.pick(self.h, [both[:, :, :wide], both[:, :, wide:]])
        return (mine.astype(F32) + lax.ppermute(other, "col", self.levels).astype(F32)).astype(BF16), other

    def join_sides(self, both):
        if not self.swap:
            return both
        rows = both.shape[1] // 2
        mine, other = self.pick(self.x, [both[:, :rows], both[:, rows:]])
        return jnp.concatenate(self.place(self.x, mine, lax.ppermute(other, "row", self.across)), axis=2)

    def rows_home(self, blocks):
        if not self.swap:
            return blocks
        moved = lax.ppermute(blocks, ("row", "col"), self.home)
        return jnp.stack(self.place(self.h, blocks, moved), axis=1)

    def rows_in(self, pair):
        got = self.exchange(pair)
        if not self.swap:
            return jnp.transpose(got, (1, 0, 2)).reshape(got.shape[1], D)
        got = got.reshape((2, self.cols // 2) + got.shape[1:])
        got = jnp.where(self.h == 0, got[0], got[1])
        return self.inner(jnp.transpose(got, (2, 1, 0, 3)).reshape(got.shape[2], D))

    def rows_out(self, own):
        tokens = own.shape[0]
        if not self.swap:
            return self.exchange(jnp.transpose(own.reshape(tokens, self.cols, -1), (1, 0, 2)))
        cut = self.natural(own).reshape(tokens, 2, self.cols // 2, D // self.cols)
        cut = jnp.transpose(cut, (2, 1, 0, 3))
        return self.exchange(jnp.concatenate([cut, cut], axis=0))

    def rows_back(self, got):
        if not self.swap:
            return got
        mine, other = self.pick(self.h, [got[:, 0], got[:, 1]])
        back = lax.ppermute(other, ("row", "col"), [(b, a) for a, b in self.home])
        return jnp.where(self.x == self.h, mine, back)

    def vectors_in(self, part):
        if not self.swap:
            mine = jnp.sum(lax.all_to_all(part, "row", 0, 0, tiled=True), axis=0, keepdims=True)
            return lax.all_to_all(jnp.broadcast_to(mine, (self.cols, mine.shape[1])), "col", 0, 0, tiled=True)
        cut = part.reshape(self.rows // 4, 1, 2, 2, -1)
        cut = jnp.broadcast_to(cut, (self.rows // 4, 2) + cut.shape[2:])
        sent = jnp.transpose(cut, (0, 1, 3, 2, 4)).reshape(self.rows, 2, -1)
        mine = jnp.sum(lax.all_to_all(sent, "row", 0, 0, tiled=True), axis=0)
        half = self.cols // 2
        sent = jnp.broadcast_to(mine[:, None], (2, half, mine.shape[1])).reshape(self.cols, -1)
        return lax.all_to_all(sent, "col", 0, 0, tiled=True)

    def vectors_out(self, part):
        got = lax.all_to_all(part, "col", 0, 0, tiled=True)
        if not self.swap:
            mine = jnp.sum(got, axis=0, keepdims=True)
            return lax.all_to_all(jnp.broadcast_to(mine, (self.rows, mine.shape[1])), "row", 0, 0, tiled=True)
        mine = jnp.sum(got.reshape(2, self.cols // 2, -1), axis=1)
        every = lax.all_to_all(jnp.broadcast_to(mine[None], (self.rows,) + mine.shape), "row", 0, 0, tiled=True)
        every = jnp.sum(every.reshape(self.rows // 4, 2, 2, 2, -1), axis=1)
        return jnp.transpose(every, (0, 2, 1, 3)).reshape(self.rows, -1)


def norm(x):
    average = jnp.mean(x, axis=1, keepdims=True)
    centred = x - average
    inverse = lax.rsqrt(jnp.mean(centred * centred, axis=1, keepdims=True) + EPS)
    return centred * inverse, inverse


def call(kernel, name, grid, ins, outs, flops=0, after=(), alias=None, scratch=(), transcendentals=0):
    args = [a for a, _, _ in ins]
    in_specs = [pl.BlockSpec(block, index) for _, block, index in ins]
    extra = list(after)
    aliases = {}
    if alias is not None:
        aliases = {len(args): 0}
        extra = [alias] + extra
    given = len(args)

    def body(*refs):
        kernel(*refs[:given], *refs[given + len(extra) :])

    moved = sum(a.size * a.dtype.itemsize for a in args)
    for shape, dtype, _, _ in outs:
        moved += math.prod(shape) * jnp.dtype(dtype).itemsize
    got = pl.pallas_call(
        body,
        grid=grid,
        in_specs=in_specs + [pl.BlockSpec(memory_space=pl.ANY)] * len(extra),
        out_specs=[pl.BlockSpec(block, index) for _, _, block, index in outs],
        out_shape=[jax.ShapeDtypeStruct(shape, dtype) for shape, dtype, _, _ in outs],
        scratch_shapes=list(scratch),
        input_output_aliases=aliases,
        compiler_params=pltpu.CompilerParams(vmem_limit_bytes=58 << 20),
        cost_estimate=pl.CostEstimate(
            flops=flops, bytes_accessed=moved, transcendentals=transcendentals
        ),
        name=name,
    )(*args, *extra)
    return got[0] if len(got) == 1 else got


def tick(index, after):
    def kernel(given, out):
        out[...] = given[...]

    one = jnp.full((8, 128), index, jnp.int32)
    whole = ((8, 128), lambda i: (0, 0))
    return call(kernel, "tick", (1,), [(one,) + whole], [((8, 128), jnp.int32) + whole], after=after)[0, 0]


def gate(array, after):
    def kernel(*refs):
        pass

    return pl.pallas_call(
        kernel,
        in_specs=[pl.BlockSpec(memory_space=pl.ANY)] * (1 + len(after)),
        out_specs=pl.BlockSpec(memory_space=pl.ANY),
        out_shape=jax.ShapeDtypeStruct(array.shape, array.dtype),
        input_output_aliases={0: 0},
        cost_estimate=pl.CostEstimate(flops=0, bytes_accessed=1024, transcendentals=0),
        name="gate",
    )(array, *after)


class Kernels:
    def __init__(self, members, ci, ct, chunks, groups, wide, hidden):
        self.q, self.ci, self.ct, self.rc, self.n = members, ci, ct, ci + ct, chunks
        self.g, self.dr = groups, D // groups
        self.wide, self.hidden = wide, hidden
        self.tokens = members * self.rc * chunks

    def sides(self, array, columns, index, lead=None):
        q, ratio = self.q, self.ci // self.ct
        if lead is None:
            return [
                (array, (q, self.ci, columns), lambda *i: (0, 0, index(*i))),
                (array, (q, self.ct, columns), lambda *i: (0, ratio, index(*i))),
            ]
        return [
            (array, (1,) * len(lead(0)) + (q, self.ci, columns), lambda *i: lead(*i) + (0, 0, index(*i))),
            (array, (1,) * len(lead(0)) + (q, self.ct, columns), lambda *i: lead(*i) + (0, ratio, index(*i))),
        ]

    def weight(self, array, columns, piece, index):
        return [
            (array, (self.g, 1, self.dr, columns), lambda *i, s=s: (0, piece(*i) + s, 0, index(*i))) for s in range(2)
        ]

    def flat(self, ref):
        value = ref[...]
        return value.reshape(-1, value.shape[-1])

    def put(self, ref, img, txt):
        cut = ref.shape[:-2]
        ref[..., : self.ci, :] = img.astype(ref.dtype).reshape(cut + (self.ci, ref.shape[-1]))
        ref[..., self.ci :, :] = txt.astype(ref.dtype).reshape(cut + (self.ct, ref.shape[-1]))

    def qkv(self, h, weights, chunk, joint, after=()):
        def kernel(hi, ht, wi, wt, out):
            self.put(out, nn(self.flat(hi), self.flat(wi)), nn(self.flat(ht), self.flat(wt)))

        return call(
            kernel,
            "qkv",
            (3,),
            self.sides(h, D, lambda j: 0) + self.weight(weights, self.wide, lambda j: 2 * j, lambda j: 0),
            [
                (
                    (self.n, self.q, self.rc, 3 * self.wide),
                    BF16,
                    (1, self.q, self.rc, self.wide),
                    lambda j: (chunk, 0, 0, j),
                )
            ],
            flops=2 * self.q * self.rc * D * 3 * self.wide,
            alias=joint,
            after=after,
        )

    def project(self, heads, weights, piece, chunk, after=()):
        def kernel(hi, ht, wi, wt, out):
            self.put(out, nt(self.flat(hi), self.flat(wi)), nt(self.flat(ht), self.flat(wt)))

        return call(
            kernel,
            "project",
            (1,),
            self.sides(heads, self.wide, lambda i: 0, lambda i: (chunk,))
            + self.weight(weights, self.wide, lambda i: piece, lambda i: 0),
            [((self.q, self.rc, D), BF16, (self.q, self.rc, D), lambda i: (0, 0, 0))],
            flops=2 * self.q * self.rc * D * self.wide,
            after=after,
        )

    def project_back(self, grad, weights, piece, chunk, joint, after=()):
        def kernel(hi, ht, wi, wt, out):
            self.put(out, nn(self.flat(hi), self.flat(wi)), nn(self.flat(ht), self.flat(wt)))

        return call(
            kernel,
            "project_back",
            (1,),
            self.sides(grad, D, lambda i: 0) + self.weight(weights, self.wide, lambda i: piece, lambda i: 0),
            [
                (
                    (self.n, self.q, self.rc, self.wide),
                    BF16,
                    (1, self.q, self.rc, self.wide),
                    lambda i: (chunk, 0, 0, 0),
                )
            ],
            flops=2 * self.q * self.rc * D * self.wide,
            alias=joint,
            after=after,
        )

    def qkv_back(self, grads, weights, chunk, after=()):
        def kernel(hi, ht, wi, wt, out, sum_i, sum_t):
            j = pl.program_id(0)
            img, txt = nt(self.flat(hi), self.flat(wi)), nt(self.flat(ht), self.flat(wt))

            @pl.when(j == 0)
            def _():
                sum_i[...] = img
                sum_t[...] = txt

            @pl.when(j == 1)
            def _():
                sum_i[...] += img
                sum_t[...] += txt

            @pl.when(j == 2)
            def _():
                self.put(out, sum_i[...] + img, sum_t[...] + txt)

        return call(
            kernel,
            "qkv_back",
            (3,),
            self.sides(grads, self.wide, lambda j: 0, lambda j: (j, chunk))
            + self.weight(weights, self.wide, lambda j: 2 * j, lambda j: 0),
            [((self.q, self.rc, D), BF16, (self.q, self.rc, D), lambda j: (0, 0, 0))],
            flops=2 * self.q * self.rc * D * 3 * self.wide,
            after=after,
            scratch=[pltpu.VMEM((self.q * self.ci, D), F32), pltpu.VMEM((self.q * self.ct, D), F32)],
        )

    def mlp(self, h, ups, downs, after=()):
        steps = 3
        block = self.hidden // steps

        def gelu(v):
            inner = 0.7978845608028654 * (v + 0.044715 * v * v * v)
            t = jnp.tanh(inner)
            half = 0.5 * (1.0 + t)
            slope = half + 0.5 * v * (1.0 - t * t) * (0.7978845608028654 * (1.0 + 3 * 0.044715 * v * v))
            return (v * half).astype(BF16), slope.astype(BF16)

        def kernel(hi, ht, ui, ut, di, dt, act, slope, out, sum_i, sum_t):
            j = pl.program_id(0)
            gi, si = gelu(nn(self.flat(hi), self.flat(ui)))
            gt, st = gelu(nn(self.flat(ht), self.flat(ut)))
            self.put(act, gi, gt)
            self.put(slope, si, st)
            img, txt = nt(gi, self.flat(di)), nt(gt, self.flat(dt))

            @pl.when(j == 0)
            def _():
                sum_i[...] = img
                sum_t[...] = txt

            @pl.when(jnp.logical_and(j > 0, j < steps - 1))
            def _():
                sum_i[...] += img
                sum_t[...] += txt

            @pl.when(j == steps - 1)
            def _():
                self.put(out, sum_i[...] + img, sum_t[...] + txt)

        return call(
            kernel,
            "mlp",
            (steps,),
            self.sides(h, D, lambda j: 0)
            + self.weight(ups, block, lambda j: 0, lambda j: j)
            + self.weight(downs, block, lambda j: 0, lambda j: j),
            [
                ((self.q, self.rc, self.hidden), BF16, (self.q, self.rc, block), lambda j: (0, 0, j)),
                ((self.q, self.rc, self.hidden), BF16, (self.q, self.rc, block), lambda j: (0, 0, j)),
                ((self.q, self.rc, D), BF16, (self.q, self.rc, D), lambda j: (0, 0, 0)),
            ],
            flops=4 * self.q * self.rc * D * self.hidden,
            transcendentals=self.q * self.rc * self.hidden,
            after=after,
            scratch=[pltpu.VMEM((self.q * self.ci, D), F32), pltpu.VMEM((self.q * self.ct, D), F32)],
        )

    def mlp_back(self, grad, slope, ups, downs, after=()):
        steps = 3
        block = self.hidden // steps

        def kernel(hi, ht, si, st, ui, ut, di, dt, pre, out, sum_i, sum_t):
            j = pl.program_id(0)
            pi = (nn(self.flat(hi), self.flat(di)) * self.flat(si).astype(F32)).astype(BF16)
            pt = (nn(self.flat(ht), self.flat(dt)) * self.flat(st).astype(F32)).astype(BF16)
            self.put(pre, pi, pt)
            img, txt = nt(pi, self.flat(ui)), nt(pt, self.flat(ut))

            @pl.when(j == 0)
            def _():
                sum_i[...] = img
                sum_t[...] = txt

            @pl.when(jnp.logical_and(j > 0, j < steps - 1))
            def _():
                sum_i[...] += img
                sum_t[...] += txt

            @pl.when(j == steps - 1)
            def _():
                self.put(out, sum_i[...] + img, sum_t[...] + txt)

        return call(
            kernel,
            "mlp_back",
            (steps,),
            self.sides(grad, D, lambda j: 0)
            + self.sides(slope, block, lambda j: j)
            + self.weight(ups, block, lambda j: 0, lambda j: j)
            + self.weight(downs, block, lambda j: 0, lambda j: j),
            [
                ((self.q, self.rc, self.hidden), BF16, (self.q, self.rc, block), lambda j: (0, 0, j)),
                ((self.q, self.rc, D), BF16, (self.q, self.rc, D), lambda j: (0, 0, 0)),
            ],
            flops=4 * self.q * self.rc * D * self.hidden,
            after=after,
            scratch=[pltpu.VMEM((self.q * self.ci, D), F32), pltpu.VMEM((self.q * self.ct, D), F32)],
        )

    def weight_grad(self, name, left, right, kinds, pieces, first, whole, after=()):
        columns = right[0][0].shape[-1]

        def rows(refs, side):
            got = [self.flat(refs[2 * c + side]) for c in range(self.n)]
            return got[0] if len(got) == 1 else jnp.concatenate(got, axis=0)

        if self.dr % 128:
            cut = []
            for kind in range(kinds):
                for side in (slice(0, self.ci), slice(self.ci, self.rc)):
                    a = jnp.concatenate([one[:, side].reshape(-1, D) for one in left], axis=0)
                    b = [one[lead(kind)] if lead else one for one, lead in right]
                    b = jnp.concatenate([one[:, side].reshape(-1, columns) for one in b], axis=0)
                    cut.append(tn(a, b).astype(BF16).reshape(self.g, self.dr, columns))
            cut = jnp.stack(cut, axis=1)
            return cut if whole is None else jnp.concatenate([whole, cut], axis=1)

        def kernel(*refs):
            ins, out = refs[:-1], refs[-1]
            for side in range(2):
                a, b = rows(ins[: 2 * self.n], side), rows(ins[2 * self.n :], side)
                out[0, side] = tn(a, b).astype(BF16)

        ins = []
        for one in left:
            ins += self.sides(one, self.dr, lambda j, g: g)
        for one, lead in right:
            ins += self.sides(one, columns, lambda j, g: 0, (lambda j, g=0, lead=lead: lead(j)) if lead else None)
        return call(
            kernel,
            name,
            (kinds, self.g),
            ins,
            [
                (
                    (self.g, pieces, self.dr, columns),
                    BF16,
                    (1, 2, self.dr, columns),
                    lambda j, g: (g, first // 2 + j, 0, 0),
                )
            ],
            flops=2 * self.tokens * D * columns * kinds,
            alias=whole,
            after=after,
        )

    def norm_in(self, mods, x, blocks=None, gate=None, after_norm=None, after=()):
        rows = self.ct

        def kernel(*refs):
            refs = list(refs)
            value = refs.pop(0)[...]
            if blocks is not None:
                added = jnp.sum(refs.pop(0)[...].astype(F32), axis=0)
                value = value + refs.pop(0)[0, gate[1] : gate[1] + 1] * added
            vectors = refs.pop(0) if after_norm is not None else None
            if blocks is not None:
                refs.pop(0)[...] = value
                refs.pop(0)[...] = added
            if after_norm is not None:
                kind = after_norm[1]
                normed = norm(value)[0]
                out = (normed * (1.0 + vectors[0, kind + 1 : kind + 2]) + vectors[0, kind : kind + 1]).astype(BF16)
                refs[0][...] = jnp.broadcast_to(out[None], refs[0].shape)

        ratio = self.ci // self.ct

        def vectors(depth):
            return (mods, (1,) + mods.shape[1:], lambda i: (depth * 2 + i // ratio, 0, 0))

        flat = ((rows, D), lambda i: (i, 0))
        many = ((self.q, rows, D), lambda i: (0, i, 0))
        ins, outs = [(x,) + flat], []
        if blocks is not None:
            ins += [(blocks,) + many, vectors(gate[0])]
            outs += [((self.rc, D), F32) + flat] * 2
        if after_norm is not None:
            ins.append(vectors(after_norm[0]))
            outs.append(((self.q, self.rc, D), BF16) + many)
        return call(kernel, "norm_in", (ratio + 1,), ins, outs, flops=20 * self.rc * D, after=after)

    def norm_back(self, mods, grad, blocks=None, x=None, scale=None, branch=None, gate=None, after=()):
        rows = self.ct
        ratio = self.ci // self.ct

        def kernel(*refs):
            refs = list(refs)
            value = refs.pop(0)[...]
            i = pl.program_id(0)
            rows_of_sums = []
            if blocks is not None:
                dh = jnp.sum(refs.pop(0)[...].astype(F32), axis=0)
                normed, inverse = norm(refs.pop(0)[...])
                dn = dh * (1.0 + refs.pop(0)[0, scale[1] : scale[1] + 1])
                value = value + inverse * (
                    dn
                    - jnp.mean(dn, axis=1, keepdims=True)
                    - normed * jnp.mean(dn * normed, axis=1, keepdims=True)
                )
                rows_of_sums += [(0, jnp.sum(dh, axis=0, keepdims=True)), (1, jnp.sum(dh * normed, axis=0, keepdims=True))]
            if branch is not None:
                rows_of_sums.append((2, jnp.sum(value * refs.pop(0)[...], axis=0, keepdims=True)))
            if gate is not None:
                factor = refs.pop(0)[0, gate[1] : gate[1] + 1]
            if blocks is not None:
                refs.pop(0)[...] = value
            if gate is not None:
                out = refs.pop(0)
                out[...] = jnp.broadcast_to((factor * value).astype(BF16)[None], out.shape)
            if not rows_of_sums:
                return
            sums = refs.pop(0)
            start = jnp.logical_or(i == 0, i == ratio)

            @pl.when(start)
            def _():
                for at, row in rows_of_sums:
                    sums[0, at : at + 1] = row

            @pl.when(jnp.logical_not(start))
            def _():
                for at, row in rows_of_sums:
                    sums[0, at : at + 1] += row

        def vectors(depth):
            return (mods, (1,) + mods.shape[1:], lambda i: (depth * 2 + i // ratio, 0, 0))

        flat = ((rows, D), lambda i: (i, 0))
        many = ((self.q, rows, D), lambda i: (0, i, 0))
        ins, outs = [(grad,) + flat], []
        if blocks is not None:
            ins += [(blocks,) + many, (x,) + flat, vectors(scale[0])]
            outs.append(((self.rc, D), F32) + flat)
        if branch is not None:
            ins.append((branch,) + flat)
        if gate is not None:
            ins.append(vectors(gate[0]))
            outs.append(((self.q, self.rc, D), BF16) + many)
        if blocks is not None or branch is not None:
            outs.append(((2, 8, D), F32, (1, 8, D), lambda i: (i // ratio, 0, 0)))
        return call(kernel, "norm_back", (ratio + 1,), ins, outs, flops=30 * self.rc * D, after=after)

    def masks(self):
        at = lax.broadcasted_iota(jnp.int32, (self.n, self.q, self.rc), 2)
        chunk = lax.broadcasted_iota(jnp.int32, (self.n, self.q, self.rc), 0)
        member = lax.broadcasted_iota(jnp.int32, (self.n, self.q, self.rc), 1)
        text = member * (self.ct * self.n) + chunk * self.ct + at - self.ci
        absent = jnp.logical_and(at >= self.ci, text >= TXT_LEN)
        return jnp.where(absent, -1e30, 0.0).astype(BF16).reshape(self.tokens, 1)

    def attend(self, joint, mask, after=()):
        t, pairs = self.tokens, self.wide // 128

        def kernel(q_ref, k_ref, v_ref, mask_ref, o_ref):
            q, k, v = q_ref[...], k_ref[...], v_ref[...]
            lane = lax.broadcasted_iota(jnp.int32, q.shape, 1)
            first = lane < HEAD
            none = jnp.zeros_like(q)
            bias = jnp.broadcast_to(mask_ref[...], k.shape)
            outs = []
            for side, spare in ((True, HEAD), (False, 0)):
                ones = jnp.where(lane == spare, jnp.ones_like(q), none)
                scaled = jnp.where(first == side, q * jnp.asarray(HEAD**-0.5, BF16), ones)
                scores = nt(scaled, jnp.where(first == side, k, bias))
                weights = jnp.exp(scores - jnp.max(scores, axis=1, keepdims=True))
                totals = jnp.sum(weights, axis=1, keepdims=True)
                outs.append(nn(weights.astype(BF16), v) * (1.0 / totals))
            o_ref[...] = jnp.where(first, outs[0], outs[1]).astype(BF16)

        flat = joint.reshape(t, 3 * self.wide)
        out = call(
            kernel,
            "attend",
            (pairs,),
            [(flat, (t, 128), lambda p, part=part: (0, part * pairs + p)) for part in range(3)]
            + [(mask, (t, 1), lambda p: (0, 0))],
            [((t, self.wide), BF16, (t, 128), lambda p: (0, p))],
            flops=pairs * 8 * t * t * 128,
            transcendentals=pairs * 2 * t * t,
            after=after,
        )
        return out.reshape(self.n, self.q, self.rc, self.wide)

    def attend_back(self, joint, mask, grad, after=()):
        t, pairs = self.tokens, self.wide // 128

        def kernel(q_ref, k_ref, v_ref, mask_ref, do_ref, out_ref):
            q, k, v, do = q_ref[...], k_ref[...], v_ref[...], do_ref[...]
            lane = lax.broadcasted_iota(jnp.int32, q.shape, 1)
            first = lane < HEAD
            none = jnp.zeros_like(q)
            bias = jnp.broadcast_to(mask_ref[...], k.shape)
            scale = jnp.asarray(HEAD**-0.5, BF16)
            dq = dk = dv = None
            for side, spare in ((True, HEAD), (False, 0)):
                mine = first == side
                ones = jnp.where(lane == spare, jnp.ones_like(q), none)
                scaled = q * scale
                grad_o = jnp.where(mine, do, none)
                scores = nt(jnp.where(mine, k, bias), jnp.where(mine, scaled, ones))
                weights = jnp.exp(scores - jnp.max(scores, axis=0, keepdims=True))
                chances = weights * (1.0 / jnp.sum(weights, axis=0, keepdims=True))
                grad_chances = nt(v, grad_o)
                centre = jnp.sum(grad_chances * chances, axis=0, keepdims=True)
                grad_scores = (chances * (grad_chances - centre)).astype(BF16)
                one_v = nn(chances.astype(BF16), grad_o)
                one_k = nn(grad_scores, jnp.where(mine, scaled, none))
                one_q = tn(grad_scores, jnp.where(mine, k * scale, none))
                dq, dk, dv = (one_q, one_k, one_v) if dq is None else (dq + one_q, dk + one_k, dv + one_v)
            out_ref[0] = dq.astype(BF16)
            out_ref[1] = dk.astype(BF16)
            out_ref[2] = dv.astype(BF16)

        flat = joint.reshape(t, 3 * self.wide)
        out = call(
            kernel,
            "attend_back",
            (pairs,),
            [(flat, (t, 128), lambda p, part=part: (0, part * pairs + p)) for part in range(3)]
            + [(mask, (t, 1), lambda p: (0, 0)), (grad.reshape(t, self.wide), (t, 128), lambda p: (0, p))],
            [((3, t, self.wide), BF16, (3, t, 128), lambda p: (0, 0, p))],
            flops=pairs * 20 * t * t * 128,
            transcendentals=pairs * 2 * t * t,
            after=after,
        )
        return out.reshape(3, self.n, self.q, self.rc, self.wide)


def order_matrix(block, kinds):
    width = block * LAYERS * kinds
    source = lax.broadcasted_iota(jnp.int32, (width, width), 0)
    target = lax.broadcasted_iota(jnp.int32, (width, width), 1)
    return (source == (target % block) * (LAYERS * kinds) + target // block).astype(BF16)


def split_columns(weight, kinds):
    rows = weight.shape[0]
    features = weight.shape[1] // (LAYERS * kinds)
    block = 128 if features % 128 == 0 else 64
    wide = block * LAYERS * kinds
    matrix = order_matrix(block, kinds)
    parts = [nn(weight[:, i * wide : (i + 1) * wide], matrix).astype(BF16) for i in range(features // block)]

    def one(at):
        return jnp.concatenate([part[:, at * block : (at + 1) * block] for part in parts], axis=1)

    return [[one(depth * kinds + kind) for kind in range(kinds)] for depth in range(LAYERS)]


def merge_columns(pieces, kinds):
    features = pieces[0][0].shape[1]
    block = 128 if features % 128 == 0 else 64
    matrix = order_matrix(block, kinds)
    parts = []
    for i in range(features // block):
        sorted_ = jnp.concatenate(
            [piece[:, i * block : (i + 1) * block] for layer in pieces for piece in layer], axis=1
        )
        parts.append(nt(sorted_, matrix))
    return jnp.concatenate(parts, axis=1)


def sort_vectors(part, kinds):
    rows = part.shape[0]
    features = part.shape[1] // (LAYERS * kinds)
    block = 128 if features % 128 == 0 else 64
    wide = block * LAYERS * kinds
    terms, rest = [], part
    for _ in range(3):
        term = lax.reduce_precision(rest, 8, 7)
        terms.append(term.astype(BF16))
        rest = rest - term
    matrix = order_matrix(block, kinds)
    cuts = jnp.concatenate(terms, axis=0)
    out = []
    for i in range(features // block):
        got = nn(cuts[:, i * wide : (i + 1) * wide], matrix).reshape(3, rows, LAYERS * kinds, block)
        out.append(got[0] + got[1] + got[2])
    return jnp.concatenate(out, axis=2)


def unsort_vectors(sorted_, kinds):
    rows, _, features = sorted_.shape
    block = 128 if features % 128 == 0 else 64
    matrix = order_matrix(block, kinds)
    out = [
        nt(sorted_[:, :, i * block : (i + 1) * block].reshape(rows, -1), matrix).astype(BF16)
        for i in range(features // block)
    ]
    return jnp.concatenate(out, axis=1)


def on_device(
    rows_count,
    cols,
    image_in,
    text_in,
    condition,
    mod_image,
    mod_text,
    qkv_image,
    qkv_text,
    out_image,
    out_text,
    up_image,
    up_text,
    down_image,
    down_text,
    cot_image,
    cot_text,
):
    features = D // cols
    swap = cols % 2 == 0 and rows_count % 4 == 0 and features % (2 * HEAD) == 0
    plan = Plan(rows_count, cols, swap)
    width_rows = mod_image.shape[0]
    img_own = IMG_LEN // cols
    txt_own = img_own // 4
    txt_pad = txt_own * cols
    wide = features + -features % 128
    k = Kernels(
        cols,
        img_own // CHUNKS,
        txt_own // CHUNKS,
        CHUNKS,
        rows_count // 2 if swap else rows_count,
        wide,
        up_image.shape[2],
    )
    chunks = range(CHUNKS)

    def filled(whole):
        return jnp.pad(whole, ((0, 0),) * 3 + ((0, wide - features),))

    qkv_shards = [split_columns(w, 3) for w in (qkv_image, qkv_text)]
    out_shards = [split_columns(w, 1) for w in (out_image, out_text)]
    w_attn, w_up, w_down = [], [], []
    sides_attn = [
        plan.swap_sides(
            [qkv_shards[s][depth][kind] for kind in range(3) for s in range(2)]
            + [out_shards[s][depth][0] for s in range(2)]
        )
        for depth in range(LAYERS)
    ]
    sides_up = [plan.swap_sides([up_image[depth], up_text[depth]]) for depth in range(LAYERS)]
    sides_down = [plan.swap_sides([down_image[depth], down_text[depth]]) for depth in range(LAYERS)]

    cond_float = condition.astype(F32)
    cond_low = jax.nn.silu(cond_float).astype(BF16)
    cond_cut = cond_low.reshape(rows_count, width_rows)
    cond_mine = lax.all_to_all(cond_cut, "row", 0, 0, tiled=True)
    mod_part = [nn(cond_mine, one) for one in (mod_image, mod_text)]
    mod_sorted = jnp.concatenate([sort_vectors(one, 6) for one in mod_part], axis=1)
    mod_cols = plan.vectors_in(mod_sorted.reshape(rows_count, -1)).reshape(cols, 2, LAYERS, 6, features)
    mods = plan.inner(jnp.transpose(mod_cols, (2, 1, 3, 0, 4)).reshape(LAYERS * 2, 6, D))

    def to_blocks(image, text):
        img = jnp.transpose(image.reshape(features, IMG_LEN)).reshape(cols, CHUNKS, k.ci, features)
        txt = jnp.pad(jnp.transpose(text.reshape(features, TXT_LEN)), ((0, txt_pad - TXT_LEN), (0, 0)))
        blocks = jnp.concatenate([img, txt.reshape(cols, CHUNKS, k.ct, features)], axis=2)
        return blocks.reshape(cols, CHUNKS * k.rc, features)

    def to_own(pair):
        own = plan.rows_in(pair).astype(F32)
        return [own[c * k.rc : (c + 1) * k.rc] for c in chunks]

    def from_blocks(got):
        got = got.reshape(cols, CHUNKS, k.rc, features)
        img = got[:, :, : k.ci].reshape(IMG_LEN, features)
        txt = got[:, :, k.ci :].reshape(txt_pad, features)[:TXT_LEN]
        return jnp.transpose(img).reshape(1, -1), jnp.transpose(txt).reshape(1, -1)

    mask = k.masks()
    pair = plan.rows_home(to_blocks(image_in, text_in))
    level = plan.swap_levels(sides_attn[0], [pair, mods, sides_up[0], sides_down[0]])
    w_qkv, w_out = [filled(plan.gather_weights(level[:6]))], [(filled(plan.gather_weights(level[6:])), 0)]
    x = to_own(pair)
    h1 = [plan.exchange(k.norm_in(mods, x[c], after_norm=(0, 0))) for c in chunks]
    kept = []
    for depth in range(LAYERS):
        last = depth + 1 == LAYERS
        side = [plan.swap_levels(gate(sides_up[depth], h1 if depth else x), h1)]
        w_up.append(plan.gather_weights(side[0]))
        if last:
            side += grads
        joint = None
        for c in chunks:
            joint = k.qkv(h1[c], w_qkv[depth], c, joint, side)
        side = []
        if last:
            side = [k.norm_back(mods, grads[c], gate=(depth, 5)) for c in chunks]
            grad_down = [plan.exchange(one) for one in side]
        heads = k.attend(joint, mask, side)
        side = grad_down if last else []
        save = dict(x=x, h1=h1, joint=joint, heads=heads, branch=[], x1=[], h2=[], act=[], slope=[], down=[])
        next_x, next_h1 = [], []
        sent = [k.project(heads, *w_out[depth], c, side) for c in chunks]
        blocks = [plan.exchange(one) for one in sent]
        side = [plan.swap_levels(gate(sides_down[depth], sent), blocks)]
        w_down.append(plan.gather_weights(side[0]))
        if not last:
            cot = to_blocks(gate(cot_image, sent), cot_text)
            side.append(cot)
        for c in chunks:
            x1, branch, h2 = k.norm_in(mods, x[c], blocks[c], (depth, 2), (depth, 3), side)
            save["x1"].append(x1)
            save["branch"].append(branch)
            save["h2"].append(plan.exchange(h2))
        side = []
        if not last:
            side = [plan.swap_levels(gate(sides_attn[depth + 1], save["x1"]), save["h2"])]
            whole = filled(plan.gather_weights(side[0]))
            w_qkv.append(whole)
            w_out.append((whole, 6))
        parts = []
        for c in chunks:
            act, slope, part = k.mlp(save["h2"][c], w_up[depth], w_down[depth], side)
            parts.append(part)
            save["act"].append(act)
            save["slope"].append(slope)
        kept.append(save)
        if last:
            break
        blocks = [plan.exchange(part) for part in parts]
        pair = plan.rows_home(gate(cot, parts))
        side = [pair, sides_up[depth + 1], sides_down[depth + 1]]
        for c in chunks:
            got = k.norm_in(mods, save["x1"][c], blocks[c], (depth, 5), (depth + 1, 0), side)
            next_x.append(got[0])
            save["down"].append(got[1])
            next_h1.append(plan.exchange(got[2]))
        grads = to_own(pair)
        x, h1 = next_x, next_h1

    start = list(grads)
    mod_grads = [None] * LAYERS
    attn_grads, up_grads, down_grads = [None] * LAYERS, [None] * LAYERS, [None] * LAYERS
    for depth in reversed(range(LAYERS)):
        first = depth + 1 == LAYERS
        save = kept[depth]
        grad_pre, blocks, grad_out, sums2, sums1, next_down = ([] for _ in range(6))
        side = []
        if not first:
            up_grads[depth + 1] = plan.join_sides(up_sum)
            side = [up_grads[depth + 1]]
        down_whole = k.weight_grad("down_grad", grad_down, [(one, None) for one in save["act"]], 1, 2, 0, None, side)
        down_both = plan.scatter_weights(down_whole)
        for c in chunks:
            pre, part = k.mlp_back(grad_down[c], save["slope"][c], w_up[depth], w_down[depth], [down_whole])
            grad_pre.append(pre)
            blocks.append(plan.exchange(part))
        up_whole = k.weight_grad("up_grad", save["h2"], [(one, None) for one in grad_pre], 1, 2, 0, None)
        side = [up_whole]
        if not first:
            attn_sum, _ = plan.sum_levels(attn_both)
            side.append(attn_sum)
        for c in chunks:
            grads[c], got, sums = k.norm_back(
                mods, grads[c], blocks[c], save["x1"][c], (depth, 4), save["branch"][c], (depth, 2), side
            )
            sums2.append(sums)
            grad_out.append(plan.exchange(got))
        up_both = plan.scatter_weights(gate(up_whole, sums2))
        down_sum, _ = plan.sum_levels(down_both)
        side = [down_sum]
        if not first:
            attn_grads[depth + 1] = plan.join_sides(attn_sum)
            side.append(attn_grads[depth + 1])
        grad_heads = None
        for c in chunks:
            grad_heads = k.project_back(grad_out[c], *w_out[depth], c, grad_heads, side)
        grad_qkv = k.attend_back(save["joint"], mask, grad_heads)
        up_sum, _ = plan.sum_levels(up_both)
        side = [up_sum]
        if first:
            last_blocks = [plan.exchange(gate(part, [grad_heads])) for part in parts]
            side += last_blocks
        else:
            image_cut = plan.rows_out(gate(image_rows, [grad_heads]))
            side += [image_cut]
        rights = [(grad_qkv, lambda kind, c=c: (kind, c)) for c in chunks]
        attn_whole = k.weight_grad("qkv_grad", save["h1"], rights, 3, 8, 0, None)
        rights = [(save["heads"], lambda kind, c=c: (c,)) for c in chunks]
        attn_whole = k.weight_grad("out_grad", grad_out, rights, 1, 8, 6, attn_whole)
        if not depth:
            side.append(attn_whole)
        for c in chunks:
            blocks[c] = plan.exchange(k.qkv_back(grad_qkv, w_qkv[depth], c, side))
        down_grads[depth] = plan.join_sides(down_sum)
        side = [attn_whole, down_grads[depth]]
        if first:
            image_rows = []
            for c in chunks:
                x2, down = k.norm_in(mods, save["x1"][c], last_blocks[c], (depth, 5))
                image_rows.append(x2.astype(BF16))
                save["down"].append(down)
            image_rows = jnp.concatenate(image_rows, axis=0)
            side.append(image_rows)
        else:
            image_out, text_out = from_blocks(plan.rows_back(image_cut))
            side.append(image_out)
        for c in chunks:
            if depth:
                grads[c], got, sums = k.norm_back(
                    mods, grads[c], blocks[c], save["x"][c], (depth, 1), kept[depth - 1]["down"][c], (depth - 1, 5), side
                )
                next_down.append(plan.exchange(got))
            else:
                grads[c], sums = k.norm_back(mods, grads[c], blocks[c], save["x"][c], (depth, 1), after=side)
            sums1.append(sums)
        if depth:
            attn_whole = gate(attn_whole, sums1)
        attn_both = plan.scatter_weights(attn_whole[..., :features])
        if first:
            gate2 = []
            for c in chunks:
                moved = start[c] * save["down"][c]
                sums = jnp.stack([jnp.sum(moved[: k.ci], axis=0), jnp.sum(moved[k.ci :], axis=0)])
                gate2.append(jnp.broadcast_to(sums[:, None], (2, 3, D)))
        first_, second, gates = sum(sums1), sum(sums2), sum(gate2)
        mod_grads[depth] = jnp.stack(
            [first_[:, 0], first_[:, 1], second[:, 2], second[:, 0], second[:, 1], gates[:, 2]], axis=1
        )
        gate2, grad_down = sums1, next_down
    up_grads[0] = plan.join_sides(up_sum)
    attn_grads[0] = plan.join_sides(plan.sum_levels(attn_both)[0])
    grad_image, grad_text = from_blocks(
        plan.rows_back(plan.rows_out(jnp.concatenate([one.astype(BF16) for one in grads], axis=0)))
    )

    mod_part = plan.natural(jnp.stack(mod_grads)).reshape(LAYERS, 2, 6, cols, features)
    mod_part = jnp.transpose(mod_part, (3, 1, 0, 2, 4)).reshape(cols, -1)
    mod_all = plan.vectors_out(mod_part).astype(BF16).reshape(rows_count, 2, LAYERS * 6, features)
    mod_cut = [unsort_vectors(mod_all[:, s], 6) for s in range(2)]
    grad_mod = [tn(cond_mine, cut) for cut in mod_cut]
    cond_part = nt(mod_cut[0], mod_image) + nt(mod_cut[1], mod_text)
    cond_sum = lax.psum(lax.all_to_all(cond_part, "row", split_axis=0, concat_axis=0, tiled=True), "col")
    _, silu_pull = jax.vjp(jax.nn.silu, cond_float)
    grad_cond = silu_pull(cond_sum.reshape(1, D))[0]

    grad_qkv_w = [
        merge_columns([[attn_grads[d][2 * kind + s] for kind in range(3)] for d in range(LAYERS)], 3)
        for s in range(2)
    ]
    grad_out_w = [merge_columns([[attn_grads[d][6 + s]] for d in range(LAYERS)], 1) for s in range(2)]
    layered = [
        jnp.stack([grads_[d][s].astype(F32) for d in range(LAYERS)]) for grads_ in (up_grads, down_grads) for s in range(2)
    ]
    return (
        image_out,
        text_out,
        grad_image.astype(F32),
        grad_text.astype(F32),
        grad_cond,
        grad_mod[0],
        grad_mod[1],
        grad_qkv_w[0],
        grad_qkv_w[1],
        grad_out_w[0],
        grad_out_w[1],
        layered[0],
        layered[1],
        layered[2],
        layered[3],
    )


def solution(mesh):
    flat = P("row", "col")
    layered = P(None, "row", "col")
    return jax.shard_map(
        functools.partial(on_device, mesh.shape["row"], mesh.shape["col"]),
        mesh=mesh,
        in_specs=(flat, flat, P("row", None)) + (flat,) * 6 + (layered,) * 4 + (flat, flat),
        out_specs=(flat,) * 4 + (P("row", None),) + (flat,) * 6 + (layered,) * 4,
        check_vma=False,
    )
```

time: 3930 us -> 2120 us (0.54)
  waiting for transfers between devices: 2170 us -> 914 us
  local copies, waits for them, and re-layouts: 651 us -> 137 us
  matrix products: 552 us -> 39.8 us
  Pallas kernels: 0 us -> 460 us
  starting transfers between devices: 8.06 us -> 190 us
  blocking collectives: 318 us -> 151 us
    all_gather x30 -> x7, waiting for transfers between devices: 797 us -> 3.09 us  [gather_weights(): return lax.all_gather(both, 'row', axis=0, axis_index_groups=self.fetch)]
    reduce_scatter x16 -> x6, waiting for transfers between devices: 793 us -> 0.04 us  [scatter_weights(): lax.psum_scatter(whole, 'row', scatter_dimension=0, tiled=True, axis_inde...]
    ppermute x0 -> x28, waiting for transfers between devices: none -> 637 us  [the longest x6 206 us: sum_levels(): lax.ppermute(other, 'col', self.levels).astype(F32)]
    unnamed x102 -> x13, waiting for transfers between devices: 582 us -> 0.21 us
    dot_general x172 -> x42, matrix products: 552 us -> 39.8 us  [dot(): lax.dot_general(a, b, (((ca,), (cb,)), ((), ())), preferred_element_type=...]
    unnamed x558 -> x262, local copies, waits for them, and re-layouts: 514 us -> 27.7 us
    pallas_call x0 -> x52, Pallas kernels: none -> 460 us  [the longest x40 460 us: call(): pl.pallas_call(body, grid=grid, in_specs=in_specs + [pl.BlockSpec(memory_...]
    all_to_all x0 -> x23, waiting for transfers between devices: none -> 273 us  [the longest x17 263 us: exchange(): lax.all_to_all(blocks, ('row', 'col'), 0, 0, tiled=True, axis_index_group...]
  transfers between devices with their start and end apart: 74 -> 64, of which waited for: 52 -> 28; matrix products, arithmetic and copies ran while one was open for 30% -> 15% of each run, Pallas kernels for 0% -> 19%
where the time goes in v1:
time: 2120 us; the launch traced here: 2090 us
  waiting for transfers between devices  914 us (43%)
  Pallas kernels  460 us (22%)
  starting transfers between devices  190 us (9%)
  other arithmetic  177 us (8%)
  blocking collectives  151 us (7%)
  local copies, waits for them, and re-layouts  137 us (6%)
  matrix products  39.8 us (2%)
    pallas_call x40, Pallas kernels, call(): pl.pallas_call(body, grid=grid, in_specs=in_specs + [pl.BlockSpec(memory_...  460 us
    all_to_all x17, waiting for transfers between devices, exchange(): lax.all_to_all(blocks, ('row', 'col'), 0, 0, tiled=True, axis_index_group...  263 us
    ppermute x6, waiting for transfers between devices, sum_levels(): lax.ppermute(other, 'col', self.levels).astype(F32)  206 us
    ppermute x6, waiting for transfers between devices, join_sides(): lax.ppermute(other, 'row', self.across)  172 us
    ppermute x6, waiting for transfers between devices, swap_levels(): lax.ppermute(both, 'col', self.levels)  132 us
    all_to_all x3, blocking collectives, exchange(): lax.all_to_all(blocks, ('row', 'col'), 0, 0, tiled=True, axis_index_group...  128 us
    ppermute x6, waiting for transfers between devices, swap_sides(): lax.ppermute(other, 'row', self.across)  119 us
    all_to_all x17, starting transfers between devices, exchange(): lax.all_to_all(blocks, ('row', 'col'), 0, 0, tiled=True, axis_index_group...  85.4 us
  transfers between devices with their start and end apart: 64, of which 28 were waited for; matrix products, arithmetic and copies ran while one was open for 15% of the time, Pallas kernels for 19%

profile of v1, /device:TPU:0, one launch (start us, length us, event | category | flops | bytes accessed | tf_op | source)
XLA Modules:
  0.0 2088.6 jit_solution(8449091005816847696)
XLA Ops:
  136.5 34.9 %collective-permute-done.4 = bf16[8,384,192]{1,2,0:T(8,128)(2,1)} collective-permute-done((bf16[8,384,192]{1,2,0:T(8,128)(2,1)}, bf16[8,384,192]{1,2,0:T(8,128)(2,1)}, u32[]{:S(2)}, u32[]{:S(2)}) %collective-permute-start.4) | collective-permute-done | bytes 1179680 | tf_op jit(solution)/shard_map/ppermute | solution.py:95
  179.4 27.6 %all_to_all.154 = bf16[4,2,320,384]{3,2,1,0:T(8,128)(2,1)S(1)} all-to-all(bf16[4,2,320,384]{3,2,1,0:T(8,128)(2,1)} %pad_maximum_fusion.6.refs_1_), channel_id=1, replica_groups={{0,1,8,9},{2,3,10,11},{4,5,12,13},{6,7,14,15},{16,17,24,25},{18,19,26,2..., dimensions={0} | all-to-all | bytes 3932160 | tf_op jit(solution)/shard_map/all_to_all | solution.py:62
  231.8 64.6 %all-to-all-done.4.refs_1_.refs_0_ = bf16[4,320,1536]{2,1,0:T(8,128)(2,1)} async-done(((bf16[4,320,1536]{2,1,0:T(8,128)(2,1)}), bf16[4,320,1536]{2,1,0:T(8,128)(2,1)}, u32[]{:S(2)}, u32[]{:S(2)}) %all-to-all-start.4) | async-done | bytes 3932192 | tf_op jit(solution)/shard_map/all_to_all | solution.py:62
  347.1 67.2 %all-to-all-done.5.refs_1_ = bf16[4,320,1536]{2,1,0:T(8,128)(2,1)} async-done(((bf16[4,320,1536]{2,1,0:T(8,128)(2,1)}), bf16[4,320,1536]{2,1,0:T(8,128)(2,1)}, u32[]{:S(2)}, u32[]{:S(2)}) %all-to-all-start.5) | async-done | bytes 3932192 | tf_op jit(solution)/shard_map/all_to_all | solution.py:62
  458.6 57.3 %collective-permute-done.7 = bf16[8,192,192]{2,1,0:T(8,128)(2,1)S(1)} collective-permute-done((bf16[8,192,192]{2,1,0:T(8,128)(2,1)S(1)}, bf16[8,192,192]{2,1,0:T(8,128)(2,1)S(1)}, u32[]{:S(2)}, u32[]{:S(2)}) %collective-permute-start.7) | collective-permute-done | bytes 589856 | tf_op jit(solution)/shard_map/ppermute | solution.py:89
  520.6 53.1 %collective-permute-done.8 = bf16[8,384,192]{1,2,0:T(8,128)(2,1)S(1)} collective-permute-done((bf16[8,384,192]{1,2,0:T(8,128)(2,1)}, bf16[8,384,192]{1,2,0:T(8,128)(2,1)S(1)}, u32[]{:S(2)}, u32[]{:S(2)}) %collective-permute-start.8) | collective-permute-done | bytes 1179680 | tf_op jit(solution)/shard_map/ppermute | solution.py:95
  581.1 23.9 %mlp.2 = (bf16[4,320,1536]{2,1,0:T(8,128)(2,1)}, bf16[4,320,1536]{2,1,0:T(8,128)(2,1)}, bf16[4,320,1536]{2,1,0:T(8,128)(2,1)}) custom-call(bf16[4,320,1536]{2,1,0:T(8,128)(2,1)} %all-to-all-done.6.refs_1_.refs_0_, bf16[4,320,1536]{2,1,0:T(8,128)(2,1)} %all-to-all-done.6.refs_1_.refs_0_, bf16[4,2,384,1536]{3,2,1,0:T(8,128)(2,1)} %bitcast.385, ...), custom_call_target="tpu_custom_call" | custom-call | flops 12079595520 | bytes 57409536 | tf_op jit(solution)/shard_map/mlp/pallas_call | solution.py:195
  615.7 52.8 %collective-permute-done.10 = bf16[2,192,768]{2,1,0:T(8,128)(2,1)} collective-permute-done((bf16[2,192,768]{2,1,0:T(8,128)(2,1)}, bf16[2,192,768]{2,1,0:T(8,128)(2,1)}, u32[]{:S(2)}, u32[]{:S(2)}) %collective-permute-start.10) | collective-permute-done | bytes 589856 | tf_op jit(solution)/shard_map/ppermute | solution.py:89
  692.6 50.2 %all_to_all.155.refs_1_.refs_0_ = bf16[4,320,1536]{2,1,0:T(8,128)(2,1)} all-to-all(bf16[4,320,1536]{2,1,0:T(8,128)(2,1)} %get-tuple-element.51), channel_id=1, replica_groups={{0,1,8,9},{2,3,10,11},{4,5,12,13},{6,7,14,15},{16,17,24,25},{18,19,26,2..., dimensions={0} | all-to-all | bytes 7864320 | tf_op jit(solution)/shard_map/all_to_all | solution.py:62
  750.5 44.3 %collective-permute-done.12 = bf16[2,384,768]{2,1,0:T(8,128)(2,1)} collective-permute-done((bf16[2,384,768]{2,1,0:T(8,128)(2,1)}, bf16[2,384,768]{2,1,0:T(8,128)(2,1)}, u32[]{:S(2)}, u32[]{:S(2)}) %collective-permute-start.12) | collective-permute-done | bytes 1179680 | tf_op jit(solution)/shard_map/ppermute | solution.py:95
  876.6 69.8 %all-to-all-done.11.refs_1_ = bf16[4,320,1536]{2,1,0:T(8,128)(2,1)} async-done(((bf16[4,320,1536]{2,1,0:T(8,128)(2,1)}), bf16[4,320,1536]{2,1,0:T(8,128)(2,1)}, u32[]{:S(2)}, u32[]{:S(2)}) %all-to-all-start.11) | async-done | bytes 3932192 | tf_op jit(solution)/shard_map/all_to_all | solution.py:62
  960.8 50.3 %all_to_all.156.refs_0_.refs_1_ = bf16[4,320,1536]{2,1,0:T(8,128)(2,1)} all-to-all(bf16[4,320,1536]{2,1,0:T(8,128)(2,1)} %get-tuple-element.53), channel_id=1, replica_groups={{0,1,8,9},{2,3,10,11},{4,5,12,13},{6,7,14,15},{16,17,24,25},{18,19,26,2..., dimensions={0} | all-to-all | bytes 7864320 | tf_op jit(solution)/shard_map/all_to_all | solution.py:62
  1086.6 34.2 %all-to-all-done.13.refs_1_ = bf16[4,320,1536]{2,1,0:T(8,128)(2,1)} async-done(((bf16[4,320,1536]{2,1,0:T(8,128)(2,1)}), bf16[4,320,1536]{2,1,0:T(8,128)(2,1)}, u32[]{:S(2)}, u32[]{:S(2)}) %all-to-all-start.13) | async-done | bytes 3932192 | tf_op jit(solution)/shard_map/all_to_all | solution.py:62
  1139.5 62.9 %collective-permute-done.14 = bf16[2,384,768]{2,1,0:T(8,128)(2,1)S(1)} collective-permute-done((bf16[2,384,768]{2,1,0:T(8,128)(2,1)S(1)}, bf16[2,384,768]{2,1,0:T(8,128)(2,1)S(1)}, u32[]{:S(2)}, u32[]{:S(2)}) %collective-permute-start.14) | collective-permute-done | bytes 1179680 | tf_op jit(solution)/shard_map/ppermute | solution.py:111
  1220.8 45.5 %attend_back.2 = bf16[3,1280,384]{2,1,0:T(8,128)(2,1)} custom-call(bf16[1280,1152]{1,0:T(8,128)(2,1)} %bitcast.465, bf16[1280,1152]{1,0:T(8,128)(2,1)} %bitcast.466, bf16[1280,1152]{1,0:T(8,128)(2,1)} %bitcast.467, bf16[1280,1]{1,0:T(8,128)(2,1)} %select_convert_fusion.refs_3_, bf16[1280,384]{1,0:T(8,128)(2,1)} %bitcast.450), custom_call_target="tpu_custom_call" | custom-call | flops 12582912000 | bytes 12782080 | tf_op jit(solution)/shard_map/attend_back/pallas_call | solution.py:195
  1326.9 32.6 %collective-permute-done.16 = bf16[2,192,768]{2,1,0:T(8,128)(2,1)S(1)} collective-permute-done((bf16[2,192,768]{2,1,0:T(8,128)(2,1)S(1)}, bf16[2,192,768]{2,1,0:T(8,128)(2,1)S(1)}, u32[]{:S(2)}, u32[]{:S(2)}) %collective-permute-start.16) | collective-permute-done | bytes 589856 | tf_op jit(solution)/shard_map/ppermute | solution.py:118
  1386.6 54.3 %collective-permute-done.17 = bf16[2,192,768]{2,1,0:T(8,128)(2,1)S(1)} collective-permute-done((bf16[2,192,768]{2,1,0:T(8,128)(2,1)S(1)}, bf16[2,192,768]{2,1,0:T(8,128)(2,1)S(1)}, u32[]{:S(2)}, u32[]{:S(2)}) %collective-permute-start.17) | collective-permute-done | bytes 589856 | tf_op jit(solution)/shard_map/ppermute | solution.py:118
  1497.1 50.8 %collective-permute-done.18 = bf16[8,384,192]{1,2,0:T(8,128)(2,1)} collective-permute-done((bf16[8,384,192]{1,2,0:T(8,128)(2,1)}, bf16[8,384,192]{1,2,0:T(8,128)(2,1)}, u32[]{:S(2)}, u32[]{:S(2)}) %collective-permute-start.18) | collective-permute-done | bytes 1179680 | tf_op jit(solution)/shard_map/ppermute | solution.py:111
  1575.3 53.7 %collective-permute-done.20 = bf16[8,192,192]{2,1,0:T(8,128)(2,1)S(1)} collective-permute-done((bf16[8,192,192]{2,1,0:T(8,128)(2,1)S(1)}, bf16[8,192,192]{2,1,0:T(8,128)(2,1)S(1)}, u32[]{:S(2)}, u32[]{:S(2)}) %collective-permute-start.20) | collective-permute-done | bytes 589856 | tf_op jit(solution)/shard_map/ppermute | solution.py:118
  1644.8 45.2 %attend_back.3 = bf16[3,1280,384]{2,1,0:T(8,128)(2,1)} custom-call(bf16[1280,1152]{1,0:T(8,128)(2,1)} %bitcast.459, bf16[1280,1152]{1,0:T(8,128)(2,1)} %bitcast.460, bf16[1280,1152]{1,0:T(8,128)(2,1)} %bitcast.461, bf16[1280,1]{1,0:T(8,128)(2,1)} %select_convert_fusion.refs_3_, bf16[1280,384]{1,0:T(8,128)(2,1)} %bitcast.452), custom_call_target="tpu_custom_call" | custom-call | flops 12582912000 | bytes 12782080 | tf_op jit(solution)/shard_map/attend_back/pallas_call | solution.py:195
  1725.4 51.2 %collective-permute-done.22 = bf16[2,384,768]{2,1,0:T(8,128)(2,1)S(1)} collective-permute-done((bf16[2,384,768]{2,1,0:T(8,128)(2,1)S(1)}, bf16[2,384,768]{2,1,0:T(8,128)(2,1)S(1)}, u32[]{:S(2)}, u32[]{:S(2)}) %collective-permute-start.22) | collective-permute-done | bytes 1179680 | tf_op jit(solution)/shard_map/ppermute | solution.py:111
  1819.0 31.0 %collective-permute-done.23 = bf16[2,192,768]{2,1,0:T(8,128)(2,1)S(1)} collective-permute-done((bf16[2,192,768]{2,1,0:T(8,128)(2,1)S(1)}, bf16[2,192,768]{2,1,0:T(8,128)(2,1)S(1)}, u32[]{:S(2)}, u32[]{:S(2)}) %collective-permute-start.23) | collective-permute-done | bytes 589856 | tf_op jit(solution)/shard_map/ppermute | solution.py:118
  1928.2 31.5 %collective-permute-start.26 = (bf16[8,192,192]{2,1,0:T(8,128)(2,1)}, bf16[8,192,192]{2,1,0:T(8,128)(2,1)}, u32[]{:S(2)}, u32[]{:S(2)}) collective-permute-start(bf16[8,192,192]{2,1,0:T(8,128)(2,1)} %broadcast_select_fusion.20), channel_id=1, source_target_pairs={{0,8},{4,12},{8,0},{12,4},{16,24},{20,28},{24,16},{28,20},{1,9},{5... | collective-permute-start | bytes 1769480 | tf_op jit(solution)/shard_map/ppermute | solution.py:118
  2046.5 23.5 %psum.7 = f32[1,1536]{1,0:T(1,128)S(1)} all-reduce(f32[1,1536]{1,0:T(1,128)S(1)} %reshape.411), channel_id=1, replica_groups=mesh['row'=8,'col'=4] {'col'}, use_global_device_ids=true, to_apply=%region_10.11 | all-reduce | flops 1536 | bytes 12288 | tf_op jit(solution)/shard_map/psum | solution.py:988
  (739 shorter events, 955.6 us)
Async XLA Ops:
  39.2 90.5 %collective-permute-start = (bf16[4,320,384]{2,1,0:T(8,128)(2,1)}, bf16[4,320,384]{2,1,0:T(8,128)(2,1)}, u32[]{:S(2)}, u32[]{:S(2)}) collective-permute-start(bf16[4,320,384]{2,1,0:T(8,128)(2,1)} %maximum_bitcast_fusion), channel_id=1, source_target_pairs={{2,0},{3,1},{8,10},{9,11},{6,4},{7,5},{12,14},{13,15},{18,16},{19,... | collective-permute-start | bytes 2949128 | tf_op jit(solution)/shard_map/ppermute | solution.py:123
  114.4 190.3 %all-gather.15.cloned.1.call-start = ((), (), s32[]{:S(2)}) async-start(), calls=%async_computation.38 | async-start | bytes 8847360 | tf_op jit(solution)/shard_map/all_gather | solution.py:100
  222.9 73.5 %all-to-all-start.4 = ((bf16[4,320,1536]{2,1,0:T(8,128)(2,1)}), bf16[4,320,1536]{2,1,0:T(8,128)(2,1)}, u32[]{:S(2)}, u32[]{:S(2)}) async-start(bf16[4,320,1536]{2,1,0:T(8,128)(2,1)} %norm_in.5), calls=%async_computation.4 | async-start | bytes 7864320 | tf_op jit(solution)/shard_map/all_to_all | solution.py:62
  227.8 107.6 %all-gather.17.cloned.1.call-start = ((), (), s32[]{:S(2)}) async-start(), calls=%async_computation.39 | async-start | bytes 2949120 | tf_op jit(solution)/shard_map/all_gather | solution.py:100
  229.9 351.2 %all-gather.19.cloned.1.call-start = ((), (), s32[]{:S(2)}) async-start(), calls=%async_computation.40 | async-start | bytes 11796480 | tf_op jit(solution)/shard_map/all_gather | solution.py:100
  346.3 234.8 %all-gather.21.cloned.1.call-start = ((), (), s32[]{:S(2)}) async-start(), calls=%async_computation.41 | async-start | bytes 11796480 | tf_op jit(solution)/shard_map/all_gather | solution.py:100
  450.4 124.9 %all-to-all-start.6 = ((bf16[4,320,1536]{2,1,0:T(8,128)(2,1)}), bf16[4,320,1536]{2,1,0:T(8,128)(2,1)}, u32[]{:S(2)}, u32[]{:S(2)}) async-start(bf16[4,320,1536]{2,1,0:T(8,128)(2,1)} %get-tuple-element.48), calls=%async_computation.6 | async-start | bytes 7864320 | tf_op jit(solution)/shard_map/all_to_all | solution.py:62
  455.4 365.0 %all-gather.23.cloned.1.call-start = ((), (), s32[]{:S(2)}) async-start(), calls=%async_computation.42 | async-start | bytes 11796480 | tf_op jit(solution)/shard_map/all_gather | solution.py:100
  605.1 79.8 %all-to-all-start.7 = ((bf16[4,320,1536]{2,1,0:T(8,128)(2,1)}), bf16[4,320,1536]{2,1,0:T(8,128)(2,1)}, u32[]{:S(2)}, u32[]{:S(2)}) async-start(bf16[4,320,1536]{2,1,0:T(8,128)(2,1)} %get-tuple-element.49.refs_1_), calls=%async_computation.7 | async-start | bytes 7864320 | tf_op jit(solution)/shard_map/all_to_all | solution.py:62
  747.3 263.9 %all-gather.25.cloned.1.call-start = ((), (), s32[]{:S(2)}) async-start(), calls=%async_computation.43 | async-start | bytes 11796480 | tf_op jit(solution)/shard_map/all_gather | solution.py:100
  871.6 74.7 %all-to-all-start.11 = ((bf16[4,320,1536]{2,1,0:T(8,128)(2,1)}), bf16[4,320,1536]{2,1,0:T(8,128)(2,1)}, u32[]{:S(2)}, u32[]{:S(2)}) async-start(bf16[4,320,1536]{2,1,0:T(8,128)(2,1)} %project.3.refs_1_), calls=%async_computation.11 | async-start | bytes 7864320 | tf_op jit(solution)/shard_map/all_to_all | solution.py:62
  876.4 137.8 %all-gather.27.cloned.1.call-start = ((), (), s32[]{:S(2)}) async-start(), calls=%async_computation.44 | async-start | bytes 11796480 | tf_op jit(solution)/shard_map/all_gather | solution.py:100
  876.5 73.0 %collective-permute-start.13 = (bf16[2,384,768]{2,1,0:T(8,128)(2,1)}, bf16[2,384,768]{2,1,0:T(8,128)(2,1)}, u32[]{:S(2)}, u32[]{:S(2)}) collective-permute-start(bf16[2,384,768]{2,1,0:T(8,128)(2,1)} %gate.18), channel_id=1, source_target_pairs={{0,2},{1,3},{2,0},{3,1},{4,6},{5,7},{6,4},{7,5},{8,10},{9,11},{10,... | collective-permute-start | bytes 3538952 | tf_op jit(solution)/shard_map/ppermute | solution.py:95
  952.5 182.4 %reduce-scatter.7.cloned.1.call-start = ((), (), s32[]{:S(2)}) async-start(), calls=%async_computation.32 | async-start | bytes 11796480 | tf_op jit(solution)/shard_map/reduce_scatter | solution.py:104
  1075.4 141.3 %reduce-scatter.9.cloned.1.call-start = ((), (), s32[]{:S(2)}) async-start(), calls=%async_computation.33 | async-start | bytes 11796480 | tf_op jit(solution)/shard_map/reduce_scatter | solution.py:104
  1130.1 74.6 %all-to-all-start.14 = ((bf16[4,320,1536]{2,1,0:T(8,128)(2,1)}), bf16[4,320,1536]{2,1,0:T(8,128)(2,1)}, u32[]{:S(2)}, u32[]{:S(2)}) async-start(bf16[4,320,1536]{2,1,0:T(8,128)(2,1)} %get-tuple-element.60), calls=%async_computation.14 | async-start | bytes 7864320 | tf_op jit(solution)/shard_map/all_to_all | solution.py:62
  1210.6 76.1 %all-to-all-start.15 = ((bf16[4,320,1536]{2,1,0:T(8,128)(2,1)}), bf16[4,320,1536]{2,1,0:T(8,128)(2,1)}, u32[]{:S(2)}, u32[]{:S(2)}) async-start(bf16[4,320,1536]{2,1,0:T(8,128)(2,1)} %gate.19), calls=%async_computation.16 | async-start | bytes 7864320 | tf_op jit(solution)/shard_map/all_to_all | solution.py:62
  1303.8 176.8 %reduce-scatter.11.cloned.1.call-start = ((), (), s32[]{:S(2)}) async-start(), calls=%async_computation.34 | async-start | bytes 11796480 | tf_op jit(solution)/shard_map/reduce_scatter | solution.py:104
  1384.5 184.4 %reduce-scatter.13.cloned.1.call-start = ((), (), s32[]{:S(2)}) async-start(), calls=%async_computation.35 | async-start | bytes 11796480 | tf_op jit(solution)/shard_map/reduce_scatter | solution.py:104
  1475.7 77.9 %all-to-all-start.18 = ((bf16[4,320,1536]{2,1,0:T(8,128)(2,1)}), bf16[4,320,1536]{2,1,0:T(8,128)(2,1)}, u32[]{:S(2)}, u32[]{:S(2)}) async-start(bf16[4,320,1536]{2,1,0:T(8,128)(2,1)} %get-tuple-element.69), calls=%async_computation.20 | async-start | bytes 7864320 | tf_op jit(solution)/shard_map/all_to_all | solution.py:62
  1480.5 241.4 %reduce-scatter.15.cloned.1.call-start = ((), (), s32[]{:S(2)}) async-start(), calls=%async_computation.36 | async-start | bytes 11796480 | tf_op jit(solution)/shard_map/reduce_scatter | solution.py:104
  1563.0 75.8 %all-to-all-start.19 = ((bf16[4,320,1536]{2,1,0:T(8,128)(2,1)}), bf16[4,320,1536]{2,1,0:T(8,128)(2,1)}, u32[]{:S(2)}, u32[]{:S(2)}) async-start(bf16[4,320,1536]{2,1,0:T(8,128)(2,1)} %get-tuple-element.73), calls=%async_computation.22 | async-start | bytes 7864320 | tf_op jit(solution)/shard_map/all_to_all | solution.py:62
  1569.0 292.5 %reduce-scatter.17.cloned.1.call-start = ((), (), s32[]{:S(2)}) async-start(), calls=%async_computation.37 | async-start | bytes 11796480 | tf_op jit(solution)/shard_map/reduce_scatter | solution.py:104
  1790.4 102.9 %all-to-all-start.21 = ((bf16[4,320,1536]{2,1,0:T(8,128)(2,1)}), bf16[4,320,1536]{2,1,0:T(8,128)(2,1)}, u32[]{:S(2)}, u32[]{:S(2)}) async-start(bf16[4,320,1536]{2,1,0:T(8,128)(2,1)} %qkv_back.3), calls=%async_computation.26 | async-start | bytes 7864320 | tf_op jit(solution)/shard_map/all_to_all | solution.py:62
  (161 other events, 3042.5 us)
Sparse Core Ops, SparseCore 0:
  179.6 50.9 all-gather.14
  232.7 24.0 all-gather.16
  302.7 63.6 all-gather.18
  420.7 61.8 all-gather.20
  581.2 60.3 all-gather.22
  797.9 61.4 all-gather.24
  952.6 61.4 all-gather.26
  1048.4 78.4 reduce-scatter.6
  1130.2 77.8 reduce-scatter.8
  1379.5 76.1 reduce-scatter.10
  1458.3 78.4 reduce-scatter.12
  1563.1 78.8 reduce-scatter.14
  1711.2 78.3 reduce-scatter.16

commit v2 on v1

--- a/solution.py
+++ b/solution.py
@@ -52,6 +52,9 @@
             self.team = [
                 [flat(a, x, k, h, l) for x in range(2) for l in range(half)] for a, k in sides for h in range(2)
             ]
+            self.plane = [
+                [flat(a, x, k, h, l) for x in range(2) for h in range(2) for l in range(half)] for a, k in sides
+            ]
             self.home = [(flat(a, x, k, 1 - x, l), flat(a, x, k, x, l)) for a, k in sides for x in range(2) for l in range(half)]
             self.across = [(r, r ^ 2) for r in range(rows)]
             self.levels = [(c, (c + half) % cols) for c in range(cols)]
@@ -80,12 +83,14 @@
     def place(self, index, mine, other):
         return jnp.where(index == 0, mine, other), jnp.where(index == 0, other, mine)
 
-    def swap_sides(self, pieces):
+    def swap_sides(self, pieces, after=()):
         mine = jnp.stack(pieces)
         if not self.swap:
             return mine
         wide = mine.shape[2] // 2
         mine, other = self.pick(self.x, [mine[:, :, :wide], mine[:, :, wide:]])
+        if len(after):
+            other = gate(other, after)
         return jnp.concatenate(self.place(self.x, mine, lax.ppermute(other, "row", self.across)), axis=1)
 
     def swap_levels(self, both, after=()):
@@ -123,16 +128,37 @@
         moved = lax.ppermute(blocks, ("row", "col"), self.home)
         return jnp.stack(self.place(self.h, blocks, moved), axis=1)
 
-    def rows_in(self, pair):
+    def rows_in(self, pair, kernels, after=()):
         got = self.exchange(pair)
+        if self.swap and kernels is not None:
+            return kernels.enter(self, got.reshape((2, 2) + got.shape[1:]), (1, 0), after)
         if not self.swap:
             return jnp.transpose(got, (1, 0, 2)).reshape(got.shape[1], D)
         got = got.reshape((2, self.cols // 2) + got.shape[1:])
         got = jnp.where(self.h == 0, got[0], got[1])
         return self.inner(jnp.transpose(got, (2, 1, 0, 3)).reshape(got.shape[2], D))
 
-    def rows_out(self, own):
-        tokens = own.shape[0]
+    def rows_over(self, blocks, kernels):
+        if not self.swap or kernels is None:
+            return self.rows_in(self.rows_home(blocks), kernels)
+        cut = blocks.reshape((2, 1, self.cols // 2) + blocks.shape[1:])
+        cut = jnp.broadcast_to(cut, (2, 2) + cut.shape[2:]).reshape((2 * self.cols,) + blocks.shape[1:])
+        got = lax.all_to_all(cut, ("row", "col"), 0, 0, tiled=True, axis_index_groups=self.plane)
+        return kernels.enter(self, got.reshape((2, 2, self.cols // 2) + blocks.shape[1:]), (0, 1))
+
+    def rows_home_again(self, own, kernels, first=(), second=()):
+        if not self.swap or kernels is None:
+            return self.rows_back(self.rows_out(own, kernels)), own
+        cut = kernels.leave(own, first)
+        cut = cut.reshape((2 * self.cols,) + cut.shape[2:])
+        got = lax.all_to_all(cut, ("row", "col"), 0, 0, tiled=True, axis_index_groups=self.plane)
+        got = got.reshape((2, 2, self.cols // 2) + got.shape[1:])
+        x = tick(self.x, second) if len(second) else self.x
+        got = jnp.where(x == 0, got[:, 0], got[:, 1])
+        return got.reshape((self.cols,) + got.shape[2:]), cut
+
+    def rows_out(self, own, kernels):
+        tokens, own = own.shape[0], own.astype(BF16)
         if not self.swap:
             return self.exchange(jnp.transpose(own.reshape(tokens, self.cols, -1), (1, 0, 2)))
         cut = self.natural(own).reshape(tokens, 2, self.cols // 2, D // self.cols)
@@ -146,28 +172,33 @@
         back = lax.ppermute(other, ("row", "col"), [(b, a) for a, b in self.home])
         return jnp.where(self.x == self.h, mine, back)
 
-    def vectors_in(self, part):
-        if not self.swap:
-            mine = jnp.sum(lax.all_to_all(part, "row", 0, 0, tiled=True), axis=0, keepdims=True)
-            return lax.all_to_all(jnp.broadcast_to(mine, (self.cols, mine.shape[1])), "col", 0, 0, tiled=True)
+    def vectors_rows(self, part):
+        if not self.swap:
+            return jnp.sum(lax.all_to_all(part, "row", 0, 0, tiled=True), axis=0, keepdims=True)
         cut = part.reshape(self.rows // 4, 1, 2, 2, -1)
         cut = jnp.broadcast_to(cut, (self.rows // 4, 2) + cut.shape[2:])
         sent = jnp.transpose(cut, (0, 1, 3, 2, 4)).reshape(self.rows, 2, -1)
-        mine = jnp.sum(lax.all_to_all(sent, "row", 0, 0, tiled=True), axis=0)
+        return jnp.sum(lax.all_to_all(sent, "row", 0, 0, tiled=True), axis=0)
+
+    def vectors_cols(self, mine):
+        if not self.swap:
+            return lax.all_to_all(jnp.broadcast_to(mine, (self.cols, mine.shape[1])), "col", 0, 0, tiled=True)
         half = self.cols // 2
         sent = jnp.broadcast_to(mine[:, None], (2, half, mine.shape[1])).reshape(self.cols, -1)
         return lax.all_to_all(sent, "col", 0, 0, tiled=True)
 
-    def vectors_out(self, part):
+    def vectors_cols_back(self, part):
         got = lax.all_to_all(part, "col", 0, 0, tiled=True)
         if not self.swap:
-            mine = jnp.sum(got, axis=0, keepdims=True)
-            return lax.all_to_all(jnp.broadcast_to(mine, (self.rows, mine.shape[1])), "row", 0, 0, tiled=True)
-        mine = jnp.sum(got.reshape(2, self.cols // 2, -1), axis=1)
+            return jnp.sum(got, axis=0, keepdims=True)
+        return jnp.sum(got.reshape(2, self.cols // 2, -1), axis=1)
+
+    def vectors_rows_back(self, mine):
         every = lax.all_to_all(jnp.broadcast_to(mine[None], (self.rows,) + mine.shape), "row", 0, 0, tiled=True)
+        if not self.swap:
+            return every.reshape(self.rows, -1)
         every = jnp.sum(every.reshape(self.rows // 4, 2, 2, 2, -1), axis=1)
         return jnp.transpose(every, (0, 2, 1, 3)).reshape(self.rows, -1)
-
 
 def norm(x):
     average = jnp.mean(x, axis=1, keepdims=True)
@@ -176,7 +207,7 @@
     return centred * inverse, inverse
 
 
-def call(kernel, name, grid, ins, outs, flops=0, after=(), alias=None, scratch=(), transcendentals=0):
+def call(kernel, name, grid, ins, outs, flops=0, after=(), alias=None, scratch=(), transcendentals=0, room=58):
     args = [a for a, _, _ in ins]
     in_specs = [pl.BlockSpec(block, index) for _, block, index in ins]
     extra = list(after)
@@ -200,9 +231,9 @@
         out_shape=[jax.ShapeDtypeStruct(shape, dtype) for shape, dtype, _, _ in outs],
         scratch_shapes=list(scratch),
         input_output_aliases=aliases,
-        compiler_params=pltpu.CompilerParams(vmem_limit_bytes=58 << 20),
+        compiler_params=pltpu.CompilerParams(vmem_limit_bytes=room << 20),
         cost_estimate=pl.CostEstimate(
-            flops=flops, bytes_accessed=moved, transcendentals=transcendentals
+            flops=flops // 8, bytes_accessed=moved // 8, transcendentals=transcendentals // 8
         ),
         name=name,
     )(*args, *extra)
@@ -240,17 +271,18 @@
         self.wide, self.hidden = wide, hidden
         self.tokens = members * self.rc * chunks
 
-    def sides(self, array, columns, index, lead=None):
-        q, ratio = self.q, self.ci // self.ct
+    def rows(self, array, columns, index, lead=None):
         if lead is None:
-            return [
-                (array, (q, self.ci, columns), lambda *i: (0, 0, index(*i))),
-                (array, (q, self.ct, columns), lambda *i: (0, ratio, index(*i))),
-            ]
-        return [
-            (array, (1,) * len(lead(0)) + (q, self.ci, columns), lambda *i: lead(*i) + (0, 0, index(*i))),
-            (array, (1,) * len(lead(0)) + (q, self.ct, columns), lambda *i: lead(*i) + (0, ratio, index(*i))),
-        ]
+            return [(array, (self.q, self.rc, columns), lambda *i: (0, 0, index(*i)))]
+        return [(array, (1,) * len(lead(0)) + (self.q, self.rc, columns), lambda *i: lead(*i) + (0, 0, index(*i)))]
+
+    def image(self, ref):
+        value = ref[..., : self.ci, :]
+        return value.reshape(-1, value.shape[-1])
+
+    def text(self, ref):
+        value = ref[..., self.ci :, :]
+        return value.reshape(-1, value.shape[-1])
 
     def weight(self, array, columns, piece, index):
         return [
@@ -267,14 +299,14 @@
         ref[..., self.ci :, :] = txt.astype(ref.dtype).reshape(cut + (self.ct, ref.shape[-1]))
 
     def qkv(self, h, weights, chunk, joint, after=()):
-        def kernel(hi, ht, wi, wt, out):
-            self.put(out, nn(self.flat(hi), self.flat(wi)), nn(self.flat(ht), self.flat(wt)))
+        def kernel(h, wi, wt, out):
+            self.put(out, nn(self.image(h), self.flat(wi)), nn(self.text(h), self.flat(wt)))
 
         return call(
             kernel,
             "qkv",
             (3,),
-            self.sides(h, D, lambda j: 0) + self.weight(weights, self.wide, lambda j: 2 * j, lambda j: 0),
+            self.rows(h, D, lambda j: 0) + self.weight(weights, self.wide, lambda j: 2 * j, lambda j: 0),
             [
                 (
                     (self.n, self.q, self.rc, 3 * self.wide),
@@ -289,14 +321,14 @@
         )
 
     def project(self, heads, weights, piece, chunk, after=()):
-        def kernel(hi, ht, wi, wt, out):
-            self.put(out, nt(self.flat(hi), self.flat(wi)), nt(self.flat(ht), self.flat(wt)))
+        def kernel(h, wi, wt, out):
+            self.put(out, nt(self.image(h), self.flat(wi)), nt(self.text(h), self.flat(wt)))
 
         return call(
             kernel,
             "project",
             (1,),
-            self.sides(heads, self.wide, lambda i: 0, lambda i: (chunk,))
+            self.rows(heads, self.wide, lambda i: 0, lambda i: (chunk,))
             + self.weight(weights, self.wide, lambda i: piece, lambda i: 0),
             [((self.q, self.rc, D), BF16, (self.q, self.rc, D), lambda i: (0, 0, 0))],
             flops=2 * self.q * self.rc * D * self.wide,
@@ -304,14 +336,14 @@
         )
 
     def project_back(self, grad, weights, piece, chunk, joint, after=()):
-        def kernel(hi, ht, wi, wt, out):
-            self.put(out, nn(self.flat(hi), self.flat(wi)), nn(self.flat(ht), self.flat(wt)))
+        def kernel(h, wi, wt, out):
+            self.put(out, nn(self.image(h), self.flat(wi)), nn(self.text(h), self.flat(wt)))
 
         return call(
             kernel,
             "project_back",
             (1,),
-            self.sides(grad, D, lambda i: 0) + self.weight(weights, self.wide, lambda i: piece, lambda i: 0),
+            self.rows(grad, D, lambda i: 0) + self.weight(weights, self.wide, lambda i: piece, lambda i: 0),
             [
                 (
                     (self.n, self.q, self.rc, self.wide),
@@ -326,9 +358,9 @@
         )
 
     def qkv_back(self, grads, weights, chunk, after=()):
-        def kernel(hi, ht, wi, wt, out, sum_i, sum_t):
+        def kernel(h, wi, wt, out, sum_i, sum_t):
             j = pl.program_id(0)
-            img, txt = nt(self.flat(hi), self.flat(wi)), nt(self.flat(ht), self.flat(wt))
+            img, txt = nt(self.image(h), self.flat(wi)), nt(self.text(h), self.flat(wt))
 
             @pl.when(j == 0)
             def _():
@@ -348,7 +380,7 @@
             kernel,
             "qkv_back",
             (3,),
-            self.sides(grads, self.wide, lambda j: 0, lambda j: (j, chunk))
+            self.rows(grads, self.wide, lambda j: 0, lambda j: (j, chunk))
             + self.weight(weights, self.wide, lambda j: 2 * j, lambda j: 0),
             [((self.q, self.rc, D), BF16, (self.q, self.rc, D), lambda j: (0, 0, 0))],
             flops=2 * self.q * self.rc * D * 3 * self.wide,
@@ -367,10 +399,10 @@
             slope = half + 0.5 * v * (1.0 - t * t) * (0.7978845608028654 * (1.0 + 3 * 0.044715 * v * v))
             return (v * half).astype(BF16), slope.astype(BF16)
 
-        def kernel(hi, ht, ui, ut, di, dt, act, slope, out, sum_i, sum_t):
+        def kernel(h, ui, ut, di, dt, act, slope, out, sum_i, sum_t):
             j = pl.program_id(0)
-            gi, si = gelu(nn(self.flat(hi), self.flat(ui)))
-            gt, st = gelu(nn(self.flat(ht), self.flat(ut)))
+            gi, si = gelu(nn(self.image(h), self.flat(ui)))
+            gt, st = gelu(nn(self.text(h), self.flat(ut)))
             self.put(act, gi, gt)
             self.put(slope, si, st)
             img, txt = nt(gi, self.flat(di)), nt(gt, self.flat(dt))
@@ -393,7 +425,7 @@
             kernel,
             "mlp",
             (steps,),
-            self.sides(h, D, lambda j: 0)
+            self.rows(h, D, lambda j: 0)
             + self.weight(ups, block, lambda j: 0, lambda j: j)
             + self.weight(downs, block, lambda j: 0, lambda j: j),
             [
@@ -411,10 +443,10 @@
         steps = 3
         block = self.hidden // steps
 
-        def kernel(hi, ht, si, st, ui, ut, di, dt, pre, out, sum_i, sum_t):
+        def kernel(h, s, ui, ut, di, dt, pre, out, sum_i, sum_t):
             j = pl.program_id(0)
-            pi = (nn(self.flat(hi), self.flat(di)) * self.flat(si).astype(F32)).astype(BF16)
-            pt = (nn(self.flat(ht), self.flat(dt)) * self.flat(st).astype(F32)).astype(BF16)
+            pi = (nn(self.image(h), self.flat(di)) * self.image(s).astype(F32)).astype(BF16)
+            pt = (nn(self.text(h), self.flat(dt)) * self.text(s).astype(F32)).astype(BF16)
             self.put(pre, pi, pt)
             img, txt = nt(pi, self.flat(ui)), nt(pt, self.flat(ut))
 
@@ -436,8 +468,8 @@
             kernel,
             "mlp_back",
             (steps,),
-            self.sides(grad, D, lambda j: 0)
-            + self.sides(slope, block, lambda j: j)
+            self.rows(grad, D, lambda j: 0)
+            + self.rows(slope, block, lambda j: j)
             + self.weight(ups, block, lambda j: 0, lambda j: j)
             + self.weight(downs, block, lambda j: 0, lambda j: j),
             [
@@ -453,7 +485,7 @@
         columns = right[0][0].shape[-1]
 
         def rows(refs, side):
-            got = [self.flat(refs[2 * c + side]) for c in range(self.n)]
+            got = [self.text(ref) if side else self.image(ref) for ref in refs]
             return got[0] if len(got) == 1 else jnp.concatenate(got, axis=0)
 
         if self.dr % 128:
@@ -470,14 +502,14 @@
         def kernel(*refs):
             ins, out = refs[:-1], refs[-1]
             for side in range(2):
-                a, b = rows(ins[: 2 * self.n], side), rows(ins[2 * self.n :], side)
+                a, b = rows(ins[: self.n], side), rows(ins[self.n :], side)
                 out[0, side] = tn(a, b).astype(BF16)
 
         ins = []
         for one in left:
-            ins += self.sides(one, self.dr, lambda j, g: g)
+            ins += self.rows(one, self.dr, lambda j, g: g)
         for one, lead in right:
-            ins += self.sides(one, columns, lambda j, g: 0, (lambda j, g=0, lead=lead: lead(j)) if lead else None)
+            ins += self.rows(one, columns, lambda j, g: 0, (lambda j, g=0, lead=lead: lead(j)) if lead else None)
         return call(
             kernel,
             name,
@@ -497,7 +529,7 @@
         )
 
     def norm_in(self, mods, x, blocks=None, gate=None, after_norm=None, after=()):
-        rows = self.ct
+        rows = self.ci // 4
 
         def kernel(*refs):
             refs = list(refs)
@@ -515,7 +547,7 @@
                 out = (normed * (1.0 + vectors[0, kind + 1 : kind + 2]) + vectors[0, kind : kind + 1]).astype(BF16)
                 refs[0][...] = jnp.broadcast_to(out[None], refs[0].shape)
 
-        ratio = self.ci // self.ct
+        ratio = 4
 
         def vectors(depth):
             return (mods, (1,) + mods.shape[1:], lambda i: (depth * 2 + i // ratio, 0, 0))
@@ -532,17 +564,21 @@
         return call(kernel, "norm_in", (ratio + 1,), ins, outs, flops=20 * self.rc * D, after=after)
 
     def norm_back(self, mods, grad, blocks=None, x=None, scale=None, branch=None, gate=None, after=()):
-        rows = self.ct
-        ratio = self.ci // self.ct
+        rows, ratio = self.ci // 4, 4
 
         def kernel(*refs):
             refs = list(refs)
-            value = refs.pop(0)[...]
             i = pl.program_id(0)
+            held = lax.broadcasted_iota(jnp.int32, (rows, 1), 0) < self.rc - i * rows
+
+            def take():
+                return jnp.where(held, refs.pop(0)[...], 0.0)
+
+            value = take()
             rows_of_sums = []
             if blocks is not None:
-                dh = jnp.sum(refs.pop(0)[...].astype(F32), axis=0)
-                normed, inverse = norm(refs.pop(0)[...])
+                dh = jnp.where(held, jnp.sum(refs.pop(0)[...].astype(F32), axis=0), 0.0)
+                normed, inverse = norm(take())
                 dn = dh * (1.0 + refs.pop(0)[0, scale[1] : scale[1] + 1])
                 value = value + inverse * (
                     dn
@@ -551,7 +587,7 @@
                 )
                 rows_of_sums += [(0, jnp.sum(dh, axis=0, keepdims=True)), (1, jnp.sum(dh * normed, axis=0, keepdims=True))]
             if branch is not None:
-                rows_of_sums.append((2, jnp.sum(value * refs.pop(0)[...], axis=0, keepdims=True)))
+                rows_of_sums.append((2, jnp.sum(value * take(), axis=0, keepdims=True)))
             if gate is not None:
                 factor = refs.pop(0)[0, gate[1] : gate[1] + 1]
             if blocks is not None:
@@ -591,6 +627,55 @@
         if blocks is not None or branch is not None:
             outs.append(((2, 8, D), F32, (1, 8, D), lambda i: (i // ratio, 0, 0)))
         return call(kernel, "norm_back", (ratio + 1,), ins, outs, flops=30 * self.rc * D, after=after)
+
+    def enter(self, plan, got, order, after=()):
+        rows, half = self.ci // 4, D // self.g // 2
+        wide = got.shape[-1]
+
+        def kernel(index, ref, out):
+            first = index[0:1, 0:1] == 0
+            for a in range(2):
+                for x in range(2):
+                    at = (a, x) if order[0] == 0 else (x, a)
+                    piece = jnp.where(first, ref[(0,) + at].astype(F32), ref[(1,) + at].astype(F32))
+                    for side in range(2):
+                        at = (a * 4 + side * 2 + x) * half
+                        out[:, at : at + half] = piece[:, side * half : (side + 1) * half]
+
+        return call(
+            kernel,
+            "enter",
+            (-(-self.rc // rows),),
+            [
+                (jnp.full((8, 128), plan.h, jnp.int32), (8, 128), lambda i: (0, 0)),
+                (got, (2, 2, 2, rows, wide), lambda i: (0, 0, 0, i, 0)),
+            ],
+            [((self.rc, D), F32, (rows, D), lambda i: (i, 0))],
+            flops=self.rc * D,
+            after=after,
+        )
+
+    def leave(self, own, after=()):
+        rows, half = self.ci // 4, D // self.g // 2
+        wide = D // self.q
+
+        def kernel(ref, out):
+            for a in range(2):
+                for x in range(2):
+                    at = [(a * 4 + side * 2 + x) * half for side in range(2)]
+                    piece = jnp.concatenate([ref[:, i : i + half] for i in at], axis=1).astype(BF16)
+                    for side in range(2):
+                        out[side, 2 * a + x] = piece
+
+        return call(
+            kernel,
+            "leave",
+            (-(-self.rc // rows),),
+            [(own, (rows, D), lambda i: (i, 0))],
+            [((2, self.q, self.rc, wide), BF16, (2, self.q, rows, wide), lambda i: (0, 0, i, 0))],
+            flops=self.rc * D,
+            after=after,
+        )
 
     def masks(self):
         at = lax.broadcasted_iota(jnp.int32, (self.n, self.q, self.rc), 2)
@@ -630,6 +715,7 @@
             flops=pairs * 8 * t * t * 128,
             transcendentals=pairs * 2 * t * t,
             after=after,
+            room=48,
         )
         return out.reshape(self.n, self.q, self.rc, self.wide)
 
@@ -674,6 +760,7 @@
             flops=pairs * 20 * t * t * 128,
             transcendentals=pairs * 2 * t * t,
             after=after,
+            room=56,
         )
         return out.reshape(3, self.n, self.q, self.rc, self.wide)
 
@@ -766,7 +853,7 @@
     plan = Plan(rows_count, cols, swap)
     width_rows = mod_image.shape[0]
     img_own = IMG_LEN // cols
-    txt_own = img_own // 4
+    txt_own = -(-TXT_LEN // (16 * cols)) * 16
     txt_pad = txt_own * cols
     wide = features + -features % 128
     k = Kernels(
@@ -779,6 +866,7 @@
         up_image.shape[2],
     )
     chunks = range(CHUNKS)
+    fast = k if swap and rows_count == 8 and cols == 4 and CHUNKS == 1 else None
 
     def filled(whole):
         return jnp.pad(whole, ((0, 0),) * 3 + ((0, wide - features),))
@@ -786,15 +874,31 @@
     qkv_shards = [split_columns(w, 3) for w in (qkv_image, qkv_text)]
     out_shards = [split_columns(w, 1) for w in (out_image, out_text)]
     w_attn, w_up, w_down = [], [], []
-    sides_attn = [
-        plan.swap_sides(
-            [qkv_shards[s][depth][kind] for kind in range(3) for s in range(2)]
-            + [out_shards[s][depth][0] for s in range(2)]
-        )
-        for depth in range(LAYERS)
-    ]
-    sides_up = [plan.swap_sides([up_image[depth], up_text[depth]]) for depth in range(LAYERS)]
-    sides_down = [plan.swap_sides([down_image[depth], down_text[depth]]) for depth in range(LAYERS)]
+    def sides_attn(depth, after=()):
+        pieces = [qkv_shards[s][depth][kind] for kind in range(3) for s in range(2)]
+        return plan.swap_sides(pieces + [out_shards[s][depth][0] for s in range(2)], after)
+
+    def sides_up(depth, after=()):
+        return plan.swap_sides([up_image[depth], up_text[depth]], after)
+
+    def sides_down(depth, after=()):
+        return plan.swap_sides([down_image[depth], down_text[depth]], after)
+
+    def to_blocks(image, text):
+        img = jnp.transpose(image.reshape(features, IMG_LEN)).reshape(cols, CHUNKS, k.ci, features)
+        txt = jnp.pad(jnp.transpose(text.reshape(features, TXT_LEN)), ((0, txt_pad - TXT_LEN), (0, 0)))
+        blocks = jnp.concatenate([img, txt.reshape(cols, CHUNKS, k.ct, features)], axis=2)
+        return blocks.reshape(cols, CHUNKS * k.rc, features)
+
+    def to_own(own):
+        own = own.astype(F32)
+        return [own[c * k.rc : (c + 1) * k.rc] for c in chunks]
+
+    def from_blocks(got):
+        got = got.reshape(cols, CHUNKS, k.rc, features)
+        img = got[:, :, : k.ci].reshape(IMG_LEN, features)
+        txt = got[:, :, k.ci :].reshape(txt_pad, features)[:TXT_LEN]
+        return jnp.transpose(img).reshape(1, -1), jnp.transpose(txt).reshape(1, -1)
 
     cond_float = condition.astype(F32)
     cond_low = jax.nn.silu(cond_float).astype(BF16)
@@ -802,38 +906,27 @@
     cond_mine = lax.all_to_all(cond_cut, "row", 0, 0, tiled=True)
     mod_part = [nn(cond_mine, one) for one in (mod_image, mod_text)]
     mod_sorted = jnp.concatenate([sort_vectors(one, 6) for one in mod_part], axis=1)
-    mod_cols = plan.vectors_in(mod_sorted.reshape(rows_count, -1)).reshape(cols, 2, LAYERS, 6, features)
+    blocks = to_blocks(image_in, text_in)
+    mod_row = plan.vectors_rows(mod_sorted.reshape(rows_count, -1))
+    mod_cols = plan.vectors_cols(mod_row).reshape(cols, 2, LAYERS, 6, features)
     mods = plan.inner(jnp.transpose(mod_cols, (2, 1, 3, 0, 4)).reshape(LAYERS * 2, 6, D))
 
-    def to_blocks(image, text):
-        img = jnp.transpose(image.reshape(features, IMG_LEN)).reshape(cols, CHUNKS, k.ci, features)
-        txt = jnp.pad(jnp.transpose(text.reshape(features, TXT_LEN)), ((0, txt_pad - TXT_LEN), (0, 0)))
-        blocks = jnp.concatenate([img, txt.reshape(cols, CHUNKS, k.ct, features)], axis=2)
-        return blocks.reshape(cols, CHUNKS * k.rc, features)
-
-    def to_own(pair):
-        own = plan.rows_in(pair).astype(F32)
-        return [own[c * k.rc : (c + 1) * k.rc] for c in chunks]
-
-    def from_blocks(got):
-        got = got.reshape(cols, CHUNKS, k.rc, features)
-        img = got[:, :, : k.ci].reshape(IMG_LEN, features)
-        txt = got[:, :, k.ci :].reshape(txt_pad, features)[:TXT_LEN]
-        return jnp.transpose(img).reshape(1, -1), jnp.transpose(txt).reshape(1, -1)
-
     mask = k.masks()
-    pair = plan.rows_home(to_blocks(image_in, text_in))
-    level = plan.swap_levels(sides_attn[0], [pair, mods, sides_up[0], sides_down[0]])
+    own = plan.rows_over(gate(blocks, [mods]), fast)
+    attn = sides_attn(0)
+    up = sides_up(0, [attn])
+    level = plan.swap_levels(attn, [own, up])
     w_qkv, w_out = [filled(plan.gather_weights(level[:6]))], [(filled(plan.gather_weights(level[6:])), 0)]
-    x = to_own(pair)
-    h1 = [plan.exchange(k.norm_in(mods, x[c], after_norm=(0, 0))) for c in chunks]
+    x = to_own(own)
+    sent = [k.norm_in(mods, x[c], after_norm=(0, 0)) for c in chunks]
+    h1 = [plan.exchange(one) for one in sent]
     kept = []
     for depth in range(LAYERS):
         last = depth + 1 == LAYERS
-        side = [plan.swap_levels(gate(sides_up[depth], h1 if depth else x), h1)]
+        if not depth:
+            down = sides_down(depth, sent)
+        side = [plan.swap_levels(gate(up, x), h1 + [down])]
         w_up.append(plan.gather_weights(side[0]))
-        if last:
-            side += grads
         joint = None
         for c in chunks:
             joint = k.qkv(h1[c], w_qkv[depth], c, joint, side)
@@ -847,22 +940,21 @@
         next_x, next_h1 = [], []
         sent = [k.project(heads, *w_out[depth], c, side) for c in chunks]
         blocks = [plan.exchange(one) for one in sent]
-        side = [plan.swap_levels(gate(sides_down[depth], sent), blocks)]
+        other = [] if last else [to_blocks(cot_image, cot_text), sides_attn(depth + 1, sent)]
+        side = [plan.swap_levels(gate(down, sent), blocks + other)]
         w_down.append(plan.gather_weights(side[0]))
-        if not last:
-            cot = to_blocks(gate(cot_image, sent), cot_text)
-            side.append(cot)
+        sent = []
         for c in chunks:
             x1, branch, h2 = k.norm_in(mods, x[c], blocks[c], (depth, 2), (depth, 3), side)
+            sent.append(h2)
             save["x1"].append(x1)
             save["branch"].append(branch)
             save["h2"].append(plan.exchange(h2))
         side = []
         if not last:
-            side = [plan.swap_levels(gate(sides_attn[depth + 1], save["x1"]), save["h2"])]
-            whole = filled(plan.gather_weights(side[0]))
-            w_qkv.append(whole)
-            w_out.append((whole, 6))
+            up = sides_up(depth + 1, sent)
+            pair = plan.rows_home(gate(other[0], sent))
+            side = [up, pair]
         parts = []
         for c in chunks:
             act, slope, part = k.mlp(save["h2"][c], w_up[depth], w_down[depth], side)
@@ -872,15 +964,20 @@
         kept.append(save)
         if last:
             break
-        blocks = [plan.exchange(part) for part in parts]
-        pair = plan.rows_home(gate(cot, parts))
-        side = [pair, sides_up[depth + 1], sides_down[depth + 1]]
+        grads = to_own(plan.rows_in(gate(pair, save["h2"] + [up]), fast, save["act"]))
+        blocks = [plan.exchange(gate(part, grads)) for part in parts]
+        down = sides_down(depth + 1, parts)
+        side = [plan.swap_levels(gate(other[1], parts), blocks + [down])]
+        whole = filled(plan.gather_weights(side[0]))
+        w_qkv.append(whole)
+        w_out.append((whole, 6))
+        sent = []
         for c in chunks:
             got = k.norm_in(mods, save["x1"][c], blocks[c], (depth, 5), (depth + 1, 0), side)
             next_x.append(got[0])
             save["down"].append(got[1])
+            sent.append(got[2])
             next_h1.append(plan.exchange(got[2]))
-        grads = to_own(pair)
         x, h1 = next_x, next_h1
 
     start = list(grads)
@@ -894,24 +991,29 @@
         if not first:
             up_grads[depth + 1] = plan.join_sides(up_sum)
             side = [up_grads[depth + 1]]
+        if not first:
+            image_cut, _ = plan.rows_home_again(gate(image_rows, grad_down), fast)
+            image_out, text_out = from_blocks(image_cut)
         down_whole = k.weight_grad("down_grad", grad_down, [(one, None) for one in save["act"]], 1, 2, 0, None, side)
         down_both = plan.scatter_weights(down_whole)
         for c in chunks:
             pre, part = k.mlp_back(grad_down[c], save["slope"][c], w_up[depth], w_down[depth], [down_whole])
             grad_pre.append(pre)
-            blocks.append(plan.exchange(part))
+            blocks.append(plan.exchange(part if first else gate(part, [image_cut])))
         up_whole = k.weight_grad("up_grad", save["h2"], [(one, None) for one in grad_pre], 1, 2, 0, None)
-        side = [up_whole]
+        side = []
         if not first:
-            attn_sum, _ = plan.sum_levels(attn_both)
+            attn_sum, _ = plan.sum_levels(jnp.concatenate([attn_both, last_out], axis=0))
             side.append(attn_sum)
+        up_whole = gate(up_whole, blocks + side)
+        side.append(up_whole)
         for c in chunks:
             grads[c], got, sums = k.norm_back(
                 mods, grads[c], blocks[c], save["x1"][c], (depth, 4), save["branch"][c], (depth, 2), side
             )
             sums2.append(sums)
             grad_out.append(plan.exchange(got))
-        up_both = plan.scatter_weights(gate(up_whole, sums2))
+        up_both = plan.scatter_weights(up_whole)
         down_sum, _ = plan.sum_levels(down_both)
         side = [down_sum]
         if not first:
@@ -920,36 +1022,40 @@
         grad_heads = None
         for c in chunks:
             grad_heads = k.project_back(grad_out[c], *w_out[depth], c, grad_heads, side)
-        grad_qkv = k.attend_back(save["joint"], mask, grad_heads)
+        rights = [(save["heads"], lambda kind, c=c: (c,)) for c in chunks]
+        out_whole = k.weight_grad("out_grad", grad_out, rights, 1, 2, 0, None, [grad_heads])
+        out_both = plan.scatter_weights(out_whole[..., :features])
+        grad_qkv = k.attend_back(save["joint"], mask, grad_heads, [out_whole])
         up_sum, _ = plan.sum_levels(up_both)
-        side = [up_sum]
         if first:
             last_blocks = [plan.exchange(gate(part, [grad_heads])) for part in parts]
-            side += last_blocks
+            down_grads[depth] = plan.join_sides(down_sum)
+            side = [up_sum, down_grads[depth]] + last_blocks
         else:
-            image_cut = plan.rows_out(gate(image_rows, [grad_heads]))
-            side += [image_cut]
+            down_grads[depth] = plan.join_sides(down_sum)
+            side = [up_sum, down_grads[depth]]
         rights = [(grad_qkv, lambda kind, c=c: (kind, c)) for c in chunks]
-        attn_whole = k.weight_grad("qkv_grad", save["h1"], rights, 3, 8, 0, None)
-        rights = [(save["heads"], lambda kind, c=c: (c,)) for c in chunks]
-        attn_whole = k.weight_grad("out_grad", grad_out, rights, 1, 8, 6, attn_whole)
+        attn_whole = k.weight_grad("qkv_grad", save["h1"], rights, 3, 6, 0, None, [] if first else side)
         if not depth:
             side.append(attn_whole)
         for c in chunks:
             blocks[c] = plan.exchange(k.qkv_back(grad_qkv, w_qkv[depth], c, side))
-        down_grads[depth] = plan.join_sides(down_sum)
-        side = [attn_whole, down_grads[depth]]
+        side = []
         if first:
             image_rows = []
             for c in chunks:
                 x2, down = k.norm_in(mods, save["x1"][c], last_blocks[c], (depth, 5))
-                image_rows.append(x2.astype(BF16))
+                image_rows.append(x2)
                 save["down"].append(down)
             image_rows = jnp.concatenate(image_rows, axis=0)
             side.append(image_rows)
+        if depth:
+            attn_whole = gate(attn_whole, blocks + side)
+            side.append(attn_whole)
         else:
-            image_out, text_out = from_blocks(plan.rows_back(image_cut))
-            side.append(image_out)
+            out_sum, _ = plan.sum_levels(out_both)
+            side.append(out_sum)
+        attn_both = plan.scatter_weights(attn_whole[..., :features])
         for c in chunks:
             if depth:
                 grads[c], got, sums = k.norm_back(
@@ -959,9 +1065,7 @@
             else:
                 grads[c], sums = k.norm_back(mods, grads[c], blocks[c], save["x"][c], (depth, 1), after=side)
             sums1.append(sums)
-        if depth:
-            attn_whole = gate(attn_whole, sums1)
-        attn_both = plan.scatter_weights(attn_whole[..., :features])
+        last_out = out_both
         if first:
             gate2 = []
             for c in chunks:
@@ -974,18 +1078,21 @@
         )
         gate2, grad_down = sums1, next_down
     up_grads[0] = plan.join_sides(up_sum)
-    attn_grads[0] = plan.join_sides(plan.sum_levels(attn_both)[0])
-    grad_image, grad_text = from_blocks(
-        plan.rows_back(plan.rows_out(jnp.concatenate([one.astype(BF16) for one in grads], axis=0)))
-    )
-
+    attn_sum, _ = plan.sum_levels(attn_both)
+    attn_grads[0] = plan.join_sides(jnp.concatenate([attn_sum, out_sum], axis=0))
     mod_part = plan.natural(jnp.stack(mod_grads)).reshape(LAYERS, 2, 6, cols, features)
     mod_part = jnp.transpose(mod_part, (3, 1, 0, 2, 4)).reshape(cols, -1)
-    mod_all = plan.vectors_out(mod_part).astype(BF16).reshape(rows_count, 2, LAYERS * 6, features)
+    mod_col = plan.vectors_cols_back(mod_part)
+    cut, _ = plan.rows_home_again(jnp.concatenate(grads, axis=0), fast, [mod_col])
+    grad_image, grad_text = from_blocks(cut)
+    mod_all = plan.vectors_rows_back(gate(mod_col, [cut, attn_sum])).astype(BF16)
+    mod_all = mod_all.reshape(rows_count, 2, LAYERS * 6, features)
     mod_cut = [unsort_vectors(mod_all[:, s], 6) for s in range(2)]
     grad_mod = [tn(cond_mine, cut) for cut in mod_cut]
     cond_part = nt(mod_cut[0], mod_image) + nt(mod_cut[1], mod_text)
-    cond_sum = lax.psum(lax.all_to_all(cond_part, "row", split_axis=0, concat_axis=0, tiled=True), "col")
+    cond_part = jnp.broadcast_to(cond_part[:, None], (rows_count, cols, width_rows)).reshape(-1, width_rows)
+    cond_sum = lax.all_to_all(cond_part, ("row", "col"), 0, 0, tiled=True)
+    cond_sum = jnp.sum(cond_sum.reshape(rows_count, cols, width_rows), axis=1)
     _, silu_pull = jax.vjp(jax.nn.silu, cond_float)
     grad_cond = silu_pull(cond_sum.reshape(1, D))[0]
 

time: 2120 us -> 1860 us (0.88)
  blocking collectives: 151 us -> 0 us
  waiting for transfers between devices: 914 us -> 835 us
    all_to_all x3 -> x0, blocking collectives: 128 us -> none  [exchange(): lax.all_to_all(blocks, ('row', 'col'), 0, 0, tiled=True, axis_index_group...]
    ppermute x6, waiting for transfers between devices: 132 us -> 37 us  [swap_levels(): lax.ppermute(both, 'col', self.levels)]
    ppermute x6, waiting for transfers between devices: 119 us -> 194 us  [swap_sides(): lax.ppermute(other, 'row', self.across)]
    ppermute x6, waiting for transfers between devices: 172 us -> 111 us  [join_sides(): lax.ppermute(other, 'row', self.across)]
    all_to_all x5 -> x8, waiting for transfers between devices: 10.4 us -> 43.1 us  [the longest x2 25.1 us: rows_home_again(): lax.all_to_all(cut, ('row', 'col'), 0, 0, tiled=True, axis_index_groups=s...]
    ppermute x6, starting transfers between devices: 39.3 us -> 11.4 us  [join_sides(): lax.ppermute(other, 'row', self.across)]
    unnamed x17 -> x18, other arithmetic: 19.2 us -> 43.3 us
    psum x1 -> x0, blocking collectives: 23.5 us -> none  [on_device(): lax.psum(lax.all_to_all(cond_part, 'row', split_axis=0, concat_axis=0, ti...]
  transfers between devices with their start and end apart: 64 -> 67, of which waited for: 28 -> 39; matrix products, arithmetic and copies ran while one was open for 15% -> 14% of each run, Pallas kernels for 19% -> 22%
where the time goes in v2:
time: 1860 us; the launch traced here: 1840 us
  waiting for transfers between devices  835 us (45%)
  Pallas kernels  468 us (25%)
  starting transfers between devices  185 us (10%)
  other arithmetic  163 us (9%)
  local copies, waits for them, and re-layouts  132 us (7%)
  matrix products  40.5 us (2%)
  between operations  20.9 us (1%)
    pallas_call x44, Pallas kernels, call(): pl.pallas_call(body, grid=grid, in_specs=in_specs + [pl.BlockSpec(memory_...  468 us
    all_to_all x17, waiting for transfers between devices, exchange(): lax.all_to_all(blocks, ('row', 'col'), 0, 0, tiled=True, axis_index_group...  253 us
    ppermute x6, waiting for transfers between devices, swap_sides(): lax.ppermute(other, 'row', self.across)  194 us
    ppermute x7, waiting for transfers between devices, sum_levels(): lax.ppermute(other, 'col', self.levels).astype(F32)  189 us
    ppermute x6, waiting for transfers between devices, join_sides(): lax.ppermute(other, 'row', self.across)  111 us
    all_to_all x17, starting transfers between devices, exchange(): lax.all_to_all(blocks, ('row', 'col'), 0, 0, tiled=True, axis_index_group...  88.1 us
    unnamed x18, other arithmetic  43.3 us
    dot_general x42, matrix products, dot(): lax.dot_general(a, b, (((ca,), (cb,)), ((), ())), preferred_element_type=...  40.5 us
  transfers between devices with their start and end apart: 67, of which 39 were waited for; matrix products, arithmetic and copies ran while one was open for 14% of the time, Pallas kernels for 22%

profile of v2, /device:TPU:0, one launch (start us, length us, event | category | flops | bytes accessed | tf_op | source)
XLA Modules:
  0.0 1844.3 jit_solution(15685656622345693354)
XLA Ops:
  107.8 27.2 %collective-permute-done = bf16[8,192,192]{2,1,0:T(8,128)(2,1)S(1)} collective-permute-done((bf16[8,192,192]{2,1,0:T(8,128)(2,1)S(1)}, bf16[8,192,192]{2,1,0:T(8,128)(2,1)S(1)}, u32[]{:S(2)}, u32[]{:S(2)}) %collective-permute-start) | collective-permute-done | bytes 589856 | tf_op jit(solution)/shard_map/ppermute | solution.py:94
  176.8 27.8 %collective-permute-done.2 = bf16[8,384,192]{1,2,0:T(8,128)(2,1)} collective-permute-done((bf16[8,384,192]{1,2,0:T(8,128)(2,1)}, bf16[8,384,192]{1,2,0:T(8,128)(2,1)}, u32[]{:S(2)}, u32[]{:S(2)}) %collective-permute-start.2) | collective-permute-done | bytes 1179680 | tf_op jit(solution)/shard_map/ppermute | solution.py:100
  239.3 43.8 %collective-permute-done.3 = bf16[2,192,768]{2,1,0:T(8,128)(2,1)S(1)} collective-permute-done((bf16[2,192,768]{2,1,0:T(8,128)(2,1)}, bf16[2,192,768]{2,1,0:T(8,128)(2,1)S(1)}, u32[]{:S(2)}, u32[]{:S(2)}) %collective-permute-start.3) | collective-permute-done | bytes 589856 | tf_op jit(solution)/shard_map/ppermute | solution.py:94
  384.4 21.0 %collective-permute-done.5 = bf16[8,192,192]{2,1,0:T(8,128)(2,1)} collective-permute-done((bf16[8,192,192]{2,1,0:T(8,128)(2,1)}, bf16[8,192,192]{2,1,0:T(8,128)(2,1)}, u32[]{:S(2)}, u32[]{:S(2)}) %collective-permute-start.5) | collective-permute-done | bytes 589856 | tf_op jit(solution)/shard_map/ppermute | solution.py:94
  437.2 48.8 %collective-permute-done.7 = bf16[2,192,768]{2,1,0:T(8,128)(2,1)} collective-permute-done((bf16[2,192,768]{2,1,0:T(8,128)(2,1)}, bf16[2,192,768]{2,1,0:T(8,128)(2,1)}, u32[]{:S(2)}, u32[]{:S(2)}) %collective-permute-start.7) | collective-permute-done | bytes 589856 | tf_op jit(solution)/shard_map/ppermute | solution.py:94
  498.9 23.0 %mlp.2 = (bf16[4,304,1536]{2,1,0:T(8,128)(2,1)}, bf16[4,304,1536]{2,1,0:T(8,128)(2,1)}, bf16[4,304,1536]{2,1,0:T(8,128)(2,1)}) custom-call(bf16[4,304,1536]{2,1,0:T(8,128)(2,1)} %all-to-all-done.6.refs_0_.refs_1_, bf16[4,2,384,1536]{3,2,1,0:T(8,128)(2,1)} %bitcast.342, bf16[4,2,384,1536]{3,2,1,0:T(8,128)(2,1)} %bitcast.343, ...), custom_call_target="tpu_custom_call" | custom-call | flops 1434451968 | bytes 6586368 | tf_op jit(solution)/shard_map/mlp/pallas_call | solution.py:226
  545.6 43.4 %collective-permute-done.9 = bf16[2,192,768]{2,1,0:T(8,128)(2,1)S(1)} collective-permute-done((bf16[2,192,768]{2,1,0:T(8,128)(2,1)}, bf16[2,192,768]{2,1,0:T(8,128)(2,1)S(1)}, u32[]{:S(2)}, u32[]{:S(2)}) %collective-permute-start.9) | collective-permute-done | bytes 589856 | tf_op jit(solution)/shard_map/ppermute | solution.py:94
  625.3 62.1 %all-to-all-done.9.refs_1_.refs_0_ = bf16[4,304,1536]{2,1,0:T(8,128)(2,1)} async-done(((bf16[4,304,1536]{2,1,0:T(8,128)(2,1)}), bf16[4,304,1536]{2,1,0:T(8,128)(2,1)}, u32[]{:S(2)}, u32[]{:S(2)}) %all-to-all-start.9) | async-done | bytes 3735584 | tf_op jit(solution)/shard_map/all_to_all | solution.py:65
  757.9 64.4 %all-to-all-done.11.refs_1_ = bf16[4,304,1536]{2,1,0:T(8,128)(2,1)} async-done(((bf16[4,304,1536]{2,1,0:T(8,128)(2,1)}), bf16[4,304,1536]{2,1,0:T(8,128)(2,1)}, u32[]{:S(2)}, u32[]{:S(2)}) %all-to-all-start.11) | async-done | bytes 3735584 | tf_op jit(solution)/shard_map/all_to_all | solution.py:65
  841.3 41.8 %all-to-all-done.12.refs_0_ = bf16[4,304,1536]{2,1,0:T(8,128)(2,1)} async-done(((bf16[4,304,1536]{2,1,0:T(8,128)(2,1)}), bf16[4,304,1536]{2,1,0:T(8,128)(2,1)}, u32[]{:S(2)}, u32[]{:S(2)}) %all-to-all-start.12) | async-done | bytes 3735584 | tf_op jit(solution)/shard_map/all_to_all | solution.py:65
  890.3 23.4 %mlp.3 = (bf16[4,304,1536]{2,1,0:T(8,128)(2,1)}, bf16[4,304,1536]{2,1,0:T(8,128)(2,1)}, bf16[4,304,1536]{2,1,0:T(8,128)(2,1)}) custom-call(bf16[4,304,1536]{2,1,0:T(8,128)(2,1)} %all-to-all-done.12.refs_0_, bf16[4,2,384,1536]{3,2,1,0:T(8,128)(2,1)} %bitcast.334, bf16[4,2,384,1536]{3,2,1,0:T(8,128)(2,1)} %bitcast.335, bf16[4,2,384,1536]{3,2,1,0:T(8,128)(2,1)} %bitcast.338, ...), custom_call_target="tpu_custom_call" | custom-call | flops 1434451968 | bytes 6586368 | tf_op jit(solution)/shard_map/mlp/pallas_call | solution.py:226
  924.6 21.8 %mlp_back.2 = (bf16[4,304,1536]{2,1,0:T(8,128)(2,1)}, bf16[4,304,1536]{2,1,0:T(8,128)(2,1)}) custom-call(bf16[4,304,1536]{2,1,0:T(8,128)(2,1)} %all-to-all-done.10.refs_3_.refs_0_, bf16[4,304,1536]{2,1,0:T(8,128)(2,1)} %get-tuple-element.56.refs_1_, bf16[4,2,384,1536]{3,2,1,0:T(8,128)(2,1)} %bitcast.336, bf16[4,2,384,1536]{3,2,1,0:T(8,128)(2,1)} %bitcast.337, ...), custom_call_target="tpu_custom_call" | custom-call | flops 1434451968 | bytes 6586368 | tf_op jit(solution)/shard_map/mlp_back/pallas_call | solution.py:226
  962.5 32.2 %all-to-all-done.13.refs_1_ = bf16[4,304,1536]{2,1,0:T(8,128)(2,1)} async-done(((bf16[4,304,1536]{2,1,0:T(8,128)(2,1)}), bf16[4,304,1536]{2,1,0:T(8,128)(2,1)}, u32[]{:S(2)}, u32[]{:S(2)}) %all-to-all-start.13) | async-done | bytes 3735584 | tf_op jit(solution)/shard_map/all_to_all | solution.py:65
  1012.9 61.1 %collective-permute-done.13 = bf16[2,384,768]{2,1,0:T(8,128)(2,1)S(1)} collective-permute-done((bf16[2,384,768]{2,1,0:T(8,128)(2,1)S(1)}, bf16[2,384,768]{2,1,0:T(8,128)(2,1)S(1)}, u32[]{:S(2)}, u32[]{:S(2)}) %collective-permute-start.13) | collective-permute-done | bytes 1179680 | tf_op jit(solution)/shard_map/ppermute | solution.py:116
  1101.2 42.9 %attend_back.2 = bf16[3,1216,384]{2,1,0:T(8,128)(2,1)} custom-call(bf16[1216,1152]{1,0:T(8,128)(2,1)} %bitcast.316, bf16[1216,1152]{1,0:T(8,128)(2,1)} %bitcast.317, bf16[1216,1152]{1,0:T(8,128)(2,1)} %bitcast.318, bf16[1216,1]{1,0:T(8,128)(2,1)} %copy-done.5, bf16[1216,384]{1,0:T(8,128)(2,1)} %bitcast.362, bf16[4,2,384,384]{3,2,1,0:T(8,128)(2,1)} %out_grad.2.refs_5_), custom_call_target="tpu_custom_call" | custom-call | flops 1419509760 | bytes 1517872 | tf_op jit(solution)/shard_map/attend_back/pallas_call | solution.py:226
  1195.5 19.6 %all-to-all-done.16.refs_1_ = bf16[4,304,1536]{2,1,0:T(8,128)(2,1)} async-done(((bf16[4,304,1536]{2,1,0:T(8,128)(2,1)}), bf16[4,304,1536]{2,1,0:T(8,128)(2,1)}, u32[]{:S(2)}, u32[]{:S(2)}) %all-to-all-start.16) | async-done | bytes 3735584 | tf_op jit(solution)/shard_map/all_to_all | solution.py:65
  1231.8 50.3 %collective-permute-done.16 = bf16[2,192,768]{2,1,0:T(8,128)(2,1)S(1)} collective-permute-done((bf16[2,192,768]{2,1,0:T(8,128)(2,1)S(1)}, bf16[2,192,768]{2,1,0:T(8,128)(2,1)S(1)}, u32[]{:S(2)}, u32[]{:S(2)}) %collective-permute-start.16) | collective-permute-done | bytes 589856 | tf_op jit(solution)/shard_map/ppermute | solution.py:123
  1305.0 23.4 %mlp_back.3 = (bf16[4,304,1536]{2,1,0:T(8,128)(2,1)}, bf16[4,304,1536]{2,1,0:T(8,128)(2,1)}) custom-call(bf16[4,304,1536]{2,1,0:T(8,128)(2,1)} %all-to-all-done.17.refs_1_.refs_0_, bf16[4,304,1536]{2,1,0:T(8,128)(2,1)} %get-tuple-element.67.refs_1_, bf16[4,2,384,1536]{3,2,1,0:T(8,128)(2,1)} %bitcast.344, bf16[4,2,384,1536]{3,2,1,0:T(8,128)(2,1)} %bitcast.345, ...), custom_call_target="tpu_custom_call" | custom-call | flops 1434451968 | bytes 6586368 | tf_op jit(solution)/shard_map/mlp_back/pallas_call | solution.py:226
  1328.4 19.7 %all-to-all-done.18 = bf16[8,304,384]{2,1,0:T(8,128)(2,1)} async-done(((bf16[8,304,384]{2,1,0:T(8,128)(2,1)}), bf16[8,304,384]{2,1,0:T(8,128)(2,1)}, u32[]{:S(2)}, u32[]{:S(2)}) %all-to-all-start.18) | async-done | bytes 1867808 | tf_op jit(solution)/shard_map/all_to_all | solution.py:154
  1370.9 47.7 %collective-permute-done.17 = bf16[8,384,192]{1,2,0:T(8,128)(2,1)} collective-permute-done((bf16[8,384,192]{1,2,0:T(8,128)(2,1)}, bf16[8,384,192]{1,2,0:T(8,128)(2,1)}, u32[]{:S(2)}, u32[]{:S(2)}) %collective-permute-start.17) | collective-permute-done | bytes 1179680 | tf_op jit(solution)/shard_map/ppermute | solution.py:116
  1446.9 52.1 %collective-permute-done.19 = bf16[8,192,192]{2,1,0:T(8,128)(2,1)S(1)} collective-permute-done((bf16[8,192,192]{2,1,0:T(8,128)(2,1)S(1)}, bf16[8,192,192]{2,1,0:T(8,128)(2,1)S(1)}, u32[]{:S(2)}, u32[]{:S(2)}) %collective-permute-start.19) | collective-permute-done | bytes 589856 | tf_op jit(solution)/shard_map/ppermute | solution.py:123
  1525.7 43.4 %attend_back.3 = bf16[3,1216,384]{2,1,0:T(8,128)(2,1)} custom-call(bf16[1216,1152]{1,0:T(8,128)(2,1)} %bitcast.310, bf16[1216,1152]{1,0:T(8,128)(2,1)} %bitcast.311, bf16[1216,1152]{1,0:T(8,128)(2,1)} %bitcast.312, bf16[1216,1]{1,0:T(8,128)(2,1)} %copy-done.5, bf16[1216,384]{1,0:T(8,128)(2,1)} %bitcast.373, bf16[4,2,384,384]{3,2,1,0:T(8,128)(2,1)} %out_grad.3.refs_5_), custom_call_target="tpu_custom_call" | custom-call | flops 1419509760 | bytes 1517872 | tf_op jit(solution)/shard_map/attend_back/pallas_call | solution.py:226
  1621.6 35.5 %collective-permute-done.22 = bf16[2,384,192]{2,1,0:T(8,128)(2,1)} collective-permute-done((bf16[2,384,192]{2,1,0:T(8,128)(2,1)}, bf16[2,384,192]{2,1,0:T(8,128)(2,1)}, u32[]{:S(2)}, u32[]{:S(2)}) %collective-permute-start.22) | collective-permute-done | bytes 294944 | tf_op jit(solution)/shard_map/ppermute | solution.py:116
  1740.7 30.9 %collective-permute-done.23 = bf16[6,384,192]{1,2,0:T(8,128)(2,1)} collective-permute-done((bf16[6,384,192]{1,2,0:T(8,128)(2,1)}, bf16[6,384,192]{1,2,0:T(8,128)(2,1)}, u32[]{:S(2)}, u32[]{:S(2)}) %collective-permute-start.23) | collective-permute-done | bytes 884768 | tf_op jit(solution)/shard_map/ppermute | solution.py:116
  (778 shorter events, 916.3 us)
Async XLA Ops:
  100.9 106.3 %all-to-all-start.3 = ((bf16[8,304,384]{2,1,0:T(8,128)(2,1)}), bf16[8,304,384]{2,1,0:T(8,128)(2,1)}, u32[]{:S(2)}, u32[]{:S(2)}) async-start(bf16[8,304,384]{2,1,0:T(8,128)(2,1)} %bitcast.382), calls=%async_computation.3 | async-start | bytes 3735552 | tf_op jit(solution)/shard_map/all_to_all | solution.py:146
  105.3 200.1 %all-gather.15.cloned.1.call-start = ((), (), s32[]{:S(2)}) async-start(), calls=%async_computation.42 | async-start | bytes 8847360 | tf_op jit(solution)/shard_map/all_gather | solution.py:105
  225.9 72.1 %all-to-all-start.4 = ((bf16[4,304,1536]{2,1,0:T(8,128)(2,1)}), bf16[4,304,1536]{2,1,0:T(8,128)(2,1)}, u32[]{:S(2)}, u32[]{:S(2)}) async-start(bf16[4,304,1536]{2,1,0:T(8,128)(2,1)} %norm_in.5.refs_1_), calls=%async_computation.4 | async-start | bytes 7471104 | tf_op jit(solution)/shard_map/all_to_all | solution.py:65
  230.9 105.3 %all-gather.17.cloned.1.call-start = ((), (), s32[]{:S(2)}) async-start(), calls=%async_computation.43 | async-start | bytes 2949120 | tf_op jit(solution)/shard_map/all_gather | solution.py:105
  233.0 265.8 %all-gather.19.cloned.1.call-start = ((), (), s32[]{:S(2)}) async-start(), calls=%async_computation.44 | async-start | bytes 11796480 | tf_op jit(solution)/shard_map/all_gather | solution.py:105
  342.1 71.8 %all-to-all-start.5 = ((bf16[4,304,1536]{2,1,0:T(8,128)(2,1)}), bf16[4,304,1536]{2,1,0:T(8,128)(2,1)}, u32[]{:S(2)}, u32[]{:S(2)}) async-start(bf16[4,304,1536]{2,1,0:T(8,128)(2,1)} %project.2.refs_1_), calls=%async_computation.5 | async-start | bytes 7471104 | tf_op jit(solution)/shard_map/all_to_all | solution.py:65
  347.0 151.9 %all-gather.21.cloned.1.call-start = ((), (), s32[]{:S(2)}) async-start(), calls=%async_computation.45 | async-start | bytes 11796480 | tf_op jit(solution)/shard_map/all_gather | solution.py:105
  530.8 71.7 %all-to-all-start.8 = ((bf16[4,304,1536]{2,1,0:T(8,128)(2,1)}), bf16[4,304,1536]{2,1,0:T(8,128)(2,1)}, u32[]{:S(2)}, u32[]{:S(2)}) async-start(bf16[4,304,1536]{2,1,0:T(8,128)(2,1)} %gate.30), calls=%async_computation.8 | async-start | bytes 7471104 | tf_op jit(solution)/shard_map/all_to_all | solution.py:65
  535.5 167.8 %all-gather.23.cloned.1.call-start = ((), (), s32[]{:S(2)}) async-start(), calls=%async_computation.46 | async-start | bytes 11796480 | tf_op jit(solution)/shard_map/all_gather | solution.py:105
  622.7 218.5 %all-gather.25.cloned.1.call-start = ((), (), s32[]{:S(2)}) async-start(), calls=%async_computation.47 | async-start | bytes 11796480 | tf_op jit(solution)/shard_map/all_gather | solution.py:105
  750.2 72.1 %all-to-all-start.11 = ((bf16[4,304,1536]{2,1,0:T(8,128)(2,1)}), bf16[4,304,1536]{2,1,0:T(8,128)(2,1)}, u32[]{:S(2)}, u32[]{:S(2)}) async-start(bf16[4,304,1536]{2,1,0:T(8,128)(2,1)} %project.3.refs_1_), calls=%async_computation.11 | async-start | bytes 7471104 | tf_op jit(solution)/shard_map/all_to_all | solution.py:65
  755.0 135.3 %all-gather.27.cloned.1.call-start = ((), (), s32[]{:S(2)}) async-start(), calls=%async_computation.48 | async-start | bytes 11796480 | tf_op jit(solution)/shard_map/all_gather | solution.py:105
  841.2 167.5 %reduce-scatter.9.cloned.1.call-start = ((), (), s32[]{:S(2)}) async-start(), calls=%async_computation.34 | async-start | bytes 11796480 | tf_op jit(solution)/shard_map/reduce_scatter | solution.py:109
  951.5 136.5 %reduce-scatter.11.cloned.1.call-start = ((), (), s32[]{:S(2)}) async-start(), calls=%async_computation.35 | async-start | bytes 11796480 | tf_op jit(solution)/shard_map/reduce_scatter | solution.py:109
  1003.9 72.4 %all-to-all-start.14 = ((bf16[4,304,1536]{2,1,0:T(8,128)(2,1)}), bf16[4,304,1536]{2,1,0:T(8,128)(2,1)}, u32[]{:S(2)}, u32[]{:S(2)}) async-start(bf16[4,304,1536]{2,1,0:T(8,128)(2,1)} %get-tuple-element.61), calls=%async_computation.14 | async-start | bytes 7471104 | tf_op jit(solution)/shard_map/all_to_all | solution.py:65
  1082.2 73.7 %all-to-all-start.15 = ((bf16[4,304,1536]{2,1,0:T(8,128)(2,1)}), bf16[4,304,1536]{2,1,0:T(8,128)(2,1)}, u32[]{:S(2)}, u32[]{:S(2)}) async-start(bf16[4,304,1536]{2,1,0:T(8,128)(2,1)} %gate.36), calls=%async_computation.16 | async-start | bytes 7471104 | tf_op jit(solution)/shard_map/all_to_all | solution.py:65
  1173.4 182.1 %reduce-scatter.15.cloned.1.call-start = ((), (), s32[]{:S(2)}) async-start(), calls=%async_computation.37 | async-start | bytes 2949120 | tf_op jit(solution)/shard_map/reduce_scatter | solution.py:109
  1173.9 181.6 %reduce-scatter.13.cloned.1.call-start = ((), (), s32[]{:S(2)}) async-start(), calls=%async_computation.36 | async-start | bytes 8847360 | tf_op jit(solution)/shard_map/reduce_scatter | solution.py:109
  1229.7 211.8 %reduce-scatter.17.cloned.1.call-start = ((), (), s32[]{:S(2)}) async-start(), calls=%async_computation.38 | async-start | bytes 11796480 | tf_op jit(solution)/shard_map/reduce_scatter | solution.py:109
  1350.7 74.2 %all-to-all-start.19 = ((bf16[4,304,1536]{2,1,0:T(8,128)(2,1)}), bf16[4,304,1536]{2,1,0:T(8,128)(2,1)}, u32[]{:S(2)}, u32[]{:S(2)}) async-start(bf16[4,304,1536]{2,1,0:T(8,128)(2,1)} %gate.39), calls=%async_computation.21 | async-start | bytes 7471104 | tf_op jit(solution)/shard_map/all_to_all | solution.py:65
  1355.4 165.3 %reduce-scatter.19.cloned.1.call-start = ((), (), s32[]{:S(2)}) async-start(), calls=%async_computation.39 | async-start | bytes 11796480 | tf_op jit(solution)/shard_map/reduce_scatter | solution.py:109
  1434.3 74.6 %all-to-all-start.20 = ((bf16[4,304,1536]{2,1,0:T(8,128)(2,1)}), bf16[4,304,1536]{2,1,0:T(8,128)(2,1)}, u32[]{:S(2)}, u32[]{:S(2)}) async-start(bf16[4,304,1536]{2,1,0:T(8,128)(2,1)} %get-tuple-element.72), calls=%async_computation.24 | async-start | bytes 7471104 | tf_op jit(solution)/shard_map/all_to_all | solution.py:65
  1441.4 168.6 %reduce-scatter.21.cloned.1.call-start = ((), (), s32[]{:S(2)}) async-start(), calls=%async_computation.40 | async-start | bytes 2949120 | tf_op jit(solution)/shard_map/reduce_scatter | solution.py:109
  1520.6 197.0 %reduce-scatter.23.cloned.1.call-start = ((), (), s32[]{:S(2)}) async-start(), calls=%async_computation.41 | async-start | bytes 8847360 | tf_op jit(solution)/shard_map/reduce_scatter | solution.py:109
  (183 other events, 3305.1 us)
Sparse Core Ops, SparseCore 0:
  220.8 50.2 all-gather.14
  273.2 24.0 all-gather.16
  304.4 62.1 all-gather.18
  420.2 61.4 all-gather.20
  609.7 64.3 all-gather.22
  693.7 64.2 all-gather.24
  828.5 61.6 all-gather.26
  924.8 78.4 reduce-scatter.8
  1005.8 78.3 reduce-scatter.10
  1177.0 33.0 reduce-scatter.14
  1215.2 61.3 reduce-scatter.12
  1295.3 77.8 reduce-scatter.16
  1425.1 79.5 reduce-scatter.18
  1520.8 31.5 reduce-scatter.20
  1591.2 61.4 reduce-scatter.22

commit v3 on v2

--- a/solution.py
+++ b/solution.py
@@ -131,31 +131,44 @@
     def rows_in(self, pair, kernels, after=()):
         got = self.exchange(pair)
         if self.swap and kernels is not None:
-            return kernels.enter(self, got.reshape((2, 2) + got.shape[1:]), (1, 0), after)
-        if not self.swap:
-            return jnp.transpose(got, (1, 0, 2)).reshape(got.shape[1], D)
+            return got, kernels.enter(self, got.reshape((2, 2) + got.shape[1:]), (1, 0), after)
+        if not self.swap:
+            return got, jnp.transpose(got, (1, 0, 2)).reshape(got.shape[1], D)
         got = got.reshape((2, self.cols // 2) + got.shape[1:])
         got = jnp.where(self.h == 0, got[0], got[1])
-        return self.inner(jnp.transpose(got, (2, 1, 0, 3)).reshape(got.shape[2], D))
+        return got, self.inner(jnp.transpose(got, (2, 1, 0, 3)).reshape(got.shape[2], D))
 
     def rows_over(self, blocks, kernels):
         if not self.swap or kernels is None:
-            return self.rows_in(self.rows_home(blocks), kernels)
+            return self.rows_in(self.rows_home(blocks), kernels)[1]
         cut = blocks.reshape((2, 1, self.cols // 2) + blocks.shape[1:])
         cut = jnp.broadcast_to(cut, (2, 2) + cut.shape[2:]).reshape((2 * self.cols,) + blocks.shape[1:])
         got = lax.all_to_all(cut, ("row", "col"), 0, 0, tiled=True, axis_index_groups=self.plane)
         return kernels.enter(self, got.reshape((2, 2, self.cols // 2) + blocks.shape[1:]), (0, 1))
 
-    def rows_home_again(self, own, kernels, first=(), second=()):
+    def rows_home_again(self, own, kernels, extra=None, second=()):
         if not self.swap or kernels is None:
-            return self.rows_back(self.rows_out(own, kernels)), own
-        cut = kernels.leave(own, first)
+            return self.rows_back(self.rows_out(own, kernels))
+        cut = kernels.leave(own)
+        tokens = cut.shape[2]
+        if extra is not None:
+            more = jnp.broadcast_to(extra.astype(BF16)[None], (2,) + extra.shape)
+            cut = jnp.concatenate([cut, more], axis=2)
         cut = cut.reshape((2 * self.cols,) + cut.shape[2:])
         got = lax.all_to_all(cut, ("row", "col"), 0, 0, tiled=True, axis_index_groups=self.plane)
         got = got.reshape((2, 2, self.cols // 2) + got.shape[1:])
         x = tick(self.x, second) if len(second) else self.x
-        got = jnp.where(x == 0, got[:, 0], got[:, 1])
-        return got.reshape((self.cols,) + got.shape[2:]), cut
+        rows = jnp.where(x == 0, got[:, 0, :, :tokens], got[:, 1, :, :tokens])
+        rows = rows.reshape((self.cols,) + rows.shape[2:])
+        if extra is None:
+            return rows
+        return rows, jnp.sum(got[:, :, :, tokens:].astype(F32), axis=(0, 2))
+
+    def vectors_near(self, mine):
+        every = jnp.broadcast_to(mine[None], (self.rows // 2,) + mine.shape)
+        every = lax.all_to_all(every, "row", 0, 0, tiled=True, axis_index_groups=self.fetch)
+        every = every.reshape((self.rows // 4, 2) + mine.shape)
+        return jnp.swapaxes(every, 1, 2).reshape(self.rows, -1)
 
     def rows_out(self, own, kernels):
         tokens, own = own.shape[0], own.astype(BF16)
@@ -743,9 +756,9 @@
                 grad_scores = (chances * (grad_chances - centre)).astype(BF16)
                 one_v = nn(chances.astype(BF16), grad_o)
                 one_k = nn(grad_scores, jnp.where(mine, scaled, none))
-                one_q = tn(grad_scores, jnp.where(mine, k * scale, none))
+                one_q = tn(jnp.where(mine, k * scale, none), grad_scores)
                 dq, dk, dv = (one_q, one_k, one_v) if dq is None else (dq + one_q, dk + one_k, dv + one_v)
-            out_ref[0] = dq.astype(BF16)
+            out_ref[0] = jnp.transpose(dq).astype(BF16)
             out_ref[1] = dk.astype(BF16)
             out_ref[2] = dv.astype(BF16)
 
@@ -964,10 +977,11 @@
         kept.append(save)
         if last:
             break
-        grads = to_own(plan.rows_in(gate(pair, save["h2"] + [up]), fast, save["act"]))
-        blocks = [plan.exchange(gate(part, grads)) for part in parts]
-        down = sides_down(depth + 1, parts)
-        side = [plan.swap_levels(gate(other[1], parts), blocks + [down])]
+        got, grads = plan.rows_in(gate(pair, save["h2"] + [up]), fast, save["act"])
+        grads = to_own(grads)
+        blocks = [plan.exchange(gate(part, [got])) for part in parts]
+        down = sides_down(depth + 1, save["act"])
+        side = [plan.swap_levels(gate(other[1], save["act"]), blocks + [down, *grads])]
         whole = filled(plan.gather_weights(side[0]))
         w_qkv.append(whole)
         w_out.append((whole, 6))
@@ -992,7 +1006,7 @@
             up_grads[depth + 1] = plan.join_sides(up_sum)
             side = [up_grads[depth + 1]]
         if not first:
-            image_cut, _ = plan.rows_home_again(gate(image_rows, grad_down), fast)
+            image_cut = plan.rows_home_again(gate(image_rows, grad_down), fast)
             image_out, text_out = from_blocks(image_cut)
         down_whole = k.weight_grad("down_grad", grad_down, [(one, None) for one in save["act"]], 1, 2, 0, None, side)
         down_both = plan.scatter_weights(down_whole)
@@ -1022,10 +1036,13 @@
         grad_heads = None
         for c in chunks:
             grad_heads = k.project_back(grad_out[c], *w_out[depth], c, grad_heads, side)
-        rights = [(save["heads"], lambda kind, c=c: (c,)) for c in chunks]
-        out_whole = k.weight_grad("out_grad", grad_out, rights, 1, 2, 0, None, [grad_heads])
-        out_both = plan.scatter_weights(out_whole[..., :features])
-        grad_qkv = k.attend_back(save["joint"], mask, grad_heads, [out_whole])
+        side = []
+        if not depth:
+            rights = [(save["heads"], lambda kind, c=c: (c,)) for c in chunks]
+            out_whole = k.weight_grad("out_grad", grad_out, rights, 1, 2, 0, None, [grad_heads])
+            out_both = plan.scatter_weights(out_whole[..., :features])
+            side = [out_whole]
+        grad_qkv = k.attend_back(save["joint"], mask, grad_heads, side)
         up_sum, _ = plan.sum_levels(up_both)
         if first:
             last_blocks = [plan.exchange(gate(part, [grad_heads])) for part in parts]
@@ -1050,8 +1067,11 @@
             image_rows = jnp.concatenate(image_rows, axis=0)
             side.append(image_rows)
         if depth:
-            attn_whole = gate(attn_whole, blocks + side)
+            rights = [(save["heads"], lambda kind, c=c: (c,)) for c in chunks]
+            out_whole = k.weight_grad("out_grad", grad_out, rights, 1, 2, 0, None)
+            attn_whole = gate(attn_whole, blocks + side + [out_whole])
             side.append(attn_whole)
+            out_both = plan.scatter_weights(gate(out_whole, [attn_whole])[..., :features])
         else:
             out_sum, _ = plan.sum_levels(out_both)
             side.append(out_sum)
@@ -1082,10 +1102,14 @@
     attn_grads[0] = plan.join_sides(jnp.concatenate([attn_sum, out_sum], axis=0))
     mod_part = plan.natural(jnp.stack(mod_grads)).reshape(LAYERS, 2, 6, cols, features)
     mod_part = jnp.transpose(mod_part, (3, 1, 0, 2, 4)).reshape(cols, -1)
-    mod_col = plan.vectors_cols_back(mod_part)
-    cut, _ = plan.rows_home_again(jnp.concatenate(grads, axis=0), fast, [mod_col])
+    grads = jnp.concatenate(grads, axis=0)
+    if fast is None:
+        mod_all = plan.vectors_rows_back(plan.vectors_cols_back(mod_part)).astype(BF16)
+        cut = plan.rows_home_again(grads, fast)
+    else:
+        cut, more = plan.rows_home_again(grads, fast, mod_part.reshape(cols, -1, features))
+        mod_all = plan.vectors_near(gate(more.reshape(2, -1).astype(BF16), [attn_sum]))
     grad_image, grad_text = from_blocks(cut)
-    mod_all = plan.vectors_rows_back(gate(mod_col, [cut, attn_sum])).astype(BF16)
     mod_all = mod_all.reshape(rows_count, 2, LAYERS * 6, features)
     mod_cut = [unsort_vectors(mod_all[:, s], 6) for s in range(2)]
     grad_mod = [tn(cond_mine, cut) for cut in mod_cut]

time: 1860 us -> 1840 us (0.989)
  waiting for transfers between devices: 835 us -> 854 us
  transfers between devices with their start and end apart: 67 -> 66, of which waited for: 39 -> 39; matrix products, arithmetic and copies ran while one was open for 14% -> 14% of each run, Pallas kernels for 22% -> 22%
where the time goes in v3:
time: 1840 us; the launch traced here: 1820 us
  waiting for transfers between devices  854 us (46%)
  Pallas kernels  452 us (25%)
  starting transfers between devices  176 us (10%)
  other arithmetic  161 us (9%)
  local copies, waits for them, and re-layouts  120 us (7%)
  matrix products  40.3 us (2%)
  between operations  21 us (1%)
    pallas_call x44, Pallas kernels, call(): pl.pallas_call(body, grid=grid, in_specs=in_specs + [pl.BlockSpec(memory_...  452 us
    all_to_all x17, waiting for transfers between devices, exchange(): lax.all_to_all(blocks, ('row', 'col'), 0, 0, tiled=True, axis_index_group...  255 us
    ppermute x7, waiting for transfers between devices, sum_levels(): lax.ppermute(other, 'col', self.levels).astype(F32)  191 us
    ppermute x6, waiting for transfers between devices, swap_sides(): lax.ppermute(other, 'row', self.across)  189 us
    ppermute x6, waiting for transfers between devices, join_sides(): lax.ppermute(other, 'row', self.across)  126 us
    all_to_all x17, starting transfers between devices, exchange(): lax.all_to_all(blocks, ('row', 'col'), 0, 0, tiled=True, axis_index_group...  87.8 us
    unnamed x18, other arithmetic  43.3 us
    dot_general x42, matrix products, dot(): lax.dot_general(a, b, (((ca,), (cb,)), ((), ())), preferred_element_type=...  40.3 us
  transfers between devices with their start and end apart: 66, of which 39 were waited for; matrix products, arithmetic and copies ran while one was open for 14% of the time, Pallas kernels for 22%

profile of v3, /device:TPU:0, one launch (start us, length us, event | category | flops | bytes accessed | tf_op | source)
XLA Modules:
  0.0 1823.4 jit_solution(8299431743593590484)
XLA Ops:
  107.9 27.2 %collective-permute-done = bf16[8,192,192]{2,1,0:T(8,128)(2,1)S(1)} collective-permute-done((bf16[8,192,192]{2,1,0:T(8,128)(2,1)S(1)}, bf16[8,192,192]{2,1,0:T(8,128)(2,1)S(1)}, u32[]{:S(2)}, u32[]{:S(2)}) %collective-permute-start) | collective-permute-done | bytes 589856 | tf_op jit(solution)/shard_map/ppermute | solution.py:94
  176.8 27.8 %collective-permute-done.2 = bf16[8,384,192]{1,2,0:T(8,128)(2,1)} collective-permute-done((bf16[8,384,192]{1,2,0:T(8,128)(2,1)}, bf16[8,384,192]{1,2,0:T(8,128)(2,1)}, u32[]{:S(2)}, u32[]{:S(2)}) %collective-permute-start.2) | collective-permute-done | bytes 1179680 | tf_op jit(solution)/shard_map/ppermute | solution.py:100
  239.3 43.8 %collective-permute-done.3 = bf16[2,192,768]{2,1,0:T(8,128)(2,1)S(1)} collective-permute-done((bf16[2,192,768]{2,1,0:T(8,128)(2,1)}, bf16[2,192,768]{2,1,0:T(8,128)(2,1)S(1)}, u32[]{:S(2)}, u32[]{:S(2)}) %collective-permute-start.3) | collective-permute-done | bytes 589856 | tf_op jit(solution)/shard_map/ppermute | solution.py:94
  359.3 18.4 %reduce.5 = bf16[393216]{0:T(1024)(128)(2,1)} reduce(bf16[1,393216]{1,0:T(2,128)(2,1)} %param.28, bf16[]{:T(256)} %constant.195), dimensions={0}, to_apply=%param.28.reduce_sub_computation | reduce | bytes 1572866 | tf_op args[13]
  384.3 21.0 %collective-permute-done.5 = bf16[8,192,192]{2,1,0:T(8,128)(2,1)} collective-permute-done((bf16[8,192,192]{2,1,0:T(8,128)(2,1)}, bf16[8,192,192]{2,1,0:T(8,128)(2,1)}, u32[]{:S(2)}, u32[]{:S(2)}) %collective-permute-start.5) | collective-permute-done | bytes 589856 | tf_op jit(solution)/shard_map/ppermute | solution.py:94
  437.1 48.9 %collective-permute-done.7 = bf16[2,192,768]{2,1,0:T(8,128)(2,1)} collective-permute-done((bf16[2,192,768]{2,1,0:T(8,128)(2,1)}, bf16[2,192,768]{2,1,0:T(8,128)(2,1)}, u32[]{:S(2)}, u32[]{:S(2)}) %collective-permute-start.7) | collective-permute-done | bytes 589856 | tf_op jit(solution)/shard_map/ppermute | solution.py:94
  498.8 23.0 %mlp.2 = (bf16[4,304,1536]{2,1,0:T(8,128)(2,1)}, bf16[4,304,1536]{2,1,0:T(8,128)(2,1)}, bf16[4,304,1536]{2,1,0:T(8,128)(2,1)}) custom-call(bf16[4,304,1536]{2,1,0:T(8,128)(2,1)} %all-to-all-done.6.refs_0_.refs_1_, bf16[4,2,384,1536]{3,2,1,0:T(8,128)(2,1)} %bitcast.343, bf16[4,2,384,1536]{3,2,1,0:T(8,128)(2,1)} %bitcast.344, ...), custom_call_target="tpu_custom_call" | custom-call | flops 1434451968 | bytes 6586368 | tf_op jit(solution)/shard_map/mlp/pallas_call | solution.py:239
  541.4 38.8 %collective-permute-done.9 = bf16[2,192,768]{2,1,0:T(8,128)(2,1)S(1)} collective-permute-done((bf16[2,192,768]{2,1,0:T(8,128)(2,1)}, bf16[2,192,768]{2,1,0:T(8,128)(2,1)S(1)}, u32[]{:S(2)}, u32[]{:S(2)}) %collective-permute-start.9) | collective-permute-done | bytes 589856 | tf_op jit(solution)/shard_map/ppermute | solution.py:94
  616.3 63.7 %all-to-all-done.9.refs_1_.refs_0_ = bf16[4,304,1536]{2,1,0:T(8,128)(2,1)} async-done(((bf16[4,304,1536]{2,1,0:T(8,128)(2,1)}), bf16[4,304,1536]{2,1,0:T(8,128)(2,1)}, u32[]{:S(2)}, u32[]{:S(2)}) %all-to-all-start.9) | async-done | bytes 3735584 | tf_op jit(solution)/shard_map/all_to_all | solution.py:65
  749.3 67.1 %all-to-all-done.11.refs_1_ = bf16[4,304,1536]{2,1,0:T(8,128)(2,1)} async-done(((bf16[4,304,1536]{2,1,0:T(8,128)(2,1)}), bf16[4,304,1536]{2,1,0:T(8,128)(2,1)}, u32[]{:S(2)}, u32[]{:S(2)}) %all-to-all-start.11) | async-done | bytes 3735584 | tf_op jit(solution)/shard_map/all_to_all | solution.py:65
  835.5 41.8 %all-to-all-done.12.refs_0_ = bf16[4,304,1536]{2,1,0:T(8,128)(2,1)} async-done(((bf16[4,304,1536]{2,1,0:T(8,128)(2,1)}), bf16[4,304,1536]{2,1,0:T(8,128)(2,1)}, u32[]{:S(2)}, u32[]{:S(2)}) %all-to-all-start.12) | async-done | bytes 3735584 | tf_op jit(solution)/shard_map/all_to_all | solution.py:65
  884.3 23.5 %mlp.3 = (bf16[4,304,1536]{2,1,0:T(8,128)(2,1)}, bf16[4,304,1536]{2,1,0:T(8,128)(2,1)}, bf16[4,304,1536]{2,1,0:T(8,128)(2,1)}) custom-call(bf16[4,304,1536]{2,1,0:T(8,128)(2,1)} %all-to-all-done.12.refs_0_, bf16[4,2,384,1536]{3,2,1,0:T(8,128)(2,1)} %bitcast.335, bf16[4,2,384,1536]{3,2,1,0:T(8,128)(2,1)} %bitcast.336, bf16[4,2,384,1536]{3,2,1,0:T(8,128)(2,1)} %bitcast.339, ...), custom_call_target="tpu_custom_call" | custom-call | flops 1434451968 | bytes 6586368 | tf_op jit(solution)/shard_map/mlp/pallas_call | solution.py:239
  918.7 21.8 %mlp_back.2 = (bf16[4,304,1536]{2,1,0:T(8,128)(2,1)}, bf16[4,304,1536]{2,1,0:T(8,128)(2,1)}) custom-call(bf16[4,304,1536]{2,1,0:T(8,128)(2,1)} %all-to-all-done.10.refs_3_.refs_0_, bf16[4,304,1536]{2,1,0:T(8,128)(2,1)} %get-tuple-element.56.refs_1_, bf16[4,2,384,1536]{3,2,1,0:T(8,128)(2,1)} %bitcast.337, bf16[4,2,384,1536]{3,2,1,0:T(8,128)(2,1)} %bitcast.338, ...), custom_call_target="tpu_custom_call" | custom-call | flops 1434451968 | bytes 6586368 | tf_op jit(solution)/shard_map/mlp_back/pallas_call | solution.py:239
  956.6 32.1 %all-to-all-done.13.refs_1_ = bf16[4,304,1536]{2,1,0:T(8,128)(2,1)} async-done(((bf16[4,304,1536]{2,1,0:T(8,128)(2,1)}), bf16[4,304,1536]{2,1,0:T(8,128)(2,1)}, u32[]{:S(2)}, u32[]{:S(2)}) %all-to-all-start.13) | async-done | bytes 3735584 | tf_op jit(solution)/shard_map/all_to_all | solution.py:65
  1006.9 61.1 %collective-permute-done.13 = bf16[2,384,768]{2,1,0:T(8,128)(2,1)S(1)} collective-permute-done((bf16[2,384,768]{2,1,0:T(8,128)(2,1)S(1)}, bf16[2,384,768]{2,1,0:T(8,128)(2,1)S(1)}, u32[]{:S(2)}, u32[]{:S(2)}) %collective-permute-start.13) | collective-permute-done | bytes 1179680 | tf_op jit(solution)/shard_map/ppermute | solution.py:116
  1087.7 36.3 %attend_back.2 = bf16[3,1216,384]{2,1,0:T(8,128)(2,1)} custom-call(bf16[1216,1152]{1,0:T(8,128)(2,1)} %bitcast.317, bf16[1216,1152]{1,0:T(8,128)(2,1)} %bitcast.318, bf16[1216,1152]{1,0:T(8,128)(2,1)} %bitcast.319, bf16[1216,1]{1,0:T(8,128)(2,1)} %copy-done.5, bf16[1216,384]{1,0:T(8,128)(2,1)} %bitcast.374), custom_call_target="tpu_custom_call" | custom-call | flops 1419509760 | bytes 1517872 | tf_op jit(solution)/shard_map/attend_back/pallas_call | solution.py:239
  1224.8 52.8 %collective-permute-done.16 = bf16[2,192,768]{2,1,0:T(8,128)(2,1)S(1)} collective-permute-done((bf16[2,192,768]{2,1,0:T(8,128)(2,1)S(1)}, bf16[2,192,768]{2,1,0:T(8,128)(2,1)S(1)}, u32[]{:S(2)}, u32[]{:S(2)}) %collective-permute-start.16) | collective-permute-done | bytes 589856 | tf_op jit(solution)/shard_map/ppermute | solution.py:123
  1300.0 22.0 %mlp_back.3 = (bf16[4,304,1536]{2,1,0:T(8,128)(2,1)}, bf16[4,304,1536]{2,1,0:T(8,128)(2,1)}) custom-call(bf16[4,304,1536]{2,1,0:T(8,128)(2,1)} %all-to-all-done.17.refs_1_.refs_0_, bf16[4,304,1536]{2,1,0:T(8,128)(2,1)} %get-tuple-element.67.refs_1_, bf16[4,2,384,1536]{3,2,1,0:T(8,128)(2,1)} %bitcast.345, bf16[4,2,384,1536]{3,2,1,0:T(8,128)(2,1)} %bitcast.346, ...), custom_call_target="tpu_custom_call" | custom-call | flops 1434451968 | bytes 6586368 | tf_op jit(solution)/shard_map/mlp_back/pallas_call | solution.py:239
  1322.1 21.8 %all-to-all-done.18 = bf16[8,304,384]{2,1,0:T(8,128)(2,1)} async-done(((bf16[8,304,384]{2,1,0:T(8,128)(2,1)}), bf16[8,304,384]{2,1,0:T(8,128)(2,1)}, u32[]{:S(2)}, u32[]{:S(2)}) %all-to-all-start.18) | async-done | bytes 1867808 | tf_op jit(solution)/shard_map/all_to_all | solution.py:158
  1366.7 48.7 %collective-permute-done.17 = bf16[8,384,192]{1,2,0:T(8,128)(2,1)} collective-permute-done((bf16[8,384,192]{1,2,0:T(8,128)(2,1)}, bf16[8,384,192]{1,2,0:T(8,128)(2,1)}, u32[]{:S(2)}, u32[]{:S(2)}) %collective-permute-start.17) | collective-permute-done | bytes 1179680 | tf_op jit(solution)/shard_map/ppermute | solution.py:116
  1443.1 51.7 %collective-permute-done.19 = bf16[8,192,192]{2,1,0:T(8,128)(2,1)S(1)} collective-permute-done((bf16[8,192,192]{2,1,0:T(8,128)(2,1)S(1)}, bf16[8,192,192]{2,1,0:T(8,128)(2,1)S(1)}, u32[]{:S(2)}, u32[]{:S(2)}) %collective-permute-start.19) | collective-permute-done | bytes 589856 | tf_op jit(solution)/shard_map/ppermute | solution.py:123
  1521.6 36.7 %attend_back.3 = bf16[3,1216,384]{2,1,0:T(8,128)(2,1)} custom-call(bf16[1216,1152]{1,0:T(8,128)(2,1)} %bitcast.311, bf16[1216,1152]{1,0:T(8,128)(2,1)} %bitcast.312, bf16[1216,1152]{1,0:T(8,128)(2,1)} %bitcast.313, bf16[1216,1]{1,0:T(8,128)(2,1)} %copy-done.5, bf16[1216,384]{1,0:T(8,128)(2,1)} %bitcast.373, bf16[4,2,384,384]{3,2,1,0:T(8,128)(2,1)} %out_grad.3.refs_5_), custom_call_target="tpu_custom_call" | custom-call | flops 1419509760 | bytes 1517872 | tf_op jit(solution)/shard_map/attend_back/pallas_call | solution.py:239
  1617.1 36.1 %collective-permute-done.22 = bf16[2,384,192]{2,1,0:T(8,128)(2,1)} collective-permute-done((bf16[2,384,192]{2,1,0:T(8,128)(2,1)}, bf16[2,384,192]{2,1,0:T(8,128)(2,1)}, u32[]{:S(2)}, u32[]{:S(2)}) %collective-permute-start.22) | collective-permute-done | bytes 294944 | tf_op jit(solution)/shard_map/ppermute | solution.py:116
  1738.9 22.2 %collective-permute-done.23 = bf16[6,384,192]{1,2,0:T(8,128)(2,1)} collective-permute-done((bf16[6,384,192]{1,2,0:T(8,128)(2,1)}, bf16[6,384,192]{1,2,0:T(8,128)(2,1)}, u32[]{:S(2)}, u32[]{:S(2)}) %collective-permute-start.23) | collective-permute-done | bytes 884768 | tf_op jit(solution)/shard_map/ppermute | solution.py:116
  (780 shorter events, 914.1 us)
Async XLA Ops:
  100.9 106.2 %all-to-all-start.3 = ((bf16[8,304,384]{2,1,0:T(8,128)(2,1)}), bf16[8,304,384]{2,1,0:T(8,128)(2,1)}, u32[]{:S(2)}, u32[]{:S(2)}) async-start(bf16[8,304,384]{2,1,0:T(8,128)(2,1)} %bitcast.381), calls=%async_computation.3 | async-start | bytes 3735552 | tf_op jit(solution)/shard_map/all_to_all | solution.py:146
  105.4 200.0 %all-gather.15.cloned.1.call-start = ((), (), s32[]{:S(2)}) async-start(), calls=%async_computation.41 | async-start | bytes 8847360 | tf_op jit(solution)/shard_map/all_gather | solution.py:105
  225.9 72.2 %all-to-all-start.4 = ((bf16[4,304,1536]{2,1,0:T(8,128)(2,1)}), bf16[4,304,1536]{2,1,0:T(8,128)(2,1)}, u32[]{:S(2)}, u32[]{:S(2)}) async-start(bf16[4,304,1536]{2,1,0:T(8,128)(2,1)} %norm_in.5.refs_1_), calls=%async_computation.4 | async-start | bytes 7471104 | tf_op jit(solution)/shard_map/all_to_all | solution.py:65
  230.8 105.3 %all-gather.17.cloned.1.call-start = ((), (), s32[]{:S(2)}) async-start(), calls=%async_computation.42 | async-start | bytes 2949120 | tf_op jit(solution)/shard_map/all_gather | solution.py:105
  233.0 265.8 %all-gather.19.cloned.1.call-start = ((), (), s32[]{:S(2)}) async-start(), calls=%async_computation.43 | async-start | bytes 11796480 | tf_op jit(solution)/shard_map/all_gather | solution.py:105
  342.1 71.8 %all-to-all-start.5 = ((bf16[4,304,1536]{2,1,0:T(8,128)(2,1)}), bf16[4,304,1536]{2,1,0:T(8,128)(2,1)}, u32[]{:S(2)}, u32[]{:S(2)}) async-start(bf16[4,304,1536]{2,1,0:T(8,128)(2,1)} %project.2.refs_1_), calls=%async_computation.5 | async-start | bytes 7471104 | tf_op jit(solution)/shard_map/all_to_all | solution.py:65
  347.0 151.9 %all-gather.21.cloned.1.call-start = ((), (), s32[]{:S(2)}) async-start(), calls=%async_computation.44 | async-start | bytes 11796480 | tf_op jit(solution)/shard_map/all_gather | solution.py:105
  526.6 169.4 %all-gather.23.cloned.1.call-start = ((), (), s32[]{:S(2)}) async-start(), calls=%async_computation.45 | async-start | bytes 11796480 | tf_op jit(solution)/shard_map/all_gather | solution.py:105
  608.1 71.9 %all-to-all-start.9 = ((bf16[4,304,1536]{2,1,0:T(8,128)(2,1)}), bf16[4,304,1536]{2,1,0:T(8,128)(2,1)}, u32[]{:S(2)}, u32[]{:S(2)}) async-start(bf16[4,304,1536]{2,1,0:T(8,128)(2,1)} %get-tuple-element.52), calls=%async_computation.9 | async-start | bytes 7471104 | tf_op jit(solution)/shard_map/all_to_all | solution.py:65
  614.7 220.9 %all-gather.25.cloned.1.call-start = ((), (), s32[]{:S(2)}) async-start(), calls=%async_computation.46 | async-start | bytes 11796480 | tf_op jit(solution)/shard_map/all_gather | solution.py:105
  744.4 72.0 %all-to-all-start.11 = ((bf16[4,304,1536]{2,1,0:T(8,128)(2,1)}), bf16[4,304,1536]{2,1,0:T(8,128)(2,1)}, u32[]{:S(2)}, u32[]{:S(2)}) async-start(bf16[4,304,1536]{2,1,0:T(8,128)(2,1)} %project.3.refs_1_), calls=%async_computation.11 | async-start | bytes 7471104 | tf_op jit(solution)/shard_map/all_to_all | solution.py:65
  749.2 135.1 %all-gather.27.cloned.1.call-start = ((), (), s32[]{:S(2)}) async-start(), calls=%async_computation.47 | async-start | bytes 11796480 | tf_op jit(solution)/shard_map/all_gather | solution.py:105
  835.4 167.2 %reduce-scatter.9.cloned.1.call-start = ((), (), s32[]{:S(2)}) async-start(), calls=%async_computation.33 | async-start | bytes 11796480 | tf_op jit(solution)/shard_map/reduce_scatter | solution.py:109
  945.5 136.7 %reduce-scatter.11.cloned.1.call-start = ((), (), s32[]{:S(2)}) async-start(), calls=%async_computation.34 | async-start | bytes 11796480 | tf_op jit(solution)/shard_map/reduce_scatter | solution.py:109
  997.9 72.4 %all-to-all-start.14 = ((bf16[4,304,1536]{2,1,0:T(8,128)(2,1)}), bf16[4,304,1536]{2,1,0:T(8,128)(2,1)}, u32[]{:S(2)}, u32[]{:S(2)}) async-start(bf16[4,304,1536]{2,1,0:T(8,128)(2,1)} %get-tuple-element.61), calls=%async_computation.14 | async-start | bytes 7471104 | tf_op jit(solution)/shard_map/all_to_all | solution.py:65
  1076.1 74.1 %all-to-all-start.15 = ((bf16[4,304,1536]{2,1,0:T(8,128)(2,1)}), bf16[4,304,1536]{2,1,0:T(8,128)(2,1)}, u32[]{:S(2)}, u32[]{:S(2)}) async-start(bf16[4,304,1536]{2,1,0:T(8,128)(2,1)} %gate.37), calls=%async_computation.16 | async-start | bytes 7471104 | tf_op jit(solution)/shard_map/all_to_all | solution.py:65
  1167.0 184.3 %reduce-scatter.15.cloned.1.call-start = ((), (), s32[]{:S(2)}) async-start(), calls=%async_computation.36 | async-start | bytes 2949120 | tf_op jit(solution)/shard_map/reduce_scatter | solution.py:109
  1208.5 142.9 %reduce-scatter.13.cloned.1.call-start = ((), (), s32[]{:S(2)}) async-start(), calls=%async_computation.35 | async-start | bytes 8847360 | tf_op jit(solution)/shard_map/reduce_scatter | solution.py:109
  1222.7 214.5 %reduce-scatter.17.cloned.1.call-start = ((), (), s32[]{:S(2)}) async-start(), calls=%async_computation.37 | async-start | bytes 11796480 | tf_op jit(solution)/shard_map/reduce_scatter | solution.py:109
  1346.3 75.3 %all-to-all-start.19 = ((bf16[4,304,1536]{2,1,0:T(8,128)(2,1)}), bf16[4,304,1536]{2,1,0:T(8,128)(2,1)}, u32[]{:S(2)}, u32[]{:S(2)}) async-start(bf16[4,304,1536]{2,1,0:T(8,128)(2,1)} %gate.40), calls=%async_computation.21 | async-start | bytes 7471104 | tf_op jit(solution)/shard_map/all_to_all | solution.py:65
  1351.2 165.3 %reduce-scatter.19.cloned.1.call-start = ((), (), s32[]{:S(2)}) async-start(), calls=%async_computation.38 | async-start | bytes 11796480 | tf_op jit(solution)/shard_map/reduce_scatter | solution.py:109
  1430.9 73.9 %all-to-all-start.20 = ((bf16[4,304,1536]{2,1,0:T(8,128)(2,1)}), bf16[4,304,1536]{2,1,0:T(8,128)(2,1)}, u32[]{:S(2)}, u32[]{:S(2)}) async-start(bf16[4,304,1536]{2,1,0:T(8,128)(2,1)} %get-tuple-element.72), calls=%async_computation.24 | async-start | bytes 7471104 | tf_op jit(solution)/shard_map/all_to_all | solution.py:65
  1437.2 167.6 %reduce-scatter.21.cloned.1.call-start = ((), (), s32[]{:S(2)}) async-start(), calls=%async_computation.39 | async-start | bytes 2949120 | tf_op jit(solution)/shard_map/reduce_scatter | solution.py:109
  1516.5 194.6 %reduce-scatter.23.cloned.1.call-start = ((), (), s32[]{:S(2)}) async-start(), calls=%async_computation.40 | async-start | bytes 8847360 | tf_op jit(solution)/shard_map/reduce_scatter | solution.py:109
  (183 other events, 3284.1 us)
Sparse Core Ops, SparseCore 0:
  220.8 50.2 all-gather.14
  273.1 24.0 all-gather.16
  304.3 62.0 all-gather.18
  420.2 61.4 all-gather.20
  600.7 65.2 all-gather.22
  686.3 62.7 all-gather.24
  822.8 61.4 all-gather.26
  918.8 78.4 reduce-scatter.8
  999.8 78.4 reduce-scatter.10
  1208.6 30.6 reduce-scatter.14
  1241.9 63.7 reduce-scatter.12
  1308.1 78.4 reduce-scatter.16
  1421.8 78.6 reduce-scatter.18
  1516.6 31.1 reduce-scatter.20
  1587.0 60.9 reduce-scatter.22

commit v4 on v3

--- a/solution.py
+++ b/solution.py
@@ -542,7 +542,7 @@
         )
 
     def norm_in(self, mods, x, blocks=None, gate=None, after_norm=None, after=()):
-        rows = self.ci // 4
+        rows = self.ci // 2
 
         def kernel(*refs):
             refs = list(refs)
@@ -560,7 +560,7 @@
                 out = (normed * (1.0 + vectors[0, kind + 1 : kind + 2]) + vectors[0, kind : kind + 1]).astype(BF16)
                 refs[0][...] = jnp.broadcast_to(out[None], refs[0].shape)
 
-        ratio = 4
+        ratio = 2
 
         def vectors(depth):
             return (mods, (1,) + mods.shape[1:], lambda i: (depth * 2 + i // ratio, 0, 0))
@@ -577,7 +577,7 @@
         return call(kernel, "norm_in", (ratio + 1,), ins, outs, flops=20 * self.rc * D, after=after)
 
     def norm_back(self, mods, grad, blocks=None, x=None, scale=None, branch=None, gate=None, after=()):
-        rows, ratio = self.ci // 4, 4
+        rows, ratio = self.ci // 2, 2
 
         def kernel(*refs):
             refs = list(refs)

time: 1840 us -> 1830 us (level)
  transfers between devices with their start and end apart: 66 -> 66, of which waited for: 39 -> 39; matrix products, arithmetic and copies ran while one was open for 14% -> 14% of each run, Pallas kernels for 22% -> 21%
where the time goes in v4:
time: 1830 us; the launch traced here: 1820 us
  waiting for transfers between devices  855 us (47%)
  Pallas kernels  442 us (24%)
  starting transfers between devices  177 us (10%)
  other arithmetic  161 us (9%)
  local copies, waits for them, and re-layouts  120 us (7%)
  matrix products  40.3 us (2%)
  between operations  21 us (1%)
    pallas_call x44, Pallas kernels, call(): pl.pallas_call(body, grid=grid, in_specs=in_specs + [pl.BlockSpec(memory_...  442 us
    all_to_all x17, waiting for transfers between devices, exchange(): lax.all_to_all(blocks, ('row', 'col'), 0, 0, tiled=True, axis_index_group...  255 us
    ppermute x7, waiting for transfers between devices, sum_levels(): lax.ppermute(other, 'col', self.levels).astype(F32)  191 us
    ppermute x6, waiting for transfers between devices, swap_sides(): lax.ppermute(other, 'row', self.across)  189 us
    ppermute x6, waiting for transfers between devices, join_sides(): lax.ppermute(other, 'row', self.across)  125 us
    all_to_all x17, starting transfers between devices, exchange(): lax.all_to_all(blocks, ('row', 'col'), 0, 0, tiled=True, axis_index_group...  87.1 us
    unnamed x18, other arithmetic  43.3 us
    dot_general x42, matrix products, dot(): lax.dot_general(a, b, (((ca,), (cb,)), ((), ())), preferred_element_type=...  40.3 us
  transfers between devices with their start and end apart: 66, of which 39 were waited for; matrix products, arithmetic and copies ran while one was open for 14% of the time, Pallas kernels for 21%

profile of v4, /device:TPU:0, one launch (start us, length us, event | category | flops | bytes accessed | tf_op | source)
XLA Modules:
  0.0 1815.5 jit_solution(5954281090268999940)
XLA Ops:
  107.9 27.2 %collective-permute-done = bf16[8,192,192]{2,1,0:T(8,128)(2,1)S(1)} collective-permute-done((bf16[8,192,192]{2,1,0:T(8,128)(2,1)S(1)}, bf16[8,192,192]{2,1,0:T(8,128)(2,1)S(1)}, u32[]{:S(2)}, u32[]{:S(2)}) %collective-permute-start) | collective-permute-done | bytes 589856 | tf_op jit(solution)/shard_map/ppermute | solution.py:94
  176.9 27.8 %collective-permute-done.2 = bf16[8,384,192]{1,2,0:T(8,128)(2,1)} collective-permute-done((bf16[8,384,192]{1,2,0:T(8,128)(2,1)}, bf16[8,384,192]{1,2,0:T(8,128)(2,1)}, u32[]{:S(2)}, u32[]{:S(2)}) %collective-permute-start.2) | collective-permute-done | bytes 1179680 | tf_op jit(solution)/shard_map/ppermute | solution.py:100
  238.1 43.8 %collective-permute-done.3 = bf16[2,192,768]{2,1,0:T(8,128)(2,1)S(1)} collective-permute-done((bf16[2,192,768]{2,1,0:T(8,128)(2,1)}, bf16[2,192,768]{2,1,0:T(8,128)(2,1)S(1)}, u32[]{:S(2)}, u32[]{:S(2)}) %collective-permute-start.3) | collective-permute-done | bytes 589856 | tf_op jit(solution)/shard_map/ppermute | solution.py:94
  358.0 18.4 %reduce.5 = bf16[393216]{0:T(1024)(128)(2,1)} reduce(bf16[1,393216]{1,0:T(2,128)(2,1)} %param.28, bf16[]{:T(256)} %constant.195), dimensions={0}, to_apply=%param.28.reduce_sub_computation | reduce | bytes 1572866 | tf_op args[13]
  383.0 21.1 %collective-permute-done.5 = bf16[8,192,192]{2,1,0:T(8,128)(2,1)} collective-permute-done((bf16[8,192,192]{2,1,0:T(8,128)(2,1)}, bf16[8,192,192]{2,1,0:T(8,128)(2,1)}, u32[]{:S(2)}, u32[]{:S(2)}) %collective-permute-start.5) | collective-permute-done | bytes 589856 | tf_op jit(solution)/shard_map/ppermute | solution.py:94
  434.6 48.9 %collective-permute-done.7 = bf16[2,192,768]{2,1,0:T(8,128)(2,1)} collective-permute-done((bf16[2,192,768]{2,1,0:T(8,128)(2,1)}, bf16[2,192,768]{2,1,0:T(8,128)(2,1)}, u32[]{:S(2)}, u32[]{:S(2)}) %collective-permute-start.7) | collective-permute-done | bytes 589856 | tf_op jit(solution)/shard_map/ppermute | solution.py:94
  496.3 22.9 %mlp.2 = (bf16[4,304,1536]{2,1,0:T(8,128)(2,1)}, bf16[4,304,1536]{2,1,0:T(8,128)(2,1)}, bf16[4,304,1536]{2,1,0:T(8,128)(2,1)}) custom-call(bf16[4,304,1536]{2,1,0:T(8,128)(2,1)} %all-to-all-done.6.refs_0_.refs_1_, bf16[4,2,384,1536]{3,2,1,0:T(8,128)(2,1)} %bitcast.343, bf16[4,2,384,1536]{3,2,1,0:T(8,128)(2,1)} %bitcast.344, ...), custom_call_target="tpu_custom_call" | custom-call | flops 1434451968 | bytes 6586368 | tf_op jit(solution)/shard_map/mlp/pallas_call | solution.py:239
  538.9 38.8 %collective-permute-done.9 = bf16[2,192,768]{2,1,0:T(8,128)(2,1)S(1)} collective-permute-done((bf16[2,192,768]{2,1,0:T(8,128)(2,1)}, bf16[2,192,768]{2,1,0:T(8,128)(2,1)S(1)}, u32[]{:S(2)}, u32[]{:S(2)}) %collective-permute-start.9) | collective-permute-done | bytes 589856 | tf_op jit(solution)/shard_map/ppermute | solution.py:94
  612.3 63.7 %all-to-all-done.9.refs_1_.refs_0_ = bf16[4,304,1536]{2,1,0:T(8,128)(2,1)} async-done(((bf16[4,304,1536]{2,1,0:T(8,128)(2,1)}), bf16[4,304,1536]{2,1,0:T(8,128)(2,1)}, u32[]{:S(2)}, u32[]{:S(2)}) %all-to-all-start.9) | async-done | bytes 3735584 | tf_op jit(solution)/shard_map/all_to_all | solution.py:65
  744.2 67.2 %all-to-all-done.11.refs_1_ = bf16[4,304,1536]{2,1,0:T(8,128)(2,1)} async-done(((bf16[4,304,1536]{2,1,0:T(8,128)(2,1)}), bf16[4,304,1536]{2,1,0:T(8,128)(2,1)}, u32[]{:S(2)}, u32[]{:S(2)}) %all-to-all-start.11) | async-done | bytes 3735584 | tf_op jit(solution)/shard_map/all_to_all | solution.py:65
  829.2 41.5 %all-to-all-done.12.refs_0_ = bf16[4,304,1536]{2,1,0:T(8,128)(2,1)} async-done(((bf16[4,304,1536]{2,1,0:T(8,128)(2,1)}), bf16[4,304,1536]{2,1,0:T(8,128)(2,1)}, u32[]{:S(2)}, u32[]{:S(2)}) %all-to-all-start.12) | async-done | bytes 3735584 | tf_op jit(solution)/shard_map/all_to_all | solution.py:65
  879.2 23.5 %mlp.3 = (bf16[4,304,1536]{2,1,0:T(8,128)(2,1)}, bf16[4,304,1536]{2,1,0:T(8,128)(2,1)}, bf16[4,304,1536]{2,1,0:T(8,128)(2,1)}) custom-call(bf16[4,304,1536]{2,1,0:T(8,128)(2,1)} %all-to-all-done.12.refs_0_, bf16[4,2,384,1536]{3,2,1,0:T(8,128)(2,1)} %bitcast.335, bf16[4,2,384,1536]{3,2,1,0:T(8,128)(2,1)} %bitcast.336, bf16[4,2,384,1536]{3,2,1,0:T(8,128)(2,1)} %bitcast.339, ...), custom_call_target="tpu_custom_call" | custom-call | flops 1434451968 | bytes 6586368 | tf_op jit(solution)/shard_map/mlp/pallas_call | solution.py:239
  913.5 21.8 %mlp_back.2 = (bf16[4,304,1536]{2,1,0:T(8,128)(2,1)}, bf16[4,304,1536]{2,1,0:T(8,128)(2,1)}) custom-call(bf16[4,304,1536]{2,1,0:T(8,128)(2,1)} %all-to-all-done.10.refs_3_.refs_0_, bf16[4,304,1536]{2,1,0:T(8,128)(2,1)} %get-tuple-element.56.refs_1_, bf16[4,2,384,1536]{3,2,1,0:T(8,128)(2,1)} %bitcast.337, bf16[4,2,384,1536]{3,2,1,0:T(8,128)(2,1)} %bitcast.338, ...), custom_call_target="tpu_custom_call" | custom-call | flops 1434451968 | bytes 6586368 | tf_op jit(solution)/shard_map/mlp_back/pallas_call | solution.py:239
  951.5 32.1 %all-to-all-done.13.refs_1_ = bf16[4,304,1536]{2,1,0:T(8,128)(2,1)} async-done(((bf16[4,304,1536]{2,1,0:T(8,128)(2,1)}), bf16[4,304,1536]{2,1,0:T(8,128)(2,1)}, u32[]{:S(2)}, u32[]{:S(2)}) %all-to-all-start.13) | async-done | bytes 3735584 | tf_op jit(solution)/shard_map/all_to_all | solution.py:65
  1001.3 61.1 %collective-permute-done.13 = bf16[2,384,768]{2,1,0:T(8,128)(2,1)S(1)} collective-permute-done((bf16[2,384,768]{2,1,0:T(8,128)(2,1)S(1)}, bf16[2,384,768]{2,1,0:T(8,128)(2,1)S(1)}, u32[]{:S(2)}, u32[]{:S(2)}) %collective-permute-start.13) | collective-permute-done | bytes 1179680 | tf_op jit(solution)/shard_map/ppermute | solution.py:116
  1082.2 36.2 %attend_back.2 = bf16[3,1216,384]{2,1,0:T(8,128)(2,1)} custom-call(bf16[1216,1152]{1,0:T(8,128)(2,1)} %bitcast.317, bf16[1216,1152]{1,0:T(8,128)(2,1)} %bitcast.318, bf16[1216,1152]{1,0:T(8,128)(2,1)} %bitcast.319, bf16[1216,1]{1,0:T(8,128)(2,1)} %copy-done.5, bf16[1216,384]{1,0:T(8,128)(2,1)} %bitcast.374), custom_call_target="tpu_custom_call" | custom-call | flops 1419509760 | bytes 1517872 | tf_op jit(solution)/shard_map/attend_back/pallas_call | solution.py:239
  1218.4 52.4 %collective-permute-done.16 = bf16[2,192,768]{2,1,0:T(8,128)(2,1)S(1)} collective-permute-done((bf16[2,192,768]{2,1,0:T(8,128)(2,1)S(1)}, bf16[2,192,768]{2,1,0:T(8,128)(2,1)S(1)}, u32[]{:S(2)}, u32[]{:S(2)}) %collective-permute-start.16) | collective-permute-done | bytes 589856 | tf_op jit(solution)/shard_map/ppermute | solution.py:123
  1293.3 22.1 %mlp_back.3 = (bf16[4,304,1536]{2,1,0:T(8,128)(2,1)}, bf16[4,304,1536]{2,1,0:T(8,128)(2,1)}) custom-call(bf16[4,304,1536]{2,1,0:T(8,128)(2,1)} %all-to-all-done.17.refs_1_.refs_0_, bf16[4,304,1536]{2,1,0:T(8,128)(2,1)} %get-tuple-element.67.refs_1_, bf16[4,2,384,1536]{3,2,1,0:T(8,128)(2,1)} %bitcast.345, bf16[4,2,384,1536]{3,2,1,0:T(8,128)(2,1)} %bitcast.346, ...), custom_call_target="tpu_custom_call" | custom-call | flops 1434451968 | bytes 6586368 | tf_op jit(solution)/shard_map/mlp_back/pallas_call | solution.py:239
  1315.3 21.8 %all-to-all-done.18 = bf16[8,304,384]{2,1,0:T(8,128)(2,1)} async-done(((bf16[8,304,384]{2,1,0:T(8,128)(2,1)}), bf16[8,304,384]{2,1,0:T(8,128)(2,1)}, u32[]{:S(2)}, u32[]{:S(2)}) %all-to-all-start.18) | async-done | bytes 1867808 | tf_op jit(solution)/shard_map/all_to_all | solution.py:158
  1360.1 48.6 %collective-permute-done.17 = bf16[8,384,192]{1,2,0:T(8,128)(2,1)} collective-permute-done((bf16[8,384,192]{1,2,0:T(8,128)(2,1)}, bf16[8,384,192]{1,2,0:T(8,128)(2,1)}, u32[]{:S(2)}, u32[]{:S(2)}) %collective-permute-start.17) | collective-permute-done | bytes 1179680 | tf_op jit(solution)/shard_map/ppermute | solution.py:116
  1436.4 51.4 %collective-permute-done.19 = bf16[8,192,192]{2,1,0:T(8,128)(2,1)S(1)} collective-permute-done((bf16[8,192,192]{2,1,0:T(8,128)(2,1)S(1)}, bf16[8,192,192]{2,1,0:T(8,128)(2,1)S(1)}, u32[]{:S(2)}, u32[]{:S(2)}) %collective-permute-start.19) | collective-permute-done | bytes 589856 | tf_op jit(solution)/shard_map/ppermute | solution.py:123
  1514.5 36.7 %attend_back.3 = bf16[3,1216,384]{2,1,0:T(8,128)(2,1)} custom-call(bf16[1216,1152]{1,0:T(8,128)(2,1)} %bitcast.311, bf16[1216,1152]{1,0:T(8,128)(2,1)} %bitcast.312, bf16[1216,1152]{1,0:T(8,128)(2,1)} %bitcast.313, bf16[1216,1]{1,0:T(8,128)(2,1)} %copy-done.5, bf16[1216,384]{1,0:T(8,128)(2,1)} %bitcast.373, bf16[4,2,384,384]{3,2,1,0:T(8,128)(2,1)} %out_grad.3.refs_5_), custom_call_target="tpu_custom_call" | custom-call | flops 1419509760 | bytes 1517872 | tf_op jit(solution)/shard_map/attend_back/pallas_call | solution.py:239
  1609.9 36.1 %collective-permute-done.22 = bf16[2,384,192]{2,1,0:T(8,128)(2,1)} collective-permute-done((bf16[2,384,192]{2,1,0:T(8,128)(2,1)}, bf16[2,384,192]{2,1,0:T(8,128)(2,1)}, u32[]{:S(2)}, u32[]{:S(2)}) %collective-permute-start.22) | collective-permute-done | bytes 294944 | tf_op jit(solution)/shard_map/ppermute | solution.py:116
  1731.0 22.2 %collective-permute-done.23 = bf16[6,384,192]{1,2,0:T(8,128)(2,1)} collective-permute-done((bf16[6,384,192]{1,2,0:T(8,128)(2,1)}, bf16[6,384,192]{1,2,0:T(8,128)(2,1)}, u32[]{:S(2)}, u32[]{:S(2)}) %collective-permute-start.23) | collective-permute-done | bytes 884768 | tf_op jit(solution)/shard_map/ppermute | solution.py:116
  (780 shorter events, 907.4 us)
Async XLA Ops:
  100.9 106.3 %all-to-all-start.3 = ((bf16[8,304,384]{2,1,0:T(8,128)(2,1)}), bf16[8,304,384]{2,1,0:T(8,128)(2,1)}, u32[]{:S(2)}, u32[]{:S(2)}) async-start(bf16[8,304,384]{2,1,0:T(8,128)(2,1)} %bitcast.381), calls=%async_computation.3 | async-start | bytes 3735552 | tf_op jit(solution)/shard_map/all_to_all | solution.py:146
  105.4 198.7 %all-gather.15.cloned.1.call-start = ((), (), s32[]{:S(2)}) async-start(), calls=%async_computation.41 | async-start | bytes 8847360 | tf_op jit(solution)/shard_map/all_gather | solution.py:105
  224.6 72.2 %all-to-all-start.4 = ((bf16[4,304,1536]{2,1,0:T(8,128)(2,1)}), bf16[4,304,1536]{2,1,0:T(8,128)(2,1)}, u32[]{:S(2)}, u32[]{:S(2)}) async-start(bf16[4,304,1536]{2,1,0:T(8,128)(2,1)} %norm_in.5.refs_1_), calls=%async_computation.4 | async-start | bytes 7471104 | tf_op jit(solution)/shard_map/all_to_all | solution.py:65
  229.5 105.3 %all-gather.17.cloned.1.call-start = ((), (), s32[]{:S(2)}) async-start(), calls=%async_computation.42 | async-start | bytes 2949120 | tf_op jit(solution)/shard_map/all_gather | solution.py:105
  231.7 264.6 %all-gather.19.cloned.1.call-start = ((), (), s32[]{:S(2)}) async-start(), calls=%async_computation.43 | async-start | bytes 11796480 | tf_op jit(solution)/shard_map/all_gather | solution.py:105
  340.8 71.8 %all-to-all-start.5 = ((bf16[4,304,1536]{2,1,0:T(8,128)(2,1)}), bf16[4,304,1536]{2,1,0:T(8,128)(2,1)}, u32[]{:S(2)}, u32[]{:S(2)}) async-start(bf16[4,304,1536]{2,1,0:T(8,128)(2,1)} %project.2.refs_1_), calls=%async_computation.5 | async-start | bytes 7471104 | tf_op jit(solution)/shard_map/all_to_all | solution.py:65
  345.7 150.6 %all-gather.21.cloned.1.call-start = ((), (), s32[]{:S(2)}) async-start(), calls=%async_computation.44 | async-start | bytes 11796480 | tf_op jit(solution)/shard_map/all_gather | solution.py:105
  524.1 166.6 %all-gather.23.cloned.1.call-start = ((), (), s32[]{:S(2)}) async-start(), calls=%async_computation.45 | async-start | bytes 11796480 | tf_op jit(solution)/shard_map/all_gather | solution.py:105
  604.1 71.9 %all-to-all-start.9 = ((bf16[4,304,1536]{2,1,0:T(8,128)(2,1)}), bf16[4,304,1536]{2,1,0:T(8,128)(2,1)}, u32[]{:S(2)}, u32[]{:S(2)}) async-start(bf16[4,304,1536]{2,1,0:T(8,128)(2,1)} %get-tuple-element.52), calls=%async_computation.9 | async-start | bytes 7471104 | tf_op jit(solution)/shard_map/all_to_all | solution.py:65
  610.5 218.7 %all-gather.25.cloned.1.call-start = ((), (), s32[]{:S(2)}) async-start(), calls=%async_computation.46 | async-start | bytes 11796480 | tf_op jit(solution)/shard_map/all_gather | solution.py:105
  739.3 72.1 %all-to-all-start.11 = ((bf16[4,304,1536]{2,1,0:T(8,128)(2,1)}), bf16[4,304,1536]{2,1,0:T(8,128)(2,1)}, u32[]{:S(2)}, u32[]{:S(2)}) async-start(bf16[4,304,1536]{2,1,0:T(8,128)(2,1)} %project.3.refs_1_), calls=%async_computation.11 | async-start | bytes 7471104 | tf_op jit(solution)/shard_map/all_to_all | solution.py:65
  744.0 135.1 %all-gather.27.cloned.1.call-start = ((), (), s32[]{:S(2)}) async-start(), calls=%async_computation.47 | async-start | bytes 11796480 | tf_op jit(solution)/shard_map/all_gather | solution.py:105
  829.2 167.9 %reduce-scatter.9.cloned.1.call-start = ((), (), s32[]{:S(2)}) async-start(), calls=%async_computation.33 | async-start | bytes 11796480 | tf_op jit(solution)/shard_map/reduce_scatter | solution.py:109
  940.4 136.3 %reduce-scatter.11.cloned.1.call-start = ((), (), s32[]{:S(2)}) async-start(), calls=%async_computation.34 | async-start | bytes 11796480 | tf_op jit(solution)/shard_map/reduce_scatter | solution.py:109
  992.3 72.4 %all-to-all-start.14 = ((bf16[4,304,1536]{2,1,0:T(8,128)(2,1)}), bf16[4,304,1536]{2,1,0:T(8,128)(2,1)}, u32[]{:S(2)}, u32[]{:S(2)}) async-start(bf16[4,304,1536]{2,1,0:T(8,128)(2,1)} %get-tuple-element.61), calls=%async_computation.14 | async-start | bytes 7471104 | tf_op jit(solution)/shard_map/all_to_all | solution.py:65
  1070.5 74.1 %all-to-all-start.15 = ((bf16[4,304,1536]{2,1,0:T(8,128)(2,1)}), bf16[4,304,1536]{2,1,0:T(8,128)(2,1)}, u32[]{:S(2)}, u32[]{:S(2)}) async-start(bf16[4,304,1536]{2,1,0:T(8,128)(2,1)} %gate.37), calls=%async_computation.16 | async-start | bytes 7471104 | tf_op jit(solution)/shard_map/all_to_all | solution.py:65
  1161.5 182.9 %reduce-scatter.15.cloned.1.call-start = ((), (), s32[]{:S(2)}) async-start(), calls=%async_computation.36 | async-start | bytes 2949120 | tf_op jit(solution)/shard_map/reduce_scatter | solution.py:109
  1202.9 141.6 %reduce-scatter.13.cloned.1.call-start = ((), (), s32[]{:S(2)}) async-start(), calls=%async_computation.35 | async-start | bytes 8847360 | tf_op jit(solution)/shard_map/reduce_scatter | solution.py:109
  1216.3 212.9 %reduce-scatter.17.cloned.1.call-start = ((), (), s32[]{:S(2)}) async-start(), calls=%async_computation.37 | async-start | bytes 11796480 | tf_op jit(solution)/shard_map/reduce_scatter | solution.py:109
  1339.6 75.4 %all-to-all-start.19 = ((bf16[4,304,1536]{2,1,0:T(8,128)(2,1)}), bf16[4,304,1536]{2,1,0:T(8,128)(2,1)}, u32[]{:S(2)}, u32[]{:S(2)}) async-start(bf16[4,304,1536]{2,1,0:T(8,128)(2,1)} %gate.40), calls=%async_computation.21 | async-start | bytes 7471104 | tf_op jit(solution)/shard_map/all_to_all | solution.py:65
  1344.4 165.0 %reduce-scatter.19.cloned.1.call-start = ((), (), s32[]{:S(2)}) async-start(), calls=%async_computation.38 | async-start | bytes 11796480 | tf_op jit(solution)/shard_map/reduce_scatter | solution.py:109
  1423.7 73.9 %all-to-all-start.20 = ((bf16[4,304,1536]{2,1,0:T(8,128)(2,1)}), bf16[4,304,1536]{2,1,0:T(8,128)(2,1)}, u32[]{:S(2)}, u32[]{:S(2)}) async-start(bf16[4,304,1536]{2,1,0:T(8,128)(2,1)} %get-tuple-element.72), calls=%async_computation.24 | async-start | bytes 7471104 | tf_op jit(solution)/shard_map/all_to_all | solution.py:65
  1429.2 168.5 %reduce-scatter.21.cloned.1.call-start = ((), (), s32[]{:S(2)}) async-start(), calls=%async_computation.39 | async-start | bytes 2949120 | tf_op jit(solution)/shard_map/reduce_scatter | solution.py:109
  1509.4 193.8 %reduce-scatter.23.cloned.1.call-start = ((), (), s32[]{:S(2)}) async-start(), calls=%async_computation.40 | async-start | bytes 8847360 | tf_op jit(solution)/shard_map/reduce_scatter | solution.py:109
  (183 other events, 3281.9 us)
Sparse Core Ops, SparseCore 0:
  220.9 50.1 all-gather.14
  273.2 24.0 all-gather.16
  303.0 62.0 all-gather.18
  418.9 61.4 all-gather.20
  598.3 65.1 all-gather.22
  682.2 62.6 all-gather.24
  817.6 61.4 all-gather.26
  913.7 78.4 reduce-scatter.8
  994.7 78.4 reduce-scatter.10
  1203.0 30.6 reduce-scatter.14
  1236.4 63.6 reduce-scatter.12
  1302.6 78.3 reduce-scatter.16
  1415.2 78.6 reduce-scatter.18
  1509.5 31.3 reduce-scatter.20
  1579.8 60.9 reduce-scatter.22
